TPU v7x, 32 devices: a whole 2x2x4 slice. The times are simulated.
32 devices in a mesh: dp: 2 (over x), ctx: 4 (over z), tp: 4 (over y, core).
Axes of the slice: x: 2, y: 2, z: 4, core: 2. Of those that a mesh axis runs over, the one named last changes fastest.
Arguments:
- tokens: bfloat16 [4096, 2048], P(('dp', 'ctx')), may hold values from -6 to 6
- cotangent: bfloat16 [4096, 2048], P(('dp', 'ctx')), may hold values from -6 to 6
- lengths: int32 [2, 3], P('dp'), may hold values from 1 to 2046, as said below
- routes: int32 [4096, 8], P(('dp', 'ctx')), may hold values from 0 to 15, all different within a row; in each aligned block of 512 rows (0 to 511, 512 to 1023, ...) at most 320 rows name the same one
- attn_gain: bfloat16 [2048], P('dp'), may hold values from 0.099609375 to 1.8984375
- w_query: bfloat16 [2048, 2048], P('dp', 'tp'), may hold values from -0.125 to 0.125
- w_key: bfloat16 [2048, 2048], P('dp', 'tp'), may hold values from -0.125 to 0.125
- w_value: bfloat16 [2048, 2048], P('dp', 'tp'), may hold values from -0.125 to 0.125
- q_gain: bfloat16 [2048], P('dp'), may hold values from 1 to 1.59375
- k_gain: bfloat16 [2048], P('dp'), may hold values from 1 to 1.59375
- w_out: bfloat16 [2048, 2048], P('tp', 'dp'), may hold values from -2 to 2
- mlp_gain: bfloat16 [2048], P('dp'), may hold values from 0.099609375 to 1.8984375
- w_router: bfloat16 [2048, 16], P('dp'), may hold values from -0.06591797 to 0.06591797
- w_gate: bfloat16 [16, 2048, 1024], P(None, 'dp', 'tp'), may hold values from -0.125 to 0.125
- w_up: bfloat16 [16, 2048, 1024], P(None, 'dp', 'tp'), may hold values from -0.125 to 0.125
- w_down: bfloat16 [16, 1024, 2048], P(None, 'tp', 'dp'), may hold values from -1.5 to 1.5
Outputs:
- output: float32 [4096, 2048], P(('dp', 'ctx'))
- d_tokens: float32 [4096, 2048], P(('dp', 'ctx'))
- d_attn_gain: float32 [2048], P('dp')
- d_w_query: float32 [2048, 2048], P('dp', 'tp')
- d_w_key: float32 [2048, 2048], P('dp', 'tp')
- d_w_value: float32 [2048, 2048], P('dp', 'tp')
- d_q_gain: float32 [2048], P('dp')
- d_k_gain: float32 [2048], P('dp')
- d_w_out: float32 [2048, 2048], P('tp', 'dp')
- d_mlp_gain: float32 [2048], P('dp')
- d_w_router: float32 [2048, 16], P('dp')
- d_w_gate: float32 [16, 2048, 1024], P(None, 'dp', 'tp')
- d_w_up: float32 [16, 2048, 1024], P(None, 'dp', 'tp')
- d_w_down: float32 [16, 1024, 2048], P(None, 'tp', 'dp')
Inputs may be any that keep to these rules, and one draw needn't show every extreme that they name: Each row's lengths sum to 2048; the first and the last are between 1 and 256, so the middle sequence covers positions of every index of ctx. In one pack the first and last are both 1. `routes`: in the 512 rows of one device no expert is named by more than 320 rows.
All inputs are finite; a program needn't handle non-finite values.
Results may differ from a plain program's by a relative error of at most 0.017.
The roundings to bfloat16 on the way count: a program that leaves them out, or rounds other values in their place, can miss the bound.
Values may be sent and summed in bfloat16 or wider, within the bound.
A program may use at most 320 MiB of HBM per device.

v0:
```python
import jax
import jax.numpy as jnp
from jax import lax
from jax.sharding import PartitionSpec as P

HEAD = 128
CAP = 320


EPS = 1e-05
THETA = 10000.0


def rms_scale(v):
    return lax.rsqrt(jnp.mean(v * v, axis=-1, keepdims=True) + EPS)


def rms_back(v, scale, pulled):
    return scale * pulled - v * scale**3 * jnp.mean(pulled * v, axis=-1, keepdims=True)


def layout(row, total):
    ends = jnp.cumsum(row)
    starts = ends - row
    index = jnp.arange(total, dtype=jnp.int32)
    segment = jnp.sum((index[:, None] >= ends[None, :]).astype(jnp.int32), axis=1)
    picked = segment[:, None] == jnp.arange(row.shape[0], dtype=jnp.int32)[None, :]
    first = jnp.sum(jnp.where(picked, starts[None, :], 0), axis=1)
    return (segment, index - first)


def rotation(position):
    inverse = THETA ** (-jnp.arange(0, HEAD, 2).astype(jnp.float32) / HEAD)
    angle = position.astype(jnp.float32)[:, None] * inverse[None, :]
    return (jnp.cos(angle), jnp.sin(angle))


def rotate(v, cosine, sine):
    count = v.shape[0]
    parts = v.reshape(count, -1, 2, HEAD // 2)
    first = parts[:, :, 0]
    second = parts[:, :, 1]
    cos_b = cosine[:, None, :]
    sin_b = sine[:, None, :]
    turned = jnp.stack([first * cos_b - second * sin_b, second * cos_b + first * sin_b], axis=2)
    return turned.reshape(count, -1)


def dispatch(routes, experts, capacity):
    flat = routes.reshape(-1)
    onehot = (flat[:, None] == jnp.arange(experts, dtype=jnp.int32)[None, :]).astype(jnp.int32)
    counts = jnp.sum(onehot, axis=0)
    starts = jnp.cumsum(counts) - counts
    order = jnp.argsort(flat, stable=True)
    slot = jnp.arange(capacity, dtype=jnp.int32)
    where_at = jnp.minimum(starts[:, None] + slot[None, :], flat.shape[0] - 1)
    picked = order[where_at] // routes.shape[1]
    valid = slot[None, :] < counts[:, None]
    return (picked, valid)


def body(
    tokens,
    cotangent,
    lengths,
    routes,
    attn_gain,
    w_query,
    w_key,
    w_value,
    q_gain,
    k_gain,
    w_out,
    mlp_gain,
    w_router,
    w_gate,
    w_up,
    w_down,
):
    fetched = (
        lax.all_gather(attn_gain, "dp", axis=0, tiled=True),
        lax.all_gather(q_gain, "dp", axis=0, tiled=True),
        lax.all_gather(k_gain, "dp", axis=0, tiled=True),
        lax.all_gather(w_query, "dp", axis=0, tiled=True),
        lax.all_gather(w_key, "dp", axis=0, tiled=True),
        lax.all_gather(w_value, "dp", axis=0, tiled=True),
        lax.all_gather(w_out, "dp", axis=1, tiled=True),
        lax.all_gather(mlp_gain, "dp", axis=0, tiled=True),
        lax.all_gather(w_router, "dp", axis=0, tiled=True),
        lax.all_gather(w_gate, "dp", axis=1, tiled=True),
        lax.all_gather(w_up, "dp", axis=1, tiled=True),
        lax.all_gather(w_down, "dp", axis=2, tiled=True),
    )
    (
        gain_one,
        gain_query,
        gain_key,
        query_w,
        key_w,
        value_w,
        out_w,
        gain_two,
        router_w,
        gate_all,
        up_all,
        down_all,
    ) = fetched
    gain_one = gain_one.astype(jnp.float32)
    gain_two = gain_two.astype(jnp.float32)
    rows = tokens.shape[0]
    width = tokens.shape[1]
    local = query_w.shape[1]
    heads = local // HEAD
    scale_attn = HEAD ** (-0.5)
    tp_at = lax.axis_index("tp")
    ctx_at = lax.axis_index("ctx")
    ctx_count = lax.axis_size("ctx")
    gain_q_mine = lax.dynamic_slice_in_dim(gain_query, tp_at * local, local).astype(jnp.float32)
    gain_k_mine = lax.dynamic_slice_in_dim(gain_key, tp_at * local, local).astype(jnp.float32)
    inputs = tokens.astype(jnp.float32)
    upstream = cotangent.astype(jnp.float32)
    scale_one = rms_scale(inputs)
    normed_one = inputs * scale_one
    hidden_one = (normed_one * gain_one).astype(jnp.bfloat16)
    q_raw = jnp.dot(hidden_one, query_w, preferred_element_type=jnp.float32)
    k_raw = jnp.dot(hidden_one, key_w, preferred_element_type=jnp.float32)
    values = jnp.dot(hidden_one, value_w, preferred_element_type=jnp.float32).astype(jnp.bfloat16)
    q_square, k_square = lax.psum(
        (jnp.sum(q_raw * q_raw, axis=1), jnp.sum(k_raw * k_raw, axis=1)), "tp"
    )
    q_scale = lax.rsqrt(q_square / width + EPS)[:, None]
    k_scale = lax.rsqrt(k_square / width + EPS)[:, None]
    q_hat = q_raw * q_scale
    k_hat = k_raw * k_scale
    pack_len = rows * ctx_count
    seg_all, pos_all = layout(lengths[0], pack_len)
    my_index = ctx_at * rows + jnp.arange(rows, dtype=jnp.int32)
    my_seg = lax.dynamic_slice_in_dim(seg_all, ctx_at * rows, rows)
    my_pos = lax.dynamic_slice_in_dim(pos_all, ctx_at * rows, rows)
    cosine, sine = rotation(my_pos)
    queries = rotate(q_hat * gain_q_mine, cosine, sine).astype(jnp.bfloat16)
    keys = rotate(k_hat * gain_k_mine, cosine, sine).astype(jnp.bfloat16)
    keys_all, values_all = (
        lax.all_gather(keys, "ctx", axis=0, tiled=True),
        lax.all_gather(values, "ctx", axis=0, tiled=True),
    )
    q_heads = queries.reshape(rows, heads, HEAD)
    k_heads = keys_all.reshape(pack_len, heads, HEAD)
    v_heads = values_all.reshape(pack_len, heads, HEAD)
    block = 512
    turns = pack_len // block

    def masked_scores(start):
        key_part = lax.dynamic_slice_in_dim(k_heads, start, block, 0)
        key_seg = lax.dynamic_slice_in_dim(seg_all, start, block, 0)
        key_index = start + jnp.arange(block, dtype=jnp.int32)
        allowed = (my_seg[:, None] == key_seg[None, :]) & (key_index[None, :] <= my_index[:, None])
        scores = (
            jnp.einsum("thd,khd->htk", q_heads, key_part, preferred_element_type=jnp.float32)
            * scale_attn
        )
        return (scores, allowed[None])

    def max_step(turn, carry):
        top, total = carry
        scores, allowed = masked_scores(turn * block)
        masked = jnp.where(allowed, scores, -1e30)
        new_top = jnp.maximum(top, jnp.max(masked, axis=2))
        kept = jnp.where(allowed, jnp.exp(masked - new_top[:, :, None]), 0.0)
        return (new_top, total * jnp.exp(top - new_top) + jnp.sum(kept, axis=2))

    top, total = lax.fori_loop(
        0,
        turns,
        max_step,
        (jnp.full((heads, rows), -1e30, jnp.float32), jnp.zeros((heads, rows), jnp.float32)),
    )
    log_sum = top + jnp.log(total)

    def probs_at(start):
        scores, allowed = masked_scores(start)
        return jnp.where(allowed, jnp.exp(scores - log_sum[:, :, None]), 0.0)

    def value_step(turn, acc):
        start = turn * block
        weights_b = probs_at(start).astype(jnp.bfloat16)
        value_part = lax.dynamic_slice_in_dim(v_heads, start, block, 0)
        return acc + jnp.einsum(
            "htk,khd->thd", weights_b, value_part, preferred_element_type=jnp.float32
        )

    attended = lax.fori_loop(0, turns, value_step, jnp.zeros((rows, heads, HEAD), jnp.float32))
    attended = attended.reshape(rows, local).astype(jnp.bfloat16)
    attn_part = jnp.dot(attended, out_w, preferred_element_type=jnp.float32)
    mixed = inputs + lax.psum(attn_part, "tp")
    scale_two = rms_scale(mixed)
    normed_two = mixed * scale_two
    hidden_two = (normed_two * gain_two).astype(jnp.bfloat16)
    logits = jnp.dot(hidden_two, router_w, preferred_element_type=jnp.float32)
    route_probs = jax.nn.softmax(logits, axis=1)
    experts = router_w.shape[1]
    slot_rows, valid = dispatch(routes, experts, CAP)
    expert_grid = jnp.broadcast_to(jnp.arange(experts, dtype=jnp.int32)[:, None], slot_rows.shape)
    slot_gate = jnp.where(valid, route_probs[slot_rows, expert_grid], 0.0)

    def expert_forward(acc, parts):
        gate_m, up_m, down_m, picked, weight = parts
        taken = hidden_two[picked]
        gate = jnp.dot(taken, gate_m, preferred_element_type=jnp.float32)
        up = jnp.dot(taken, up_m, preferred_element_type=jnp.float32)
        inner = (jax.nn.silu(gate) * up).astype(jnp.bfloat16)
        result = jnp.dot(inner, down_m, preferred_element_type=jnp.float32)
        acc = acc.at[picked].add(weight[:, None] * result)
        return (acc, (gate, up, jnp.sum(upstream[picked] * result, axis=1)))

    mixture, (gates_kept, ups_kept, slot_dots) = lax.scan(
        expert_forward,
        jnp.zeros((rows, width), jnp.float32),
        (gate_all, up_all, down_all, slot_rows, slot_gate),
    )
    output = mixed + lax.psum(mixture, "tp")

    def expert_backward(acc, parts):
        gate_m, up_m, down_m, picked, weight, gate, up = parts
        taken = hidden_two[picked]
        active = jax.nn.silu(gate)
        inner = (active * up).astype(jnp.bfloat16)
        back = (weight[:, None] * upstream[picked]).astype(jnp.bfloat16)
        d_inner = jnp.dot(back, down_m.T, preferred_element_type=jnp.float32)
        sigma = jax.nn.sigmoid(gate)
        d_gate = (d_inner * up * sigma * (1.0 + gate * (1.0 - sigma))).astype(jnp.bfloat16)
        d_up = (d_inner * active).astype(jnp.bfloat16)
        d_taken = jnp.dot(d_gate, gate_m.T, preferred_element_type=jnp.float32) + jnp.dot(
            d_up, up_m.T, preferred_element_type=jnp.float32
        )
        shares = (
            lax.psum_scatter(
                jnp.dot(taken.T, d_gate, preferred_element_type=jnp.float32),
                ("dp", "ctx"),
                scatter_dimension=0,
                tiled=True,
            ),
            lax.psum_scatter(
                jnp.dot(taken.T, d_up, preferred_element_type=jnp.float32),
                ("dp", "ctx"),
                scatter_dimension=0,
                tiled=True,
            ),
            lax.psum_scatter(
                jnp.dot(inner.T, back, preferred_element_type=jnp.float32),
                ("dp", "ctx"),
                scatter_dimension=1,
                tiled=True,
            ),
        )
        return (acc.at[picked].add(d_taken), shares)

    expert_in, (gate_shares, up_shares, down_shares) = lax.scan(
        expert_backward,
        jnp.zeros((rows, width), jnp.float32),
        (gate_all, up_all, down_all, slot_rows, slot_gate, gates_kept, ups_kept),
    )
    expert_in, dots_total = lax.psum((expert_in, slot_dots), "tp")
    d_route = (
        jnp.zeros((rows, experts), jnp.float32)
        .at[slot_rows, expert_grid]
        .add(jnp.where(valid, dots_total, 0.0))
    )
    d_logits = (
        route_probs * (d_route - jnp.sum(route_probs * d_route, axis=1, keepdims=True))
    ).astype(jnp.bfloat16)
    router_grad = jnp.dot(hidden_two.T, d_logits, preferred_element_type=jnp.float32)
    d_hidden_two = expert_in + jnp.dot(d_logits, router_w.T, preferred_element_type=jnp.float32)
    gain_two_grad = jnp.sum(d_hidden_two * normed_two, axis=0)
    d_mixed = upstream + rms_back(mixed, scale_two, d_hidden_two * gain_two)
    d_branch = d_mixed.astype(jnp.bfloat16)
    out_grad = jnp.dot(attended.T, d_branch, preferred_element_type=jnp.float32)
    d_attended = (
        jnp.dot(d_branch, out_w.T, preferred_element_type=jnp.float32)
        .astype(jnp.bfloat16)
        .reshape(rows, heads, HEAD)
    )

    def delta_step(turn, acc):
        start = turn * block
        probs = probs_at(start)
        value_part = lax.dynamic_slice_in_dim(v_heads, start, block, 0)
        d_probs = jnp.einsum(
            "thd,khd->htk", d_attended, value_part, preferred_element_type=jnp.float32
        )
        return acc + jnp.sum(probs * d_probs, axis=2)

    delta = lax.fori_loop(0, turns, delta_step, jnp.zeros((heads, rows), jnp.float32))

    def grad_step(turn, carry):
        d_query, d_keys, d_values = carry
        start = turn * block
        probs = probs_at(start)
        key_part = lax.dynamic_slice_in_dim(k_heads, start, block, 0)
        value_part = lax.dynamic_slice_in_dim(v_heads, start, block, 0)
        d_probs = jnp.einsum(
            "thd,khd->htk", d_attended, value_part, preferred_element_type=jnp.float32
        )
        d_raw = (probs * (d_probs - delta[:, :, None]) * scale_attn).astype(jnp.bfloat16)
        d_query = d_query + jnp.einsum(
            "htk,khd->thd", d_raw, key_part, preferred_element_type=jnp.float32
        )
        key_block = jnp.einsum("htk,thd->khd", d_raw, q_heads, preferred_element_type=jnp.float32)
        value_block = jnp.einsum(
            "htk,thd->khd",
            probs.astype(jnp.bfloat16),
            d_attended,
            preferred_element_type=jnp.float32,
        )
        d_keys = lax.dynamic_update_slice_in_dim(d_keys, key_block, start, 0)
        d_values = lax.dynamic_update_slice_in_dim(d_values, value_block, start, 0)
        return (d_query, d_keys, d_values)

    d_query, d_keys, d_values = lax.fori_loop(
        0,
        turns,
        grad_step,
        (
            jnp.zeros((rows, heads, HEAD), jnp.float32),
            jnp.zeros((pack_len, heads, HEAD), jnp.float32),
            jnp.zeros((pack_len, heads, HEAD), jnp.float32),
        ),
    )
    d_keys_mine, d_values_mine = (
        lax.psum_scatter(d_keys.reshape(pack_len, local), "ctx", scatter_dimension=0, tiled=True),
        lax.psum_scatter(d_values.reshape(pack_len, local), "ctx", scatter_dimension=0, tiled=True),
    )
    d_q_normed = rotate(d_query.reshape(rows, local), cosine, -sine)
    d_k_normed = rotate(d_keys_mine, cosine, -sine)
    q_pull = d_q_normed * gain_q_mine
    k_pull = d_k_normed * gain_k_mine
    q_total, k_total = lax.psum(
        (jnp.sum(q_pull * q_raw, axis=1), jnp.sum(k_pull * k_raw, axis=1)), "tp"
    )
    d_q_raw = (q_scale * q_pull - q_raw * q_scale**3 * (q_total / width)[:, None]).astype(
        jnp.bfloat16
    )
    d_k_raw = (k_scale * k_pull - k_raw * k_scale**3 * (k_total / width)[:, None]).astype(
        jnp.bfloat16
    )
    d_values_raw = d_values_mine.astype(jnp.bfloat16)
    q_gain_row = lax.dynamic_update_slice_in_dim(
        jnp.zeros((width,), jnp.float32), jnp.sum(d_q_normed * q_hat, axis=0), tp_at * local, 0
    )
    k_gain_row = lax.dynamic_update_slice_in_dim(
        jnp.zeros((width,), jnp.float32), jnp.sum(d_k_normed * k_hat, axis=0), tp_at * local, 0
    )
    d_hidden_part = (
        jnp.dot(d_q_raw, query_w.T, preferred_element_type=jnp.float32)
        + jnp.dot(d_k_raw, key_w.T, preferred_element_type=jnp.float32)
        + jnp.dot(d_values_raw, value_w.T, preferred_element_type=jnp.float32)
    )
    d_hidden_one, q_gain_full, k_gain_full = lax.psum((d_hidden_part, q_gain_row, k_gain_row), "tp")
    gain_one_grad = jnp.sum(d_hidden_one * normed_one, axis=0)
    d_inputs = d_mixed + rms_back(inputs, scale_one, d_hidden_one * gain_one)
    query_grad = jnp.dot(hidden_one.T, d_q_raw, preferred_element_type=jnp.float32)
    key_grad = jnp.dot(hidden_one.T, d_k_raw, preferred_element_type=jnp.float32)
    value_grad = jnp.dot(hidden_one.T, d_values_raw, preferred_element_type=jnp.float32)
    (
        sum_gain_one,
        sum_gain_q,
        sum_gain_k,
        sum_gain_two,
        sum_query,
        sum_key,
        sum_value,
        sum_out,
        sum_router,
    ) = (
        lax.psum_scatter(gain_one_grad, ("dp", "ctx"), scatter_dimension=0, tiled=True),
        lax.psum_scatter(q_gain_full, ("dp", "ctx"), scatter_dimension=0, tiled=True),
        lax.psum_scatter(k_gain_full, ("dp", "ctx"), scatter_dimension=0, tiled=True),
        lax.psum_scatter(gain_two_grad, ("dp", "ctx"), scatter_dimension=0, tiled=True),
        lax.psum_scatter(query_grad, ("dp", "ctx"), scatter_dimension=0, tiled=True),
        lax.psum_scatter(key_grad, ("dp", "ctx"), scatter_dimension=0, tiled=True),
        lax.psum_scatter(value_grad, ("dp", "ctx"), scatter_dimension=0, tiled=True),
        lax.psum_scatter(out_grad, ("dp", "ctx"), scatter_dimension=1, tiled=True),
        lax.psum_scatter(router_grad, ("dp", "ctx"), scatter_dimension=0, tiled=True),
    )
    (
        grad_gate,
        grad_up,
        grad_down,
        grad_gain_one,
        grad_gain_q,
        grad_gain_k,
        grad_gain_two,
        grad_query,
        grad_key,
        grad_value,
        grad_out,
        grad_router,
    ) = (
        lax.all_gather(gate_shares, "ctx", axis=1, tiled=True),
        lax.all_gather(up_shares, "ctx", axis=1, tiled=True),
        lax.all_gather(down_shares, "ctx", axis=2, tiled=True),
        lax.all_gather(sum_gain_one, "ctx", axis=0, tiled=True),
        lax.all_gather(sum_gain_q, "ctx", axis=0, tiled=True),
        lax.all_gather(sum_gain_k, "ctx", axis=0, tiled=True),
        lax.all_gather(sum_gain_two, "ctx", axis=0, tiled=True),
        lax.all_gather(sum_query, "ctx", axis=0, tiled=True),
        lax.all_gather(sum_key, "ctx", axis=0, tiled=True),
        lax.all_gather(sum_value, "ctx", axis=0, tiled=True),
        lax.all_gather(sum_out, "ctx", axis=1, tiled=True),
        lax.all_gather(sum_router, "ctx", axis=0, tiled=True),
    )
    return (
        output,
        d_inputs,
        grad_gain_one,
        grad_query,
        grad_key,
        grad_value,
        grad_gain_q,
        grad_gain_k,
        grad_out,
        grad_gain_two,
        grad_router,
        grad_gate,
        grad_up,
        grad_down,
    )


def solution(mesh):
    in_specs = (
        P(("dp", "ctx"), None),
        P(("dp", "ctx"), None),
        P("dp", None),
        P(("dp", "ctx"), None),
        P("dp"),
        P("dp", "tp"),
        P("dp", "tp"),
        P("dp", "tp"),
        P("dp"),
        P("dp"),
        P("tp", "dp"),
        P("dp"),
        P("dp", None),
        P(None, "dp", "tp"),
        P(None, "dp", "tp"),
        P(None, "tp", "dp"),
    )
    out_specs = (
        P(("dp", "ctx"), None),
        P(("dp", "ctx"), None),
        P("dp"),
        P("dp", "tp"),
        P("dp", "tp"),
        P("dp", "tp"),
        P("dp"),
        P("dp"),
        P("tp", "dp"),
        P("dp"),
        P("dp", None),
        P(None, "dp", "tp"),
        P(None, "dp", "tp"),
        P(None, "tp", "dp"),
    )
    return jax.shard_map(body, mesh=mesh, in_specs=in_specs, out_specs=out_specs, check_vma=False)
```

profile of v0, /device:TPU:0, one launch (start us, length us, event | category | flops | bytes accessed | tf_op | source)
XLA Modules:
  0.0 7118.7 jit_solution(12242318818087587576)
XLA Ops:
  380.8 153.3 %all-gather.33.cloned.1.call-done = bf16[16,2048,256]{2,1,0:T(8,128)(2,1)} async-done(((bf16[16,1024,256]{2,1,0:T(8,128)(2,1)}), bf16[16,2048,256]{2,1,0:T(8,128)(2,1)}) %all-gather.33.cloned.1.call-update) | async-done | bytes 16777232 | tf_op jit(solution)/shard_map/all_gather | solution.py:90
  534.1 200.5 %all-gather.35.cloned.1.call-done = bf16[16,2048,256]{2,1,0:T(8,128)(2,1)} async-done(((bf16[16,1024,256]{2,1,0:T(8,128)(2,1)}), bf16[16,2048,256]{2,1,0:T(8,128)(2,1)}) %all-gather.35.cloned.1.call-update) | async-done | bytes 16777232 | tf_op jit(solution)/shard_map/all_gather | solution.py:91
  734.6 200.4 %all-gather.37.cloned.1.call-done = bf16[16,256,2048]{2,1,0:T(8,128)(2,1)} async-done(((bf16[16,256,1024]{2,1,0:T(8,128)(2,1)}), bf16[16,256,2048]{2,1,0:T(8,128)(2,1)}) %all-gather.37.cloned.1.call-update) | async-done | bytes 16777232 | tf_op jit(solution)/shard_map/all_gather | solution.py:92
  937.5 484.0 %while.100 = (s32[]{:T(128)}, f32[512,2048]{1,0:T(8,128)}, f32[16,320,256]{2,1,0:T(8,128)}, f32[16,320,256]{2,1,0:T(8,128)}, f32[16,320]{1,0:T(8,128)}, /*index=...) while((s32[]{:T(128)}, f32[512,2048]{1,0:T(8,128)}, ...), condition=%wide.region_24.25_spmd.clone, body=%wide.region_21.24_spmd.sunk.clone | while | flops 1009747584 | bytes 30301880 | solution.py:216
  1424.0 3623.5 %while.101 = (s32[]{:T(128)}, f32[512,2048]{1,0:T(8,128)}, f32[16,256,256]{2,1,0:T(8,128)}, f32[16,256,256]{2,1,0:T(8,128)}, f32[16,256,256]{2,1,0:T(8,128)}, /*...) while((s32[]{:T(128)}, f32[512,2048]{1,0:T(8,128)}, ...), condition=%wide.region_31.32_spmd.clone, body=%wide.region_26.31_spmd.sunk.clone | while | flops 2018756608 | bytes 67979128 | solution.py:258
  1580.3 69.6 reduce-scatter.29.cloned.1.call-done
  1806.6 69.3 reduce-scatter.29.cloned.1.call-done
  2032.4 69.5 reduce-scatter.29.cloned.1.call-done
  2258.7 69.6 reduce-scatter.29.cloned.1.call-done
  2485.0 69.9 reduce-scatter.29.cloned.1.call-done
  2711.8 69.6 reduce-scatter.29.cloned.1.call-done
  2938.2 69.7 reduce-scatter.29.cloned.1.call-done
  3164.4 69.6 reduce-scatter.29.cloned.1.call-done
  3391.0 69.7 reduce-scatter.29.cloned.1.call-done
  3617.6 69.6 reduce-scatter.29.cloned.1.call-done
  3773.3 69.3 reduce-scatter.27.cloned.1.call-done
  3844.3 69.6 reduce-scatter.29.cloned.1.call-done
  4070.9 69.5 reduce-scatter.29.cloned.1.call-done
  4297.0 69.5 reduce-scatter.29.cloned.1.call-done
  4523.1 69.7 reduce-scatter.29.cloned.1.call-done
  4749.5 69.7 reduce-scatter.29.cloned.1.call-done
  4976.3 69.5 reduce-scatter.29.cloned.1.call-done
  5174.1 98.3 %while.105 = (s32[]{:T(128)}, f32[512,4,128]{0,2,1:T(8,128)}, f32[2048,4,128]{0,2,1:T(8,128)}, f32[2048,4,128]{0,2,1:T(8,128)}, bf16[2048,4,128]{2,0,1:T(8,128)(...) while((s32[]{:T(128)}, f32[512,4,128]{0,2,1:T(8,128)}, ...), condition=%wide.region_41.42_spmd.clone.clone, body=%wide.region_40.41_spmd.clone.sunk.clone | while | flops 1355023360 | bytes 61120776 | solution.py:319
  5278.9 70.5 reduce-scatter.11.cloned.1.call-done
  5436.2 86.1 %reduce-scatter.21.cloned.1.call-done = f32[512,256]{1,0:T(8,128)} async-done(((f32[512,2048]{1,0:T(8,128)}), f32[512,256]{1,0:T(8,128)}) %reduce-scatter.21.cloned.1.call-update) | async-done | bytes 524304 | tf_op jit(solution)/shard_map/reduce_scatter | solution.py:382
  5530.9 83.1 %reduce-scatter.17.cloned.1.call-done = f32[256,512]{1,0:T(8,128)} async-done(((f32[2048,512]{1,0:T(8,128)}), f32[256,512]{1,0:T(8,128)}) %reduce-scatter.17.cloned.1.call-update) | async-done | bytes 524304 | tf_op jit(solution)/shard_map/reduce_scatter | solution.py:380
  5614.0 91.3 %reduce-scatter.15.cloned.1.call-done = f32[256,512]{1,0:T(8,128)} async-done(((f32[2048,512]{1,0:T(8,128)}), f32[256,512]{1,0:T(8,128)}) %reduce-scatter.15.cloned.1.call-update) | async-done | bytes 524304 | tf_op jit(solution)/shard_map/reduce_scatter | solution.py:379
  5705.4 92.4 %reduce-scatter.19.cloned.1.call-done = f32[256,512]{1,0:T(8,128)} async-done(((f32[2048,512]{1,0:T(8,128)}), f32[256,512]{1,0:T(8,128)}) %reduce-scatter.19.cloned.1.call-update) | async-done | bytes 524304 | tf_op jit(solution)/shard_map/reduce_scatter | solution.py:381
  5909.2 155.7 %all-reduce.17.cloned.1.call-done = (f32[512,2048]{1,0:T(8,128)}, f32[512,2048]{1,0:T(8,128)}) async-done(((f32[512,2048]{1,0:T(8,128)}, f32[512,2048]{1,0:T(8,128)}), (f32[512,2048]{1,0:T(8,128)}, f32[512,2048]{1,0:T(8,128)})) %all-reduce.17.cloned.1.call-update) | async-done | bytes 8388624 | tf_op jit(solution)/shard_map/psum | solution.py:221
  6206.0 286.9 %all-gather.47.cloned.1.call-done = f32[16,1024,256]{2,1,0:T(8,128)} async-done(((f32[16,256,256]{2,1,0:T(8,128)}), f32[16,1024,256]{2,1,0:T(8,128)}) %all-gather.47.cloned.1.call-update) | async-done | bytes 16777232 | tf_op jit(solution)/shard_map/all_gather | solution.py:399
  6493.0 286.4 %all-gather.49.cloned.1.call-done = f32[16,1024,256]{2,1,0:T(8,128)} async-done(((f32[16,256,256]{2,1,0:T(8,128)}), f32[16,1024,256]{2,1,0:T(8,128)}) %all-gather.49.cloned.1.call-update) | async-done | bytes 16777232 | tf_op jit(solution)/shard_map/all_gather | solution.py:400
  6779.4 286.4 %all-gather.51.cloned.1.call-done = f32[16,256,1024]{2,1,0:T(8,128)} async-done(((f32[16,256,256]{2,1,0:T(8,128)}), f32[16,256,1024]{2,1,0:T(8,128)}) %all-gather.51.cloned.1.call-update) | async-done | bytes 16777232 | tf_op jit(solution)/shard_map/all_gather | solution.py:401
  (1225 shorter events, 3996.5 us)
Async XLA Ops:
  119.2 214.2 %all-reduce.13.cloned.1.call-start = ((), (), s32[]{:S(2)}) async-start(), calls=%async_computation.16 | async-start | bytes 8388608 | tf_op jit(solution)/shard_map/psum | solution.py:195
  247.7 286.3 %all-gather.33.cloned.1.call-start = ((), (), s32[]{:S(2)}) async-start(), calls=%async_computation.17 | async-start | bytes 25165824 | tf_op jit(solution)/shard_map/all_gather | solution.py:90
  248.5 486.1 %all-gather.35.cloned.1.call-start = ((), (), s32[]{:S(2)}) async-start(), calls=%async_computation.18 | async-start | bytes 25165824 | tf_op jit(solution)/shard_map/all_gather | solution.py:91
  249.2 685.7 %all-gather.37.cloned.1.call-start = ((), (), s32[]{:S(2)}) async-start(), calls=%async_computation.19 | async-start | bytes 25165824 | tf_op jit(solution)/shard_map/all_gather | solution.py:92
  1443.1 206.8 %reduce-scatter.29.cloned.1.call-start = ((), (), s32[]{:S(2)}) async-start(), calls=%async_computation.38 | async-start | bytes 2359296 | tf_op jit(solution)/shard_map/while/body/eval_jaxpr/reduce_scatter | solution.py:249
  2122.4 205.9 %reduce-scatter.29.cloned.1.call-start = ((), (), s32[]{:S(2)}) async-start(), calls=%async_computation.38 | async-start | bytes 2359296 | tf_op jit(solution)/shard_map/while/body/eval_jaxpr/reduce_scatter | solution.py:249
  2348.8 206.1 %reduce-scatter.29.cloned.1.call-start = ((), (), s32[]{:S(2)}) async-start(), calls=%async_computation.38 | async-start | bytes 2359296 | tf_op jit(solution)/shard_map/while/body/eval_jaxpr/reduce_scatter | solution.py:249
  2575.4 206.0 %reduce-scatter.29.cloned.1.call-start = ((), (), s32[]{:S(2)}) async-start(), calls=%async_computation.38 | async-start | bytes 2359296 | tf_op jit(solution)/shard_map/while/body/eval_jaxpr/reduce_scatter | solution.py:249
  2801.9 205.9 %reduce-scatter.29.cloned.1.call-start = ((), (), s32[]{:S(2)}) async-start(), calls=%async_computation.38 | async-start | bytes 2359296 | tf_op jit(solution)/shard_map/while/body/eval_jaxpr/reduce_scatter | solution.py:249
  3028.4 205.7 %reduce-scatter.29.cloned.1.call-start = ((), (), s32[]{:S(2)}) async-start(), calls=%async_computation.38 | async-start | bytes 2359296 | tf_op jit(solution)/shard_map/while/body/eval_jaxpr/reduce_scatter | solution.py:249
  3254.6 206.1 %reduce-scatter.29.cloned.1.call-start = ((), (), s32[]{:S(2)}) async-start(), calls=%async_computation.38 | async-start | bytes 2359296 | tf_op jit(solution)/shard_map/while/body/eval_jaxpr/reduce_scatter | solution.py:249
  3481.2 206.0 %reduce-scatter.29.cloned.1.call-start = ((), (), s32[]{:S(2)}) async-start(), calls=%async_computation.38 | async-start | bytes 2359296 | tf_op jit(solution)/shard_map/while/body/eval_jaxpr/reduce_scatter | solution.py:249
  3707.7 206.2 %reduce-scatter.29.cloned.1.call-start = ((), (), s32[]{:S(2)}) async-start(), calls=%async_computation.38 | async-start | bytes 2359296 | tf_op jit(solution)/shard_map/while/body/eval_jaxpr/reduce_scatter | solution.py:249
  3934.5 206.0 %reduce-scatter.29.cloned.1.call-start = ((), (), s32[]{:S(2)}) async-start(), calls=%async_computation.38 | async-start | bytes 2359296 | tf_op jit(solution)/shard_map/while/body/eval_jaxpr/reduce_scatter | solution.py:249
  4160.9 205.6 %reduce-scatter.29.cloned.1.call-start = ((), (), s32[]{:S(2)}) async-start(), calls=%async_computation.38 | async-start | bytes 2359296 | tf_op jit(solution)/shard_map/while/body/eval_jaxpr/reduce_scatter | solution.py:249
  4387.0 205.9 %reduce-scatter.29.cloned.1.call-start = ((), (), s32[]{:S(2)}) async-start(), calls=%async_computation.38 | async-start | bytes 2359296 | tf_op jit(solution)/shard_map/while/body/eval_jaxpr/reduce_scatter | solution.py:249
  4613.4 205.8 %reduce-scatter.29.cloned.1.call-start = ((), (), s32[]{:S(2)}) async-start(), calls=%async_computation.38 | async-start | bytes 2359296 | tf_op jit(solution)/shard_map/while/body/eval_jaxpr/reduce_scatter | solution.py:249
  4839.7 206.1 %reduce-scatter.29.cloned.1.call-start = ((), (), s32[]{:S(2)}) async-start(), calls=%async_computation.38 | async-start | bytes 2359296 | tf_op jit(solution)/shard_map/while/body/eval_jaxpr/reduce_scatter | solution.py:249
  5048.1 301.3 %reduce-scatter.11.cloned.1.call-start = ((), (), s32[]{:S(2)}) async-start(), calls=%async_computation.21 | async-start | bytes 5242880 | tf_op jit(solution)/shard_map/reduce_scatter | solution.py:330
  5273.1 249.2 %reduce-scatter.21.cloned.1.call-start = ((), (), s32[]{:S(2)}) async-start(), calls=%async_computation.29 | async-start | bytes 4718592 | tf_op jit(solution)/shard_map/reduce_scatter | solution.py:382
  5278.9 335.1 %reduce-scatter.17.cloned.1.call-start = ((), (), s32[]{:S(2)}) async-start(), calls=%async_computation.25 | async-start | bytes 4718592 | tf_op jit(solution)/shard_map/reduce_scatter | solution.py:380
  5367.4 337.9 %reduce-scatter.15.cloned.1.call-start = ((), (), s32[]{:S(2)}) async-start(), calls=%async_computation.23 | async-start | bytes 4718592 | tf_op jit(solution)/shard_map/reduce_scatter | solution.py:379
  5375.4 422.4 %reduce-scatter.19.cloned.1.call-start = ((), (), s32[]{:S(2)}) async-start(), calls=%async_computation.27 | async-start | bytes 4718592 | tf_op jit(solution)/shard_map/reduce_scatter | solution.py:381
  5435.1 427.6 %reduce-scatter.23.cloned.1.call-start = ((), (), s32[]{:S(2)}) async-start(), calls=%async_computation.31 | async-start | bytes 147456 | tf_op jit(solution)/shard_map/reduce_scatter | solution.py:383
  5436.2 473.0 %all-gather.45.cloned.1.call-start = ((), (), s32[]{:S(2)}) async-start(), calls=%async_computation.30 | async-start | bytes 2621440 | tf_op jit(solution)/shard_map/all_gather | solution.py:409
  5522.3 542.6 %all-reduce.17.cloned.1.call-start = ((), (), s32[]{:S(2)}) async-start(), calls=%async_computation.35 | async-start | bytes 16777216 | tf_op jit(solution)/shard_map/psum | solution.py:221
  5530.8 627.6 %all-gather.41.cloned.1.call-start = ((), (), s32[]{:S(2)}) async-start(), calls=%async_computation.26 | async-start | bytes 2621440 | tf_op jit(solution)/shard_map/all_gather | solution.py:407
  5614.0 545.8 %all-gather.39.cloned.1.call-start = ((), (), s32[]{:S(2)}) async-start(), calls=%async_computation.24 | async-start | bytes 2621440 | tf_op jit(solution)/shard_map/all_gather | solution.py:406
  5705.3 500.7 %all-gather.43.cloned.1.call-start = ((), (), s32[]{:S(2)}) async-start(), calls=%async_computation.28 | async-start | bytes 2621440 | tf_op jit(solution)/shard_map/all_gather | solution.py:408
  5797.8 695.2 %all-gather.47.cloned.1.call-start = ((), (), s32[]{:S(2)}) async-start(), calls=%async_computation.32 | async-start | bytes 20971520 | tf_op jit(solution)/shard_map/all_gather | solution.py:399
  5798.4 981.0 %all-gather.49.cloned.1.call-start = ((), (), s32[]{:S(2)}) async-start(), calls=%async_computation.33 | async-start | bytes 20971520 | tf_op jit(solution)/shard_map/all_gather | solution.py:400
  5799.0 1266.8 %all-gather.51.cloned.1.call-start = ((), (), s32[]{:S(2)}) async-start(), calls=%async_computation.34 | async-start | bytes 20971520 | tf_op jit(solution)/shard_map/all_gather | solution.py:401
  (213 other events, 7247.9 us)
Sparse Core Ops, SparseCore 0:
  247.9 85.5 all-reduce.12
  335.0 198.9 all-gather.32
  535.7 198.8 all-gather.34
  736.1 198.8 all-gather.36
  1440.1 67.6 reduce-scatter.24
  1582.8 67.0 reduce-scatter.28
  2034.8 67.0 reduce-scatter.28
  2261.1 67.1 reduce-scatter.28
  2487.4 67.4 reduce-scatter.28
  2714.3 67.0 reduce-scatter.28
  2940.6 67.1 reduce-scatter.28
  3166.9 67.1 reduce-scatter.28
  3393.3 67.3 reduce-scatter.28
  3620.0 67.1 reduce-scatter.28
  3846.6 67.3 reduce-scatter.28
  4073.2 67.1 reduce-scatter.28
  4299.3 67.1 reduce-scatter.28
  4525.6 67.2 reduce-scatter.28
  4751.9 67.2 reduce-scatter.28
  4836.8 66.9 reduce-scatter.24
  4978.6 67.1 reduce-scatter.28
  5050.5 84.7 all-reduce.14
  5272.5 76.8 reduce-scatter.10
  5352.4 77.2 reduce-scatter.12
  5433.3 88.9 reduce-scatter.20
  5526.2 87.6 reduce-scatter.16
  5617.4 87.7 reduce-scatter.14
  5709.9 87.8 reduce-scatter.18
  5912.9 151.9 all-reduce.16
  6207.5 285.4 all-gather.46
  6494.4 284.9 all-gather.48
  6780.8 284.9 all-gather.50
  (42 shorter events, 2533.7 us)
where the time goes:
time: 7140 us; the launch traced here: 7120 us
  waiting for transfers between devices  5330 us (75%)
  local copies, waits for them, and re-layouts  621 us (9%)
  matrix products  581 us (8%)
  other arithmetic  420 us (6%)
  blocking collectives  141 us (2%)
    reduce_scatter x16, waiting for transfers between devices, expert_backward(): lax.psum_scatter(jnp.dot(inner.T, back, preferred_element_type=jnp.float3...  1110 us
    reduce_scatter x16, waiting for transfers between devices, expert_backward(): lax.psum_scatter(jnp.dot(taken.T, d_up, preferred_element_type=jnp.float3...  1110 us
    reduce_scatter x16, waiting for transfers between devices, expert_backward(): lax.psum_scatter(jnp.dot(taken.T, d_gate, preferred_element_type=jnp.floa...  716 us
    all_gather x1, waiting for transfers between devices, body(): lax.all_gather(gate_shares, 'ctx', axis=1, tiled=True)  287 us
    all_gather x1, waiting for transfers between devices, body(): lax.all_gather(down_shares, 'ctx', axis=2, tiled=True)  286 us
    all_gather x1, waiting for transfers between devices, body(): lax.all_gather(up_shares, 'ctx', axis=1, tiled=True)  286 us
    all_gather x1, waiting for transfers between devices, body(): lax.all_gather(w_up, 'dp', axis=1, tiled=True)  201 us
    all_gather x1, waiting for transfers between devices, body(): lax.all_gather(w_down, 'dp', axis=2, tiled=True)  200 us
  transfers between devices with their start and end apart: 74, of which 73 were waited for; matrix products, arithmetic and copies ran while one was open for 9% of the time, Pallas kernels for 0%

commit v1 on v0

v1 whole, which is shorter than its diff:
```python
import functools

import jax
import jax.numpy as jnp
from jax import lax
from jax.experimental import pallas as pl
from jax.experimental.pallas import tpu as pltpu
from jax.sharding import PartitionSpec as P

HEAD = 128
EPS = 1e-05
THETA = 10000.0
BLOCK = 256
BF16 = jnp.bfloat16
F32 = jnp.float32
MESH = pl.DeviceIdType.MESH
MICRO = 1 << 30


def dot(a, b):
    return jnp.dot(a, b, preferred_element_type=F32)


def dot_t(a, b):
    return lax.dot_general(a, b, (((1,), (1,)), ((), ())), preferred_element_type=F32)


def t_dot(a, b):
    return lax.dot_general(a, b, (((0,), (0,)), ((), ())), preferred_element_type=F32)


def rotation(row, first, rows):
    ends = jnp.cumsum(row)
    index = first + jnp.arange(rows, dtype=jnp.int32)
    before = jnp.where(index[:, None] >= ends[None, :], ends[None, :], 0)
    position = index - jnp.max(before, axis=1)
    inverse = THETA ** (-jnp.arange(0, HEAD, 2).astype(F32) / HEAD)
    angle = position.astype(F32)[:, None] * inverse[None, :]
    cosine, sine = jnp.cos(angle), jnp.sin(angle)
    return (
        jnp.concatenate([cosine, cosine], axis=1)[:, None, :],
        jnp.concatenate([-sine, sine], axis=1)[:, None, :],
    )


def rotate(v, cosine, sine):
    return v * cosine + jnp.roll(v, HEAD // 2, axis=2) * sine


def allowed_block(lengths_ref, base, rows, columns):
    index = base + lax.broadcasted_iota(jnp.int32, (rows, 1), 0)
    start = jnp.zeros((rows, 1), jnp.int32)
    end = 0
    for at in range(lengths_ref.shape[1]):
        end = end + lengths_ref[0, at]
        start = jnp.where(index >= end, end, start)
    key = lax.broadcasted_iota(jnp.int32, (rows, columns), 1)
    return (key >= start) & (key <= index)


def attend_kernel(lengths_ref, q_ref, k_ref, v_ref, out_ref, log_ref):
    scale = HEAD ** (-0.5)
    rows = q_ref.shape[0]
    for base in range(0, rows, BLOCK):
        upto = base + BLOCK
        own = pl.ds(base, BLOCK)
        keys, values = k_ref[pl.ds(0, upto), :], v_ref[pl.ds(0, upto), :]
        scores = dot_t(q_ref[own, :], keys) * scale
        scores = jnp.where(allowed_block(lengths_ref, base, BLOCK, upto), scores, -1e30)
        top = jnp.max(scores, axis=1, keepdims=True)
        weights = jnp.exp(scores - top)
        total = jnp.sum(weights, axis=1, keepdims=True)
        probs = (weights * (1.0 / total)).astype(BF16)
        out_ref[own, :] = dot(probs, values).astype(BF16)
        log_ref[own, :] = top + jnp.log(total)


def attend(lengths, q, k, v):
    heads, rows, _ = q.shape
    spec = pl.BlockSpec((None, rows, HEAD), lambda h: (h, 0, 0))
    column = pl.BlockSpec((None, rows, 1), lambda h: (h, 0, 0))
    return pl.pallas_call(
        attend_kernel,
        cost_estimate=pl.CostEstimate(flops=7 * MICRO, bytes_accessed=0, transcendentals=0),
        grid=(heads,),
        out_shape=(
            jax.ShapeDtypeStruct((heads, rows, HEAD), BF16),
            jax.ShapeDtypeStruct((heads, rows, 1), F32),
        ),
        in_specs=[pl.BlockSpec(memory_space=pltpu.SMEM), spec, spec, spec],
        out_specs=(spec, column),
        compiler_params=pltpu.CompilerParams(vmem_limit_bytes=48 << 20),
    )(lengths, q, k, v)


def attend_back_kernel(
    lengths_ref, q_ref, k_ref, v_ref, d_ref, log_ref, dq_ref, dk_ref, dv_ref, dk_sum, dv_sum
):
    scale = HEAD ** (-0.5)
    rows = q_ref.shape[0]
    dk_sum[...] = jnp.zeros_like(dk_sum)
    dv_sum[...] = jnp.zeros_like(dv_sum)
    for base in range(0, rows, BLOCK):
        upto = base + BLOCK
        own, seen = pl.ds(base, BLOCK), pl.ds(0, upto)
        q, d = q_ref[own, :], d_ref[own, :]
        keys, values = k_ref[seen, :], v_ref[seen, :]
        scores = dot_t(q, keys) * scale - log_ref[own, :]
        probs = jnp.where(
            allowed_block(lengths_ref, base, BLOCK, upto), jnp.exp(scores), 0.0
        )
        d_probs = dot_t(d, values)
        delta = jnp.sum(probs * d_probs, axis=1, keepdims=True)
        d_raw = (probs * (d_probs - delta) * scale).astype(BF16)
        dq_ref[own, :] = dot(d_raw, keys).astype(dq_ref.dtype)
        dk_sum[seen, :] += t_dot(d_raw, q)
        dv_sum[seen, :] += t_dot(probs.astype(BF16), d)
    dk_ref[...] = dk_sum[...].astype(dk_ref.dtype)
    dv_ref[...] = dv_sum[...].astype(dv_ref.dtype)


def attend_back(lengths, q, k, v, d, log):
    heads, rows, _ = q.shape
    spec = pl.BlockSpec((None, rows, HEAD), lambda h: (h, 0, 0))
    column = pl.BlockSpec((None, rows, 1), lambda h: (h, 0, 0))
    return pl.pallas_call(
        attend_back_kernel,
        cost_estimate=pl.CostEstimate(flops=10 * MICRO, bytes_accessed=0, transcendentals=0),
        grid=(heads,),
        out_shape=(jax.ShapeDtypeStruct((heads, rows, HEAD), BF16),) * 3,
        in_specs=[pl.BlockSpec(memory_space=pltpu.SMEM), spec, spec, spec, spec, column],
        out_specs=(spec,) * 3,
        scratch_shapes=[pltpu.VMEM((rows, HEAD), F32)] * 2,
        compiler_params=pltpu.CompilerParams(vmem_limit_bytes=48 << 20),
    )(lengths, q, k, v, d, log)


def to_heads(parts, heads):
    count = lax.axis_size("ctx")
    rows = parts[0].shape[0]
    stacked = jnp.stack([p.reshape(rows, count, heads // count, HEAD) for p in parts])
    sent = stacked.transpose(2, 0, 3, 1, 4)
    got = lax.all_to_all(sent, "ctx", 0, 0, tiled=True)
    return got.transpose(1, 2, 0, 3, 4).reshape(len(parts), heads // count, count * rows, HEAD)


def to_rows(parts):
    count = lax.axis_size("ctx")
    mine, pack, _ = parts[0].shape
    stacked = jnp.stack([p.reshape(mine, count, pack // count, HEAD) for p in parts])
    sent = stacked.transpose(2, 0, 1, 3, 4)
    got = lax.all_to_all(sent, "ctx", 0, 0, tiled=True)
    turned = got.transpose(1, 3, 0, 2, 4)
    return turned.reshape(len(parts), pack // count, count * mine, HEAD)


def expert_kernel(blocks, at_ref, hidden_ref, up_ref, chosen_ref, router_ref, *refs):
    gate_w, up_w, down_w = (refs[i * blocks : (i + 1) * blocks] for i in range(3))
    inner_ref, dgate_ref, dup_ref, dots_ref, grads_ref = refs[3 * blocks : 3 * blocks + 5]
    gate_sum, up_sum, down_sum = refs[3 * blocks + 5 :]
    turn, last = pl.program_id(0), pl.num_programs(0) - 1
    wide = gate_w[0].shape[0]
    hidden, upstream = hidden_ref[...], up_ref[...]

    def over(v, ws, f):
        return sum(f(v[:, s * wide : (s + 1) * wide], w[...]) for s, w in enumerate(ws))

    gate, up = over(hidden, gate_w, dot), over(hidden, up_w, dot)
    pulled = over(upstream, down_w, dot_t)
    logits = dot_t(hidden, router_ref[...])
    odds = jnp.exp(logits - jnp.max(logits, axis=1, keepdims=True))
    probs = odds / jnp.sum(odds, axis=1, keepdims=True) * chosen_ref[...]
    named = lax.broadcasted_iota(jnp.int32, probs.shape, 1) == at_ref[0]
    weight = jnp.sum(jnp.where(named, probs, 0.0), axis=1, keepdims=True)
    sigma = jax.nn.sigmoid(gate)
    active = gate * sigma
    inner = (active * up).astype(BF16).astype(F32)
    dots = jnp.sum(inner * pulled, axis=1, keepdims=True)
    dots_ref[...] = jnp.where(weight > 0.0, dots, 0.0)
    inner = (weight * inner).astype(BF16)
    pulled = weight * pulled
    d_gate = (pulled * up * sigma * (1.0 + gate * (1.0 - sigma))).astype(BF16)
    d_up = (pulled * active).astype(BF16)
    inner_ref[...], dgate_ref[...], dup_ref[...] = inner, d_gate, d_up

    @pl.when(turn == 0)
    def _():
        for total in (gate_sum, up_sum, down_sum):
            total[...] = jnp.zeros_like(total)

    gate_sum[...] += t_dot(d_gate, hidden)
    up_sum[...] += t_dot(d_up, hidden)
    down_sum[...] += t_dot(inner, upstream)

    @pl.when(turn == last)
    def _():
        fine = down_sum.shape[0]
        for s in range(blocks):
            own = pl.ds(s * wide, wide)
            grads_ref[s, 0] = gate_sum[:, own].T.astype(BF16)
            grads_ref[s, 1] = up_sum[:, own].T.astype(BF16)
            for j in range(wide // fine):
                grads_ref[s, 2, pl.ds(j * fine, fine), :] = down_sum[
                    :, pl.ds(s * wide + j * fine, fine)
                ].astype(BF16)


def expert(at, hidden, upstream, chosen, router, gate_w, up_w, down_w, tile=512):
    blocks = len(gate_w)
    pack, width = hidden.shape
    _, wide, fine = gate_w[0].shape

    def weight_spec(which, shape):
        return pl.BlockSpec((None,) + shape, lambda i, at_ref: (at_ref[which], 0, 0))

    ups = [weight_spec(0 if s == 0 else 1, (wide, fine)) for s in range(blocks)]
    downs = [weight_spec(0 if s == 0 else 1, (fine, wide)) for s in range(blocks)]
    def token(n):
        return pl.BlockSpec((tile, n), lambda i, at_ref: (i, 0))

    whole = pl.BlockSpec((blocks, 3, wide, fine), lambda i, at_ref: (0, 0, 0, 0))
    return pl.pallas_call(
        functools.partial(expert_kernel, blocks),
        cost_estimate=pl.CostEstimate(flops=27 * MICRO, bytes_accessed=0, transcendentals=0),
        grid_spec=pltpu.PrefetchScalarGridSpec(
            num_scalar_prefetch=1,
            grid=(pack // tile,),
            in_specs=[token(width), token(width), token(chosen.shape[1])]
            + [pl.BlockSpec(router.shape, lambda i, at_ref: (0, 0))]
            + ups
            + ups
            + downs,
            out_specs=[token(fine)] * 3 + [token(1), whole],
            scratch_shapes=[pltpu.VMEM((fine, width), F32)] * 3,
        ),
        out_shape=[jax.ShapeDtypeStruct((pack, fine), BF16)] * 3
        + [
            jax.ShapeDtypeStruct((pack, 1), F32),
            jax.ShapeDtypeStruct((blocks, 3, wide, fine), BF16),
        ],
        compiler_params=pltpu.CompilerParams(vmem_limit_bytes=56 << 20),
    )(at, hidden, upstream, chosen, router, *gate_w, *up_w, *down_w)

def signal_all(partners):
    barrier = pltpu.get_barrier_semaphore()
    count = 0
    for device, there in partners:

        @pl.when(there)
        def _():
            pl.semaphore_signal(barrier, inc=1, device_id=device, device_id_type=MESH)

        count = count + jnp.where(there, 1, 0)
    pl.semaphore_wait(barrier, count)


def place():
    c, t = lax.axis_index("ctx"), lax.axis_index("tp")
    core, side = lax.rem(t, 2), t // 2
    over_core = {"tp": t + 1 - 2 * core}
    over_side = {"tp": t + 2 - 4 * side}
    return c, lax.axis_size("ctx"), core, side, over_core, over_side


def remote(source, target, sems, at, device):
    send, recv = sems
    return pltpu.make_async_remote_copy(
        src_ref=source,
        dst_ref=target,
        send_sem=send.at[at],
        recv_sem=recv.at[at],
        device_id=device,
        device_id_type=MESH,
    )


def spread_kernel(x_ref, out_ref, local, zs, zr, ys, yr, cs, cr):
    c, n, core, side, over_core, over_side = place()
    rows, part = x_ref.shape
    left, right = {"ctx": c - 1}, {"ctx": c + 1}
    signal_all([(left, c > 0), (right, c < n - 1), (over_core, c >= 0), (over_side, c >= 0)])
    mine = core * 2 + side
    other = core * 2 + 1 - side

    def tile(owner, column):
        return out_ref.at[
            pl.ds(pl.multiple_of(owner * rows, rows), rows),
            pl.ds(pl.multiple_of(column * part, part), part),
        ]

    def along(owner, source, target, at):
        return remote(source, tile(owner, mine), (zs, zr), at, target)

    keep = pltpu.make_async_copy(x_ref, tile(c, mine), local)
    keep.start()

    @pl.when(c > 0)
    def _():
        along(c, x_ref, left, n + c).start()

    @pl.when(c < n - 1)
    def _():
        along(c, x_ref, right, c).start()

    def to_side(owner, source):
        return remote(source, tile(owner, mine), (ys, yr), owner, over_side)

    def to_core(owner, column, source, which):
        return remote(source, tile(owner, column), (cs, cr), which * n + owner, over_core)

    to_side(c, x_ref).start()
    to_core(c, mine, x_ref, 0).start()

    def from_side(owner):
        here = tile(owner, other)
        remote(here, here, (ys, yr), owner, over_side).wait_recv()
        to_core(owner, other, here, 1).start()

    from_side(c)
    for far in range(1, n):
        for sign, there, onward, more in (
            (-1, c - far >= 0, right, c < n - 1),
            (1, c + far < n, left, c > 0),
        ):
            owner = c + sign * far
            slot = owner if sign < 0 else n + owner

            @pl.when(there)
            def _():
                here = tile(owner, mine)
                along(owner, here, onward, slot).wait_recv()

                @pl.when(more)
                def _():
                    along(owner, here, onward, slot).start()

                to_side(owner, here).start()
                to_core(owner, mine, here, 0).start()

        for sign, there in ((-1, c - far >= 0), (1, c + far < n)):

            @pl.when(there)
            def _():
                from_side(c + sign * far)

    keep.wait()

    @pl.when(c > 0)
    def _():
        along(c, x_ref, left, n + c).wait_send()

    @pl.when(c < n - 1)
    def _():
        along(c, x_ref, right, c).wait_send()

    for far in range(1, n):
        for sign, there, onward, more in (
            (-1, c - far >= 0, right, c < n - 1),
            (1, c + far < n, left, c > 0),
        ):
            owner = c + sign * far

            @pl.when(there & more)
            def _():
                here = tile(owner, mine)
                along(owner, here, onward, owner if sign < 0 else n + owner).wait_send()

    for owner in range(n):
        to_side(owner, tile(owner, mine)).wait_send()
        to_core(owner, mine, tile(owner, mine), 0).wait_send()
        to_core(owner, other, tile(owner, other), 1).wait_send()
        for which, column in ((0, (1 - core) * 2 + side), (1, (1 - core) * 2 + 1 - side)):
            here = tile(owner, column)
            remote(here, here, (cs, cr), which * n + owner, over_core).wait_recv()


def spread(v, ident):
    n, tp = lax.axis_size("ctx"), lax.axis_size("tp")
    rows, part = v.shape
    dma = pltpu.SemaphoreType.DMA
    return pl.pallas_call(
        spread_kernel,
        cost_estimate=pl.CostEstimate(flops=60 * MICRO, bytes_accessed=0, transcendentals=0),
        out_shape=jax.ShapeDtypeStruct((n * rows, tp * part), v.dtype),
        in_specs=[pl.BlockSpec(memory_space=pl.ANY)],
        out_specs=pl.BlockSpec(memory_space=pl.ANY),
        scratch_shapes=[dma] + [dma((2 * n,))] * 2 + [dma((n,))] * 2 + [dma((2 * n,))] * 2,
        compiler_params=pltpu.CompilerParams(collective_id=ident, has_side_effects=True),
    )(v)


def join_kernel(x_ref, out_ref, local, ss, sr):
    c, n, core, side, over_core, over_side = place()
    rows, part = x_ref.shape
    signal_all([(over_core, c >= 0), (over_side, c >= 0)])
    mine, other = core * 2 + side, core * 2 + 1 - side

    def tile(column):
        return out_ref.at[:, pl.ds(pl.multiple_of(column * part, part), part)]

    keep = pltpu.make_async_copy(x_ref, tile(mine), local)
    keep.start()
    first = remote(x_ref, tile(mine), (ss, sr), 0, over_side)
    first.start()
    second = remote(x_ref, tile(mine), (ss, sr), 1, over_core)
    second.start()
    first.wait_recv()
    third = remote(tile(other), tile(other), (ss, sr), 2, over_core)
    third.start()
    keep.wait()
    first.wait_send()
    second.wait()
    third.wait()


def join(v, ident):
    tp = lax.axis_size("tp")
    rows, part = v.shape
    dma = pltpu.SemaphoreType.DMA
    return pl.pallas_call(
        join_kernel,
        cost_estimate=pl.CostEstimate(flops=25 * MICRO, bytes_accessed=0, transcendentals=0),
        out_shape=jax.ShapeDtypeStruct((rows, tp * part), v.dtype),
        in_specs=[pl.BlockSpec(memory_space=pl.ANY)],
        out_specs=pl.BlockSpec(memory_space=pl.ANY),
        scratch_shapes=[dma] + [dma((3,))] * 2,
        compiler_params=pltpu.CompilerParams(collective_id=ident, has_side_effects=True),
    )(v)


def collect_kernel(
    owners, x_ref, out_ref, core_in, side_out, side_in, z_out, z_in, cs, cr, ys, yr, zs, zr
):
    c, n, core, side, over_core, over_side = place()
    rows, part = out_ref.shape
    left, right = {"ctx": c - 1}, {"ctx": c + 1}
    partners = [(over_core, c >= 0), (over_side, c >= 0)]
    if owners > 1:
        partners += [(left, c > 0), (right, c < n - 1)]
    signal_all(partners)

    def owner_of(i):
        if owners == 1:
            return 0
        owner = 0
        for at in range(n):
            for turn, far in enumerate(sorted(range(n), key=lambda o: -abs(o - at))):
                owner = jnp.where((c == at) & (i == turn), far, owner)
        return owner

    def own_rows(owner):
        return pl.ds(pl.multiple_of(owner * rows, rows), rows)

    def half(which):
        return pl.ds(pl.multiple_of(which * 2 * part, 2 * part), 2 * part)

    def quarter(which):
        return pl.ds(pl.multiple_of((core * 2 + which) * part, part), part)

    def to_core(i):
        source = x_ref.at[own_rows(owner_of(i)), half(1 - core)]
        return remote(source, core_in.at[i], (cs, cr), i, over_core)

    def to_side(i):
        return remote(side_out.at[i], side_in.at[i], (ys, yr), i, over_side)

    def to_left(owner):
        return remote(z_out.at[owner], z_in.at[1, owner], (zs, zr), n + owner, left)

    def to_right(owner):
        return remote(z_out.at[owner], z_in.at[0, owner], (zs, zr), owner, right)

    def from_core(i, which):
        local = x_ref[own_rows(owner_of(i)), quarter(which)].astype(F32)
        near = core_in[i, :, pl.ds(pl.multiple_of(which * part, part), part)]
        return local + near.astype(F32)

    for i in range(owners):
        to_core(i).start()

    def finish(i):
        to_side(i).wait_recv()
        owner = owner_of(i)
        total = from_core(i, side) + side_in[i].astype(F32)
        if owners == 1:
            out_ref[...] = total
            return

        @pl.when(owner > c)
        def _():
            @pl.when(c > 0)
            def _():
                to_right(owner).wait_recv()
                z_out[owner] = (total + z_in[0, owner].astype(F32)).astype(z_out.dtype)

            @pl.when(c == 0)
            def _():
                z_out[owner] = total.astype(z_out.dtype)

            to_right(owner).start()

        @pl.when(owner < c)
        def _():
            @pl.when(c < n - 1)
            def _():
                to_left(owner).wait_recv()
                z_out[owner] = (total + z_in[1, owner].astype(F32)).astype(z_out.dtype)

            @pl.when(c == n - 1)
            def _():
                z_out[owner] = total.astype(z_out.dtype)

            to_left(owner).start()

        @pl.when(owner == c)
        def _():
            out_ref[...] = total

    def step(i, carry):
        @pl.when(i < owners)
        def _():
            to_core(i).wait_recv()
            side_out[i] = from_core(i, 1 - side).astype(side_out.dtype)
            to_side(i).start()

        @pl.when(i > 0)
        def _():
            finish(i - 1)

        return carry

    lax.fori_loop(0, owners + 1, step, 0)

    if owners > 1:

        @pl.when(c > 0)
        def _():
            to_right(c).wait_recv()
            out_ref[...] += z_in[0, c].astype(F32)

        @pl.when(c < n - 1)
        def _():
            to_left(c).wait_recv()
            out_ref[...] += z_in[1, c].astype(F32)

    def close(i, carry):
        to_core(i).wait_send()
        to_side(i).wait_send()
        if owners > 1:
            owner = owner_of(i)

            @pl.when(owner > c)
            def _():
                to_right(owner).wait_send()

            @pl.when(owner < c)
            def _():
                to_left(owner).wait_send()

        return carry

    lax.fori_loop(0, owners, close, 0)


def collect(v, owners, ident):
    n, tp = lax.axis_size("ctx"), lax.axis_size("tp")
    rows, part = v.shape[0] // owners, v.shape[1] // tp
    dma = pltpu.SemaphoreType.DMA
    z = n if owners > 1 else 1
    return pl.pallas_call(
        functools.partial(collect_kernel, owners),
        cost_estimate=pl.CostEstimate(flops=17 * MICRO, bytes_accessed=0, transcendentals=0),
        out_shape=jax.ShapeDtypeStruct((rows, part), F32),
        in_specs=[pl.BlockSpec(memory_space=pltpu.VMEM)],
        out_specs=pl.BlockSpec(memory_space=pltpu.VMEM),
        scratch_shapes=[
            pltpu.VMEM((owners, rows, 2 * part), BF16),
            pltpu.VMEM((owners, rows, part), BF16),
            pltpu.VMEM((owners, rows, part), BF16),
            pltpu.VMEM((z, rows, part), BF16),
            pltpu.VMEM((2, z, rows, part), BF16),
        ]
        + [dma((owners,))] * 4
        + [dma((2 * z,))] * 2,
        compiler_params=pltpu.CompilerParams(
            collective_id=ident, has_side_effects=True, vmem_limit_bytes=48 << 20
        ),
    )(v)


def returns_kernel(kinds, mine, blocks, flipped, with_dots, *refs):
    refs = list(refs)
    take = lambda count: [refs.pop(0) for _ in range(count)]
    lhs_refs, own_refs, other_refs = take(kinds * mine), take(kinds), take(kinds * (blocks - 1))
    dots_ref = take(1)[0] if with_dots else None
    out_ref = take(1)[0]
    dots_out = take(1)[0] if with_dots else None
    lhs, weights, core_out, core_in, keep, near, side_out, side_in, z_out, z_in = take(10)
    ls, ws, cs, cr, ys, yr, zs, zr = take(8)
    dots_in, ds, dr = take(3) if with_dots else (None, None, None)
    c, n, core, side, over_core, over_side = place()
    t, tp = lax.axis_index("tp"), lax.axis_size("tp")
    rows, part = out_ref.shape
    fine = lhs_refs[0].shape[1]
    wide = out_ref.shape[1] * tp // blocks
    half_blocks = blocks // 2
    left, right = {"ctx": c - 1}, {"ctx": c + 1}

    loads = []
    for k in range(kinds):
        for e in range(mine):
            at = k * mine + e
            columns = pl.ds(at * fine, fine)
            loads.append(pltpu.make_async_copy(lhs_refs[at], lhs.at[:, columns], ls.at[at]))
            for s in range(blocks):
                source = own_refs[k].at[c * mine + e] if s == 0 else other_refs[k * (blocks - 1) + s - 1].at[e]
                target = weights.at[s, columns, :] if flipped else weights.at[s, :, columns]
                loads.append(pltpu.make_async_copy(source, target, ws.at[at * blocks + s]))
    for load in loads:
        load.start()
    if with_dots:
        others = []
        for far_c in range(n):
            for far_t in range(tp):
                others.append(({"ctx": far_c, "tp": far_t}, (c != far_c) | (t != far_t)))
        signal_all(others)
    else:
        signal_all(
            [(over_core, c >= 0), (over_side, c >= 0), (left, c > 0), (right, c < n - 1)]
        )

    def own_rows(owner):
        return pl.ds(pl.multiple_of(owner * rows, rows), rows)

    def dots_copy(owner, far_t):
        source = dots_ref.at[:, own_rows(owner)]
        return pltpu.make_async_remote_copy(
            src_ref=source,
            dst_ref=dots_in.at[c * tp + t],
            send_sem=ds.at[owner * tp + far_t],
            recv_sem=dr.at[c * tp + t],
            device_id={"ctx": owner, "tp": far_t},
            device_id_type=MESH,
        )

    def dots_from(at):
        here = dots_in.at[at]
        return pltpu.make_async_remote_copy(
            src_ref=here,
            dst_ref=here,
            send_sem=ds.at[at],
            recv_sem=dr.at[at],
            device_id=over_core,
            device_id_type=MESH,
        )

    if with_dots:
        for owner in range(n):
            for far_t in range(tp):

                @pl.when((c != owner) | (t != far_t))
                def _():
                    dots_copy(owner, far_t).start()

        dots_in[c * tp + t] = dots_ref[:, own_rows(c)]

    for load in loads:
        load.wait()

    def owner_of(i):
        owner = 0
        for at in range(n):
            for turn, far in enumerate(sorted(range(n), key=lambda o: -abs(o - at))):
                owner = jnp.where((c == at) & (i == turn), far, owner)
        return owner

    def to_core(i):
        return remote(core_out.at[i], core_in.at[i], (cs, cr), i, over_core)

    def to_side(i):
        return remote(side_out.at[i], side_in.at[i], (ys, yr), i, over_side)

    def to_left(owner):
        return remote(z_out.at[owner], z_in.at[1, owner], (zs, zr), n + owner, left)

    def to_right(owner):
        return remote(z_out.at[owner], z_in.at[0, owner], (zs, zr), owner, right)

    def product(i, which, into):
        taken = lhs[own_rows(owner_of(i)), :]
        for j in range(half_blocks):
            w = weights[which * half_blocks + j]
            into(j, dot(taken, w) if flipped else dot_t(taken, w))

    def columns_of(j):
        return pl.ds(j * wide, wide)

    def quarter(which):
        return pl.ds(pl.multiple_of(which * part, part), part)

    def begin(i):
        def send_part(j, v):
            core_out[i, :, columns_of(j)] = v.astype(core_out.dtype)

        def keep_part(j, v):
            keep[lax.rem(i, 2), :, columns_of(j)] = v

        product(i, 1 - core, send_part)
        to_core(i).start()
        product(i, core, keep_part)

    def cross(i):
        to_core(i).wait_recv()
        slot = lax.rem(i, 2)

        def summed(which):
            return keep[slot, :, quarter(which)] + core_in[i, :, quarter(which)].astype(F32)

        side_out[i] = summed(1 - side).astype(side_out.dtype)
        to_side(i).start()
        near[slot] = summed(side)

    def finish(i):
        to_side(i).wait_recv()
        owner = owner_of(i)
        total = near[lax.rem(i, 2)] + side_in[i].astype(F32)

        @pl.when(owner > c)
        def _():
            @pl.when(c > 0)
            def _():
                to_right(owner).wait_recv()
                z_out[owner] = (total + z_in[0, owner].astype(F32)).astype(z_out.dtype)

            @pl.when(c == 0)
            def _():
                z_out[owner] = total.astype(z_out.dtype)

            to_right(owner).start()

        @pl.when(owner < c)
        def _():
            @pl.when(c < n - 1)
            def _():
                to_left(owner).wait_recv()
                z_out[owner] = (total + z_in[1, owner].astype(F32)).astype(z_out.dtype)

            @pl.when(c == n - 1)
            def _():
                z_out[owner] = total.astype(z_out.dtype)

            to_left(owner).start()

        @pl.when(owner == c)
        def _():
            out_ref[...] = total

    def step(i, carry):
        @pl.when(i < n)
        def _():
            begin(i)

        @pl.when(i > 1)
        def _():
            finish(i - 2)

        @pl.when((i > 0) & (i <= n))
        def _():
            cross(i - 1)

        return carry

    lax.fori_loop(0, n + 2, step, 0)

    @pl.when(c > 0)
    def _():
        to_right(c).wait_recv()
        out_ref[...] += z_in[0, c].astype(F32)

    @pl.when(c < n - 1)
    def _():
        to_left(c).wait_recv()
        out_ref[...] += z_in[1, c].astype(F32)

    if with_dots:
        for at in range(n * tp):

            @pl.when(c * tp + t != at)
            def _():
                dots_from(at).wait_recv()

        for at in range(n):
            dots_out[at] = sum(dots_in[at * tp + far_t] for far_t in range(tp))
        for owner in range(n):
            for far_t in range(tp):

                @pl.when((c != owner) | (t != far_t))
                def _():
                    dots_copy(owner, far_t).wait_send()

    def close(i, carry):
        to_core(i).wait_send()
        to_side(i).wait_send()
        owner = owner_of(i)

        @pl.when(owner > c)
        def _():
            to_right(owner).wait_send()

        @pl.when(owner < c)
        def _():
            to_left(owner).wait_send()

        return carry

    lax.fori_loop(0, n, close, 0)


def returns(lhs, own, others, dots, flipped, ident):
    n, tp = lax.axis_size("ctx"), lax.axis_size("tp")
    kinds, mine = len(lhs), len(lhs[0])
    blocks = len(others[0]) + 1
    pack, fine = lhs[0][0].shape
    wide = own[0].shape[2 if flipped else 1]
    rows, part = pack // n, wide * blocks // tp
    deep = kinds * mine * fine
    dma, vmem = pltpu.SemaphoreType.DMA, pltpu.VMEM
    hbm = pl.BlockSpec(memory_space=pl.ANY)
    near = pl.BlockSpec(memory_space=pltpu.VMEM)
    operands = [v for kind in lhs for v in kind] + list(own) + [v for kind in others for v in kind]
    in_specs = [hbm] * len(operands)
    out_shape = [jax.ShapeDtypeStruct((rows, part), F32)]
    extra = []
    if dots is not None:
        operands.append(dots)
        in_specs.append(near)
        out_shape.append(jax.ShapeDtypeStruct((n, mine, rows), F32))
        extra = [vmem((n * tp, mine, rows), F32), dma((n * tp,)), dma((n * tp,))]
    return pl.pallas_call(
        functools.partial(returns_kernel, kinds, mine, blocks, flipped, dots is not None),
        cost_estimate=pl.CostEstimate(flops=65 * MICRO, bytes_accessed=0, transcendentals=0),
        out_shape=out_shape,
        in_specs=in_specs,
        out_specs=[near] * len(out_shape),
        scratch_shapes=[
            vmem((pack, deep), BF16),
            vmem((blocks, deep, wide) if flipped else (blocks, wide, deep), BF16),
            vmem((n, rows, 2 * part), BF16),
            vmem((n, rows, 2 * part), BF16),
            vmem((2, rows, 2 * part), F32),
            vmem((2, rows, part), F32),
            vmem((n, rows, part), BF16),
            vmem((n, rows, part), BF16),
            vmem((n, rows, part), BF16),
            vmem((2, n, rows, part), BF16),
            dma((kinds * mine,)),
            dma((kinds * mine * blocks,)),
        ]
        + [dma((n,))] * 4
        + [dma((2 * n,))] * 2
        + extra,
        compiler_params=pltpu.CompilerParams(
            collective_id=ident, has_side_effects=True, vmem_limit_bytes=56 << 20
        ),
    )(*operands)


def body(
    tokens,
    cotangent,
    lengths,
    routes,
    attn_gain,
    w_query,
    w_key,
    w_value,
    q_gain,
    k_gain,
    w_out,
    mlp_gain,
    w_router,
    w_gate,
    w_up,
    w_down,
):
    dp_at, ctx_at, tp_at = (lax.axis_index(a) for a in ("dp", "ctx", "tp"))
    dp_count, ctx_count, tp_count = (lax.axis_size(a) for a in ("dp", "ctx", "tp"))
    rows, width = tokens.shape
    wide = w_query.shape[0]
    local = w_query.shape[1]
    heads = local // HEAD
    experts = w_router.shape[1]
    mine = experts // ctx_count
    part = width // tp_count
    column_at = lax.rem(tp_at, 2) * 2 + tp_at // 2

    def fetch(v):
        others = [
            lax.ppermute(v, "dp", [((i + s) % dp_count, i) for i in range(dp_count)])
            for s in range(1, dp_count)
        ]
        return [v] + others

    def hand_over(blocks):
        total = blocks[0].astype(F32)
        for s in range(1, dp_count):
            pairs = [(i, (i + s) % dp_count) for i in range(dp_count)]
            total = total + lax.ppermute(blocks[s].astype(BF16), "dp", pairs).astype(F32)
        return total

    def columns(v):
        return lax.dynamic_slice_in_dim(v, column_at * part, part, v.ndim - 1)

    def block(v, s):
        return v[:, s * wide : (s + 1) * wide]

    def own_experts(w):
        return lax.dynamic_slice_in_dim(w, ctx_at * mine, mine, 0)

    small = jnp.concatenate(
        [attn_gain[None], q_gain[None], k_gain[None], mlp_gain[None], w_router.T], axis=0
    )
    small = jnp.concatenate(fetch(small), axis=1)
    gains = small[:4].astype(F32)
    router_w = small[4:]
    gain_one, gain_two = gains[0], columns(gains[3])

    def heads_gain(v):
        back = jnp.roll(v, dp_at * wide)
        return lax.dynamic_slice_in_dim(back, tp_at * local, local)

    gain_q, gain_k = heads_gain(gains[1]), heads_gain(gains[2])
    query_w, key_w, value_w = fetch(w_query), fetch(w_key), fetch(w_value)
    out_w = fetch(w_out)
    gate_others = fetch(own_experts(w_gate))[1:]
    up_others = fetch(own_experts(w_up))[1:]
    down_others = fetch(own_experts(w_down))[1:]
    tokens = jnp.roll(tokens, -dp_at * wide, axis=1)
    cotangent = jnp.roll(cotangent, -dp_at * wide, axis=1)
    chosen = jnp.any(
        routes[:, :, None] == jnp.arange(experts, dtype=jnp.int32)[None, None, :], axis=1
    )
    upstream_all = jnp.concatenate(
        [
            lax.dynamic_slice_in_dim(cotangent, tp_at * part, part, 1),
            jnp.pad(chosen.astype(BF16), ((0, 0), (0, HEAD - experts))),
        ],
        axis=1,
    )
    upstream_all = lax.all_gather(upstream_all, "ctx", axis=0, tiled=True)
    chosen_all = upstream_all[:, part : part + experts].astype(F32)
    upstream_all = lax.all_gather(upstream_all[:, :part], "tp", axis=1, tiled=True)

    inputs = tokens.astype(F32)
    scale_one = lax.rsqrt(jnp.mean(inputs * inputs, axis=1, keepdims=True) + EPS)
    hidden_one = (inputs * scale_one * gain_one).astype(BF16)

    def project(blocks):
        return sum(dot(block(hidden_one, s), w) for s, w in enumerate(blocks))

    q_raw, k_raw = project(query_w), project(key_w)
    values = project(value_w).astype(BF16)
    squares = lax.psum(
        jnp.stack([jnp.sum(q_raw * q_raw, axis=1), jnp.sum(k_raw * k_raw, axis=1)]), "tp"
    )
    q_scale, k_scale = lax.rsqrt(squares / width + EPS)[:, :, None]
    q_hat, k_hat = q_raw * q_scale, k_raw * k_scale
    cosine, sine = rotation(lengths[0], ctx_at * rows, rows)

    def turn(v):
        return rotate(v.reshape(rows, heads, HEAD), cosine, sine).astype(BF16)

    q_all, k_all, v_all = to_heads(
        (turn(q_hat * gain_q), turn(k_hat * gain_k), values), heads
    )
    q_all, out_w, gate_others = lax.optimization_barrier((q_all, out_w, gate_others))
    attended_all, log = attend(lengths, q_all, k_all, v_all)
    attended = to_rows((attended_all,))[0].reshape(rows, local)
    branch = jnp.concatenate([dot(attended, w).astype(BF16) for w in out_w], axis=1)
    branch, up_others = lax.optimization_barrier((branch, up_others))
    branch = collect(branch, 1, 2)
    inputs_c = columns(inputs)
    mixed = inputs_c + branch
    square = lax.psum(jnp.sum(mixed * mixed, axis=1), "tp")
    scale_two = lax.rsqrt(square / width + EPS)[:, None]
    normed_two = mixed * scale_two
    hidden_mine = (normed_two * gain_two).astype(BF16)
    hidden_two = spread(hidden_mine, 3)
    hidden_two, down_others = lax.optimization_barrier((hidden_two, down_others))

    parts, sums = [], []
    for e in range(mine):
        at = ctx_at * mine + e
        if e > 1:
            hidden_two, sums[e - 2] = lax.optimization_barrier((hidden_two, sums[e - 2]))
        parts.append(
            expert(
                jnp.stack([at, jnp.int32(e)]).astype(jnp.int32),
                hidden_two,
                upstream_all,
                chosen_all,
                router_w,
                [w_gate] + gate_others,
                [w_up] + up_others,
                [w_down] + down_others,
            )
        )
        sums.append(hand_over(list(parts[-1][-1])).astype(BF16))

    gathered = [lax.all_gather(v, "ctx", axis=0, tiled=False) for v in sums]

    dots = jnp.concatenate([p[3] for p in parts], axis=1).T
    expert_in, dots = returns(
        [[p[1] for p in parts], [p[2] for p in parts]],
        [w_gate, w_up],
        [gate_others, up_others],
        dots,
        False,
        4,
    )

    dots = dots.reshape(experts, rows).T
    hidden_rows = lax.dynamic_slice_in_dim(hidden_two, ctx_at * rows, rows, 0)
    route_mine = jax.nn.softmax(dot_t(hidden_rows, router_w), axis=1)
    d_logits = (
        route_mine * (dots - jnp.sum(route_mine * dots, axis=1, keepdims=True))
    ).astype(BF16)
    router_grad = t_dot(d_logits, hidden_mine)
    d_hidden_two = expert_in + dot(d_logits, columns(router_w))
    gain_two_grad = jnp.sum(d_hidden_two * normed_two, axis=0)
    pull_two = d_hidden_two * gain_two
    mean_two = lax.psum(jnp.sum(pull_two * mixed, axis=1), "tp")[:, None] / width
    d_mixed = (
        columns(cotangent).astype(F32) + scale_two * pull_two - mixed * scale_two**3 * mean_two
    )

    d_branch = join(d_mixed.astype(BF16), 7)
    d_attended = sum(dot_t(block(d_branch, s), w) for s, w in enumerate(out_w)).astype(BF16)
    d_all = to_heads((d_attended,), heads)[0]
    d_all, gathered[0] = lax.optimization_barrier((d_all, gathered[0]))
    dq_all, dk_all, dv_all = attend_back(lengths, q_all, k_all, v_all, d_all, log)
    d_query, d_key, d_value = to_rows((dq_all, dk_all, dv_all))
    d_values_raw = d_value.reshape(rows, local)
    d_q_normed = rotate(d_query.astype(F32), cosine, -sine).reshape(rows, local)
    d_k_normed = rotate(d_key.astype(F32), cosine, -sine).reshape(rows, local)
    q_pull, k_pull = d_q_normed * gain_q, d_k_normed * gain_k
    totals = lax.psum(
        jnp.stack([jnp.sum(q_pull * q_raw, axis=1), jnp.sum(k_pull * k_raw, axis=1)]), "tp"
    )
    q_mean, k_mean = totals[:, :, None] / width
    d_q_raw = (q_scale * q_pull - q_raw * q_scale**3 * q_mean).astype(BF16)
    d_k_raw = (k_scale * k_pull - k_raw * k_scale**3 * k_mean).astype(BF16)
    d_hidden = jnp.concatenate(
        [
            (
                dot_t(d_q_raw, query_w[s])
                + dot_t(d_k_raw, key_w[s])
                + dot_t(d_values_raw, value_w[s])
            ).astype(BF16)
            for s in range(dp_count)
        ],
        axis=1,
    )
    d_hidden, gathered[1] = lax.optimization_barrier((d_hidden, gathered[1]))
    d_hidden = collect(d_hidden, 1, 8)
    gain_one_grad = jnp.sum(d_hidden * inputs_c * scale_one, axis=0)
    pull_one = d_hidden * columns(gain_one)
    mean_one = lax.psum(jnp.sum(pull_one * inputs_c, axis=1), "tp")[:, None] / width
    d_inputs = d_mixed + scale_one * pull_one - inputs_c * scale_one**3 * mean_one
    d_inputs = jnp.roll(join(d_inputs, 9), dp_at * wide, axis=1)

    def in_order(v):
        return jnp.roll(v, dp_at * wide, axis=-1)

    small_grads = jnp.concatenate(
        [
            gain_one_grad[None],
            gain_two_grad[None],
            router_grad,
            jnp.sum(d_q_normed * q_hat, axis=0)[None],
            jnp.sum(d_k_normed * k_hat, axis=0)[None],
        ]
    )
    small_grads = lax.all_gather(small_grads, "tp", axis=0, tiled=False)
    turned = [small_grads[(p % 2) * 2 + p // 2, : 2 + experts] for p in range(tp_count)]
    heads_grads = small_grads[:, 2 + experts :].transpose(1, 0, 2).reshape(2, width)
    heads_grads = jnp.roll(heads_grads, -dp_at * wide, axis=1)
    small_grads = jnp.concatenate([jnp.concatenate(turned, axis=1), heads_grads])
    small_rows = small_grads.shape[0] * wide // local
    filler = -small_rows % (16 * ctx_count)

    def grad_blocks(s):
        hidden, grads = block(hidden_one, s), (d_q_raw, d_k_raw, d_values_raw)
        small = block(small_grads, s).reshape(small_rows, local)
        return jnp.concatenate(
            [t_dot(hidden, d) for d in grads]
            + [t_dot(block(d_branch, s), attended), jnp.pad(small, ((0, filler), (0, 0)))]
        )

    grads = hand_over([grad_blocks(s) for s in range(dp_count)]).astype(BF16)
    grads = lax.psum_scatter(grads, "ctx", scatter_dimension=0, tiled=True)
    grads = lax.all_gather(grads, "ctx", axis=0, tiled=True).astype(F32)
    grad_query, grad_key, grad_value, grad_out = (
        grads[i * wide : (i + 1) * wide] for i in range(4)
    )
    small_grads = grads[4 * wide : 4 * wide + small_rows].reshape(-1, wide)

    inners = [p[0] for p in parts]
    inners, d_inputs = lax.optimization_barrier((inners, d_inputs))
    (mixture,) = returns([inners], [w_down], [down_others], None, True, 5)
    mixture, gathered[2] = lax.optimization_barrier((mixture, gathered[2]))
    output = jnp.roll(join(mixed + mixture, 6), dp_at * wide, axis=1)

    fine = w_gate.shape[2]

    def assemble(which):
        each = [v[:, which].astype(F32) for v in gathered]
        if which == 2:
            each = [
                v.reshape(ctx_count, wide // fine, fine, fine)
                .transpose(0, 2, 1, 3)
                .reshape(ctx_count, fine, wide)
                for v in each
            ]
        stacked = jnp.stack(each, axis=1)
        return stacked.reshape((experts,) + stacked.shape[2:])

    return (
        output,
        d_inputs,
        small_grads[0],
        grad_query,
        grad_key,
        grad_value,
        small_grads[2 + experts],
        small_grads[3 + experts],
        grad_out.T,
        small_grads[1],
        small_grads[2 : 2 + experts].T,
        assemble(0),
        assemble(1),
        assemble(2),
    )


def solution(mesh):
    in_specs = (
        P(("dp", "ctx"), None),
        P(("dp", "ctx"), None),
        P("dp", None),
        P(("dp", "ctx"), None),
        P("dp"),
        P("dp", "tp"),
        P("dp", "tp"),
        P("dp", "tp"),
        P("dp"),
        P("dp"),
        P("tp", "dp"),
        P("dp"),
        P("dp", None),
        P(None, "dp", "tp"),
        P(None, "dp", "tp"),
        P(None, "tp", "dp"),
    )
    out_specs = (
        P(("dp", "ctx"), None),
        P(("dp", "ctx"), None),
        P("dp"),
        P("dp", "tp"),
        P("dp", "tp"),
        P("dp", "tp"),
        P("dp"),
        P("dp"),
        P("tp", "dp"),
        P("dp"),
        P("dp", None),
        P(None, "dp", "tp"),
        P(None, "dp", "tp"),
        P(None, "tp", "dp"),
    )
    return jax.shard_map(body, mesh=mesh, in_specs=in_specs, out_specs=out_specs, check_vma=False)
```

time: 7140 us -> 1270 us (0.18)
  waiting for transfers between devices: 5330 us -> 380 us
  matrix products: 581 us -> 40.7 us
  local copies, waits for them, and re-layouts: 621 us -> 120 us
  Pallas kernels: 0 us -> 491 us
  other arithmetic: 420 us -> 121 us
  blocking collectives: 141 us -> 36.5 us
    reduce_scatter x55 -> x1, waiting for transfers between devices: 3470 us -> 0.01 us  [body(): grads = lax.psum_scatter(grads, 'ctx', scatter_dimension=0, tiled=True)]
    all_gather x16 -> x7, waiting for transfers between devices: 1620 us -> 46.4 us  [the longest x1 46.3 us: body(): grads = lax.all_gather(grads, 'ctx', axis=0, tiled=True).astype(F32)]
    dot_general x195 -> x27, matrix products: 581 us -> 40.7 us  [the longest x9 15.8 us: dot(): return jnp.dot(a, b, preferred_element_type=F32)]
    pallas_call x0 -> x14, Pallas kernels: none -> 491 us  [the longest x2 188 us: returns(): pl.pallas_call(functools.partial(returns_kernel, kinds, mine, blocks, fli...]
    gather x69 -> x0, local copies, waits for them, and re-layouts: 375 us -> none  [the longest x16 114 us: expert_forward(): return (acc, (gate, up, jnp.sum(upstream[picked] * result, axis=1)))]
    scatter-add x32 -> x0, other arithmetic: 318 us -> none  [the longest x16 161 us: expert_forward(): acc = acc.at[picked].add(weight[:, None] * result)]
    ppermute x0 -> x13, waiting for transfers between devices: none -> 234 us  [the longest x5 143 us: hand_over(): lax.ppermute(blocks[s].astype(BF16), 'dp', pairs).astype(F32)]
    psum x3 -> x0, waiting for transfers between devices: 226 us -> none  [the longest x1 156 us: body(): output = mixed + lax.psum(mixture, 'tp')]
  transfers between devices with their start and end apart: 74 -> 25, of which waited for: 73 -> 14; matrix products, arithmetic and copies ran while one was open for 9% -> 20% of each run, Pallas kernels for 0% -> 37%
where the time goes in v1:
time: 1270 us; the launch traced here: 1250 us
  Pallas kernels  491 us (39%)
  waiting for transfers between devices  380 us (30%)
  other arithmetic  121 us (10%)
  local copies, waits for them, and re-layouts  120 us (9%)
  starting transfers between devices  48.7 us (4%)
  matrix products  40.7 us (3%)
  blocking collectives  36.5 us (3%)
  between operations  15.7 us (1%)
    pallas_call x2, Pallas kernels, returns(): pl.pallas_call(functools.partial(returns_kernel, kinds, mine, blocks, fli...  188 us
    ppermute x5, waiting for transfers between devices, hand_over(): lax.ppermute(blocks[s].astype(BF16), 'dp', pairs).astype(F32)  143 us
    pallas_call x4, Pallas kernels, expert(): pl.pallas_call(functools.partial(expert_kernel, blocks), cost_estimate=pl...  104 us
    ppermute x8, waiting for transfers between devices, fetch(): lax.ppermute(v, 'dp', [((i + s) % dp_count, i) for i in range(dp_count)])  90.6 us
    pallas_call x3, Pallas kernels, join(): pl.pallas_call(join_kernel, cost_estimate=pl.CostEstimate(flops=25 * MICR...  86.8 us
    pallas_call x1, Pallas kernels, spread(): pl.pallas_call(spread_kernel, cost_estimate=pl.CostEstimate(flops=60 * MI...  62.1 us
    all_to_all x2, waiting for transfers between devices, to_rows(): got = lax.all_to_all(sent, 'ctx', 0, 0, tiled=True)  59.1 us
    all_gather x1, waiting for transfers between devices, body(): grads = lax.all_gather(grads, 'ctx', axis=0, tiled=True).astype(F32)  46.3 us
  transfers between devices with their start and end apart: 25, of which 14 were waited for; matrix products, arithmetic and copies ran while one was open for 20% of the time, Pallas kernels for 37%

profile of v1, /device:TPU:0, one launch (start us, length us, event | category | flops | bytes accessed | tf_op | source)
XLA Modules:
  0.0 1254.4 jit_solution(16933696754336021582)
XLA Ops:
  45.2 17.5 %collective-permute-done.1 = bf16[1024,512]{1,0:T(8,128)(2,1)S(1)} collective-permute-done((bf16[1024,512]{1,0:T(8,128)(2,1)}, bf16[1024,512]{1,0:T(8,128)(2,1)S(1)}, u32[]{:S(2)}, u32[]{:S(2)}) %collective-permute-start.1) | collective-permute-done | bytes 1048608 | tf_op jit(solution)/shard_map/ppermute | solution.py:899
  66.0 17.8 %collective-permute-done.2 = bf16[1024,512]{1,0:T(8,128)(2,1)} collective-permute-done((bf16[1024,512]{1,0:T(8,128)(2,1)}, bf16[1024,512]{1,0:T(8,128)(2,1)}, u32[]{:S(2)}, u32[]{:S(2)}) %collective-permute-start.2) | collective-permute-done | bytes 1048608 | tf_op jit(solution)/shard_map/ppermute | solution.py:899
  133.1 18.4 %all-to-all-done = bf16[4,3,1,512,128]{4,3,2,1,0:T(8,128)(2,1)S(1)} async-done(((bf16[4,3,1,512,128]{4,3,2,1,0:T(8,128)(2,1)}), bf16[4,3,1,512,128]{4,3,2,1,0:T(8,128)(2,1)S(1)}, u32[]{:S(2)}, u32[]{:S(2)}) %all-to-all-start) | async-done | bytes 1572896 | tf_op jit(solution)/shard_map/all_to_all | solution.py:143
  151.7 37.7 %collective-permute-done.4 = bf16[512,1024]{1,0:T(8,128)(2,1)} collective-permute-done((bf16[512,1024]{1,0:T(8,128)(2,1)S(1)}, bf16[512,1024]{1,0:T(8,128)(2,1)}, u32[]{:S(2)}, u32[]{:S(2)}) %collective-permute-start.4) | collective-permute-done | bytes 1048608 | tf_op jit(solution)/shard_map/ppermute | solution.py:899
  189.4 7.1 shard_map.263
  206.4 8.5 all-to-all-done.1
  218.1 16.3 %collective-permute-done.6.refs_3_.refs_11_ = bf16[4,1024,256]{2,1,0:T(8,128)(2,1)} collective-permute-done((bf16[4,1024,256]{2,1,0:T(8,128)(2,1)}, bf16[4,1024,256]{2,1,0:T(8,128)(2,1)}, u32[]{:S(2)}, u32[]{:S(2)}) %collective-permute-start.6) | collective-permute-done | bytes 2097184 | tf_op jit(solution)/shard_map/ppermute | solution.py:899
  234.4 17.1 %shard_map.264 = f32[512,512]{1,0:T(8,128)S(1)} custom-call(bf16[512,2048]{1,0:T(8,128)(2,1)S(1)} %pad_maximum_fusion.3.x_ref), custom_call_target="tpu_custom_call" | custom-call | flops 18253611008 | tf_op jit(solution)/shard_map/pallas_call | solution.py:570
  261.7 62.1 %shard_map.265.hidden_ref = bf16[2048,2048]{1,0:T(8,128)(2,1)} custom-call(bf16[512,512]{1,0:T(8,128)(2,1)} %multiply_convert_fusion.1.x_ref), custom_call_target="tpu_custom_call" | custom-call | flops 64424509440 | tf_op jit(solution)/shard_map/pallas_call | solution.py:381
  323.8 25.9 %shard_map.266 = (bf16[2048,256]{1,0:T(8,128)(2,1)}, bf16[2048,256]{1,0:T(8,128)(2,1)}, bf16[2048,256]{1,0:T(8,128)(2,1)}, f32[2048,1]{1,0:T(8,128)}, bf16[2,3,1024,256]{3,2,1,0:T(8,128)(2,1)}) custom-call(s32[2]{0:T(128)} %pad_add_fusion.at_ref, bf16[2048,2048]{1,0:T(8,128)(2,1)} %shard_map.265.hidden_ref, ...), custom_call_target="tpu_custom_call" | custom-call | flops 28991029248 | tf_op jit(solution)/shard_map/pallas_call | solution.py:222
  354.2 35.4 %collective-permute-done.8 = bf16[3,1024,256]{2,1,0:T(8,128)(2,1)} collective-permute-done((bf16[3,1024,256]{2,1,0:T(8,128)(2,1)}, bf16[3,1024,256]{2,1,0:T(8,128)(2,1)}, u32[]{:S(2)}, u32[]{:S(2)}) %collective-permute-start.8) | collective-permute-done | bytes 1572896 | tf_op jit(solution)/shard_map/ppermute | solution.py:908
  392.7 25.9 %shard_map.267 = (bf16[2048,256]{1,0:T(8,128)(2,1)}, bf16[2048,256]{1,0:T(8,128)(2,1)}, bf16[2048,256]{1,0:T(8,128)(2,1)}, f32[2048,1]{1,0:T(8,128)}, bf16[2,3,1024,256]{3,2,1,0:T(8,128)(2,1)}) custom-call(s32[2]{0:T(128)} %get-tuple-element.259.at_ref, bf16[2048,2048]{1,0:T(8,128)(2,1)} %shard_map.265.hidden_ref, ...), custom_call_target="tpu_custom_call" | custom-call | flops 28991029248 | tf_op jit(solution)/shard_map/pallas_call | solution.py:222
  423.0 34.6 %collective-permute-done.9 = bf16[3,1024,256]{2,1,0:T(8,128)(2,1)} collective-permute-done((bf16[3,1024,256]{2,1,0:T(8,128)(2,1)}, bf16[3,1024,256]{2,1,0:T(8,128)(2,1)}, u32[]{:S(2)}, u32[]{:S(2)}) %collective-permute-start.9) | collective-permute-done | bytes 1572896 | tf_op jit(solution)/shard_map/ppermute | solution.py:908
  460.5 25.9 %shard_map.269 = (bf16[2048,256]{1,0:T(8,128)(2,1)}, bf16[2048,256]{1,0:T(8,128)(2,1)}, bf16[2048,256]{1,0:T(8,128)(2,1)}, f32[2048,1]{1,0:T(8,128)}, bf16[2,3,1024,256]{3,2,1,0:T(8,128)(2,1)}) custom-call(s32[2]{0:T(128)} %pad_add_fusion.3.at_ref, bf16[2048,2048]{1,0:T(8,128)(2,1)} %shard_map.265.hidden_ref, ...), custom_call_target="tpu_custom_call" | custom-call | flops 28991029248 | tf_op jit(solution)/shard_map/pallas_call | solution.py:222
  489.2 34.0 %collective-permute-done.12 = bf16[3,1024,256]{2,1,0:T(8,128)(2,1)S(1)} collective-permute-done((bf16[3,1024,256]{2,1,0:T(8,128)(2,1)S(1)}, bf16[3,1024,256]{2,1,0:T(8,128)(2,1)S(1)}, u32[]{:S(2)}, u32[]{:S(2)}) %collective-permute-start.12) | collective-permute-done | bytes 1572896 | tf_op jit(solution)/shard_map/ppermute | solution.py:908
  526.6 26.2 %shard_map.268 = (bf16[2048,256]{1,0:T(8,128)(2,1)}, bf16[2048,256]{1,0:T(8,128)(2,1)}, bf16[2048,256]{1,0:T(8,128)(2,1)}, f32[2048,1]{1,0:T(8,128)}, bf16[2,3,1024,256]{3,2,1,0:T(8,128)(2,1)}) custom-call(s32[2]{0:T(128)} %get-tuple-element.260.at_ref, bf16[2048,2048]{1,0:T(8,128)(2,1)} %shard_map.265.hidden_ref, ...), custom_call_target="tpu_custom_call" | custom-call | flops 28991029248 | tf_op jit(solution)/shard_map/pallas_call | solution.py:222
  555.1 96.9 %shard_map.270 = (f32[512,512]{1,0:T(8,128)}, f32[4,4,512]{2,1,0:T(4,128)}) custom-call(bf16[2048,256]{1,0:T(8,128)(2,1)} %get-tuple-element.84.refs_0_, bf16[2048,256]{1,0:T(8,128)(2,1)} %get-tuple-element.85.refs_1_, bf16[2048,256]{1,0:T(8,128)(2,1)} %get-tuple-element.86.refs_2_, bf16[2048,256]{1,0:T(8,128)(2,1)} %get-tuple-element.87.refs_3_, ...), custom_call_target="tpu_custom_call" | custom-call | flops 69793218560 | tf_op jit(solution)/shard_map/pallas_call | solution.py:839
  665.1 18.8 %shard_map.271 = bf16[512,2048]{1,0:T(8,128)(2,1)} custom-call(bf16[512,512]{1,0:T(8,128)(2,1)} %get-tuple-element.183.x_ref), custom_call_target="tpu_custom_call" | custom-call | flops 26843545600 | tf_op jit(solution)/shard_map/pallas_call | solution.py:420
  688.5 16.1 %all-to-all-start.2 = ((bf16[4,1,1,512,128]{4,3,2,1,0:T(8,128)(2,1)}), bf16[4,1,1,512,128]{4,3,2,1,0:T(8,128)(2,1)S(1)}, u32[]{:S(2)}, u32[]{:S(2)}) async-start(bf16[4,1,1,512,128]{4,3,2,1,0:T(8,128)(2,1)} %bitcast.42), calls=%async_computation.2 | async-start | bytes 1048576 | tf_op jit(solution)/shard_map/all_to_all | solution.py:143
  708.8 22.2 %all-to-all-done.2 = bf16[4,1,1,512,128]{4,3,2,1,0:T(8,128)(2,1)S(1)} async-done(((bf16[4,1,1,512,128]{4,3,2,1,0:T(8,128)(2,1)}), bf16[4,1,1,512,128]{4,3,2,1,0:T(8,128)(2,1)S(1)}, u32[]{:S(2)}, u32[]{:S(2)}) %all-to-all-start.2) | async-done | bytes 524320 | tf_op jit(solution)/shard_map/all_to_all | solution.py:143
  733.3 9.5 shard_map.272
  775.9 50.5 %all-to-all-done.3 = bf16[4,3,1,512,128]{3,4,2,1,0:T(8,128)(2,1)} async-done(((bf16[4,3,1,512,128]{3,4,2,1,0:T(8,128)(2,1)}), bf16[4,3,1,512,128]{3,4,2,1,0:T(8,128)(2,1)}, u32[]{:S(2)}, u32[]{:S(2)}) %all-to-all-start.3) | async-done | bytes 1572896 | tf_op jit(solution)/shard_map/all_to_all | solution.py:152
  850.3 17.2 %shard_map.273 = f32[512,512]{1,0:T(8,128)S(1)} custom-call(bf16[512,2048]{1,0:T(8,128)(2,1)S(1)} %pad_maximum_fusion.4.x_ref), custom_call_target="tpu_custom_call" | custom-call | flops 18253611008 | tf_op jit(solution)/shard_map/pallas_call | solution.py:570
  895.0 34.0 %shard_map.274 = f32[512,2048]{1,0:T(8,128)} custom-call(f32[512,512]{1,0:T(8,128)} %multiply_subtract_fusion.x_ref), custom_call_target="tpu_custom_call" | custom-call | flops 26843545600 | tf_op jit(solution)/shard_map/pallas_call | solution.py:420
  939.3 39.3 %collective-permute-done.11 = bf16[4160,512]{1,0:T(8,128)(2,1)} collective-permute-done((bf16[4160,512]{1,0:T(8,128)(2,1)}, bf16[4160,512]{1,0:T(8,128)(2,1)}, u32[]{:S(2)}, u32[]{:S(2)}) %collective-permute-start.11) | collective-permute-done | bytes 4259872 | tf_op jit(solution)/shard_map/ppermute | solution.py:908
  984.3 90.7 %shard_map.275 = f32[512,512]{1,0:T(8,128)} custom-call(bf16[2048,256]{1,0:T(8,128)(2,1)} %get-tuple-element.106.refs_0_, bf16[2048,256]{1,0:T(8,128)(2,1)} %get-tuple-element.107.refs_1_, bf16[2048,256]{1,0:T(8,128)(2,1)} %get-tuple-element.108.refs_2_, bf16[2048,256]{1,0:T(8,128)(2,1)} %get-tuple-element.109.refs_3_, bf16[16,256,1024]{2,1,0:T(8,128)(2,1)} %refs_4_.9, ...), custom_call_target="tpu_custom_call" | custom-call | flops 69793218560 | tf_op jit(solution)/shard_map/pallas_call | solution.py:839
  1096.8 34.0 %shard_map.276 = f32[512,2048]{1,0:T(8,128)} custom-call(f32[512,512]{1,0:T(8,128)} %add.233.x_ref), custom_call_target="tpu_custom_call" | custom-call | flops 26843545600 | tf_op jit(solution)/shard_map/pallas_call | solution.py:420
  1140.5 7.8 pad_maximum_fusion.1
  1152.2 11.7 bitcast_convert_fusion.2
  1163.9 11.4 bitcast_convert_fusion.1
  1175.3 11.8 bitcast_convert_fusion
  1187.0 46.3 %all-gather.18.cloned.1.call-done = bf16[4160,512]{1,0:T(8,128)(2,1)} async-done(((bf16[1040,512]{1,0:T(8,128)(2,1)}), bf16[4160,512]{1,0:T(8,128)(2,1)}) %all-gather.18.cloned.1.call-update) | async-done | bytes 4259856 | tf_op jit(solution)/shard_map/all_gather | solution.py:1102
  (402 shorter events, 310.1 us)
Async XLA Ops:
  7.2 111.9 %all-gather.14.cloned.1.call-start = ((), (), s32[]{:S(2)}) async-start(), calls=%async_computation.5 | async-start | bytes 3276800 | tf_op jit(solution)/shard_map/all_gather | solution.py:950
  10.9 192.8 %copy-start.63 = (bf16[20,1024]{1,0:T(8,128)(2,1)}, bf16[20,1024]{1,0:T(8,128)(2,1)S(1)}, u32[]{:S(2)}) copy-start(bf16[20,1024]{1,0:T(8,128)(2,1)S(1)} %concatenate.92) | copy-start | bytes 122884
  10.9 19.6 %collective-permute-start = (bf16[20,1024]{1,0:T(8,128)(2,1)S(1)}, bf16[20,1024]{1,0:T(8,128)(2,1)S(1)}, u32[]{:S(2)}, u32[]{:S(2)}) collective-permute-start(bf16[20,1024]{1,0:T(8,128)(2,1)S(1)} %concatenate.92), channel_id=1, source_target_pairs={{16,0},{0,16},{17,1},{1,17},{18,2},{2,18},{19,3},{3,19},{20,4},{4,... | collective-permute-start | bytes 122888 | tf_op jit(solution)/shard_map/ppermute | solution.py:899
  13.9 26.4 %collective-permute-start.3 = (bf16[1024,512]{1,0:T(8,128)(2,1)}, bf16[1024,512]{1,0:T(8,128)(2,1)}, u32[]{:S(2)}, u32[]{:S(2)}) collective-permute-start(bf16[1024,512]{1,0:T(8,128)(2,1)} %param.29), channel_id=1, source_target_pairs={{16,0},{0,16},{17,1},{1,17},{18,2},{2,18},{19,3},{3,19},{20,4},{4,... | collective-permute-start | bytes 3145736 | tf_op jit(solution)/shard_map/ppermute | solution.py:899
  14.0 48.7 %collective-permute-start.1 = (bf16[1024,512]{1,0:T(8,128)(2,1)}, bf16[1024,512]{1,0:T(8,128)(2,1)S(1)}, u32[]{:S(2)}, u32[]{:S(2)}) collective-permute-start(bf16[1024,512]{1,0:T(8,128)(2,1)} %param.27), channel_id=1, source_target_pairs={{16,0},{0,16},{17,1},{1,17},{18,2},{2,18},{19,3},{3,19},{20,4},{4,... | collective-permute-start | bytes 3145736 | tf_op jit(solution)/shard_map/ppermute | solution.py:899
  15.9 67.8 %collective-permute-start.2 = (bf16[1024,512]{1,0:T(8,128)(2,1)}, bf16[1024,512]{1,0:T(8,128)(2,1)}, u32[]{:S(2)}, u32[]{:S(2)}) collective-permute-start(bf16[1024,512]{1,0:T(8,128)(2,1)} %param.28), channel_id=1, source_target_pairs={{16,0},{0,16},{17,1},{1,17},{18,2},{2,18},{19,3},{3,19},{20,4},{4,... | collective-permute-start | bytes 3145736 | tf_op jit(solution)/shard_map/ppermute | solution.py:899
  30.5 173.1 %copy-start.69 = (bf16[20,1024]{1,0:T(8,128)(2,1)}, bf16[20,1024]{1,0:T(8,128)(2,1)S(1)}, u32[]{:S(2)}) copy-start(bf16[20,1024]{1,0:T(8,128)(2,1)S(1)} %collective-permute-done) | copy-start | bytes 122884
  37.3 62.0 %copy-start.83 = (f32[512]{0:T(512)}, f32[512]{0:T(512)S(1)}, u32[]{:S(2)}) copy-start(f32[512]{0:T(512)S(1)} %fusion.57) | copy-start | bytes 6148
  109.7 41.9 %all-to-all-start = ((bf16[4,3,1,512,128]{4,3,2,1,0:T(8,128)(2,1)}), bf16[4,3,1,512,128]{4,3,2,1,0:T(8,128)(2,1)S(1)}, u32[]{:S(2)}, u32[]{:S(2)}) async-start(bf16[4,3,1,512,128]{4,3,2,1,0:T(8,128)(2,1)} %maximum_bitcast_fusion), calls=%async_computation | async-start | bytes 3145728 | tf_op jit(solution)/shard_map/all_to_all | solution.py:143
  114.6 209.2 %all-gather.16.cloned.1.call-start = ((), (), s32[]{:S(2)}) async-start(), calls=%async_computation.6 | async-start | bytes 10485760 | tf_op jit(solution)/shard_map/all_gather | solution.py:952
  118.1 71.3 %collective-permute-start.5 = (bf16[4,1024,256]{2,1,0:T(8,128)(2,1)}, bf16[4,1024,256]{2,1,0:T(8,128)(2,1)}, u32[]{:S(2)}, u32[]{:S(2)}) collective-permute-start(bf16[4,1024,256]{2,1,0:T(8,128)(2,1)} %constant_dynamic-slice_fusion.5), channel_id=1, source_target_pairs={{16,0},{0,16},{17,1},{1,17},{18,2},{2,18},{19,3},{3,19},{20,4},{4,... | collective-permute-start | bytes 6291464 | tf_op jit(solution)/shard_map/ppermute | solution.py:899
  123.3 66.1 %collective-permute-start.4 = (bf16[512,1024]{1,0:T(8,128)(2,1)S(1)}, bf16[512,1024]{1,0:T(8,128)(2,1)}, u32[]{:S(2)}, u32[]{:S(2)}) collective-permute-start(bf16[512,1024]{1,0:T(8,128)(2,1)S(1)} %copy-done.89), channel_id=1, source_target_pairs={{16,0},{0,16},{17,1},{1,17},{18,2},{2,18},{19,3},{3,19},{20,4},{4,... | collective-permute-start | bytes 3145736 | tf_op jit(solution)/shard_map/ppermute | solution.py:899
  127.5 106.9 %collective-permute-start.6 = (bf16[4,1024,256]{2,1,0:T(8,128)(2,1)}, bf16[4,1024,256]{2,1,0:T(8,128)(2,1)}, u32[]{:S(2)}, u32[]{:S(2)}) collective-permute-start(bf16[4,1024,256]{2,1,0:T(8,128)(2,1)} %constant_dynamic-slice_fusion.4), channel_id=1, source_target_pairs={{16,0},{0,16},{17,1},{1,17},{18,2},{2,18},{19,3},{3,19},{20,4},{4,... | collective-permute-start | bytes 6291464 | tf_op jit(solution)/shard_map/ppermute | solution.py:899
  131.8 192.0 %collective-permute-start.7 = (bf16[4,256,1024]{2,1,0:T(8,128)(2,1)}, bf16[4,256,1024]{2,1,0:T(8,128)(2,1)}, u32[]{:S(2)}, u32[]{:S(2)}) collective-permute-start(bf16[4,256,1024]{2,1,0:T(8,128)(2,1)} %constant_dynamic-slice_fusion.2), channel_id=1, source_target_pairs={{16,0},{0,16},{17,1},{1,17},{18,2},{2,18},{19,3},{3,19},{20,4},{4,... | collective-permute-start | bytes 6291464 | tf_op jit(solution)/shard_map/ppermute | solution.py:899
  198.5 16.4 %all-to-all-start.1 = ((bf16[4,1,1,512,128]{3,4,2,1,0:T(8,128)(2,1)}), bf16[4,1,1,512,128]{3,4,2,1,0:T(8,128)(2,1)S(1)}, u32[]{:S(2)}, u32[]{:S(2)}) async-start(bf16[4,1,1,512,128]{3,4,2,1,0:T(8,128)(2,1)} %copy.112), calls=%async_computation.1 | async-start | bytes 1048576 | tf_op jit(solution)/shard_map/all_to_all | solution.py:152
  203.7 527.4 %all-gather.20.cloned.1.call-start = ((), (), s32[]{:S(2)}) async-start(), calls=%async_computation.9 | async-start | bytes 7864320 | tf_op jit(solution)/shard_map/all_gather | solution.py:1010
  203.7 56.4 %copy-start.81 = (f32[1,512]{1,0:T(1,128)}, f32[1,512]{1,0:T(1,128)S(1)}, u32[]{:S(2)}) copy-start(f32[1,512]{1,0:T(1,128)S(1)} %constant_dynamic-slice_fusion.3) | copy-start | bytes 6148
  252.9 70.8 %copy-start.10 = (f32[512,512]{1,0:T(8,128)}, f32[512,512]{1,0:T(8,128)S(1)}, u32[]{:S(2)}) copy-start(f32[512,512]{1,0:T(8,128)S(1)} %get-tuple-element.186) | copy-start | bytes 3145732
  352.5 37.0 %collective-permute-start.8 = (bf16[3,1024,256]{2,1,0:T(8,128)(2,1)}, bf16[3,1024,256]{2,1,0:T(8,128)(2,1)}, u32[]{:S(2)}, u32[]{:S(2)}) collective-permute-start(bf16[3,1024,256]{2,1,0:T(8,128)(2,1)} %slice_bitcast_fusion.4), channel_id=1, source_target_pairs={{0,16},{16,0},{1,17},{17,1},{2,18},{18,2},{3,19},{19,3},{4,20},{20... | collective-permute-start | bytes 4718600 | tf_op jit(solution)/shard_map/ppermute | solution.py:908
  392.5 373.7 %all-gather.26.cloned.1.call-start = ((), (), s32[]{:S(2)}) async-start(), calls=%async_computation.12 | async-start | bytes 7864320 | tf_op jit(solution)/shard_map/all_gather | solution.py:1010
  421.4 36.2 %collective-permute-start.9 = (bf16[3,1024,256]{2,1,0:T(8,128)(2,1)}, bf16[3,1024,256]{2,1,0:T(8,128)(2,1)}, u32[]{:S(2)}, u32[]{:S(2)}) collective-permute-start(bf16[3,1024,256]{2,1,0:T(8,128)(2,1)} %slice_bitcast_fusion.3), channel_id=1, source_target_pairs={{0,16},{16,0},{1,17},{17,1},{2,18},{18,2},{3,19},{19,3},{4,20},{20... | collective-permute-start | bytes 4718600 | tf_op jit(solution)/shard_map/ppermute | solution.py:908
  488.2 35.0 %collective-permute-start.12 = (bf16[3,1024,256]{2,1,0:T(8,128)(2,1)S(1)}, bf16[3,1024,256]{2,1,0:T(8,128)(2,1)S(1)}, u32[]{:S(2)}, u32[]{:S(2)}) collective-permute-start(bf16[3,1024,256]{2,1,0:T(8,128)(2,1)S(1)} %slice_bitcast_fusion.1), channel_id=1, source_target_pairs={{0,16},{16,0},{1,17},{17,1},{2,18},{18,2},{3,19},{19,3},{4,20},{20... | collective-permute-start | bytes 4718600 | tf_op jit(solution)/shard_map/ppermute | solution.py:908
  524.8 325.5 %all-gather.22.cloned.1.call-start = ((), (), s32[]{:S(2)}) async-start(), calls=%async_computation.10 | async-start | bytes 7864320 | tf_op jit(solution)/shard_map/all_gather | solution.py:1010
  555.1 97.9 %copy-start.71 = (bf16[16,2048]{1,0:T(8,128)(2,1)S(1)}, bf16[16,2048]{1,0:T(8,128)(2,1)}, u32[]{:S(2)}) copy-start(bf16[16,2048]{1,0:T(8,128)(2,1)} %pad_maximum_fusion.9.router_ref) | copy-start | bytes 196612
  688.5 42.5 %all-to-all-start.2 = ((bf16[4,1,1,512,128]{4,3,2,1,0:T(8,128)(2,1)}), bf16[4,1,1,512,128]{4,3,2,1,0:T(8,128)(2,1)S(1)}, u32[]{:S(2)}, u32[]{:S(2)}) async-start(bf16[4,1,1,512,128]{4,3,2,1,0:T(8,128)(2,1)} %bitcast.42), calls=%async_computation.2 | async-start | bytes 1048576 | tf_op jit(solution)/shard_map/all_to_all | solution.py:143
  707.2 45.9 %collective-permute-start.10 = (bf16[3,1024,256]{2,1,0:T(8,128)(2,1)}, bf16[3,1024,256]{2,1,0:T(8,128)(2,1)}, u32[]{:S(2)}, u32[]{:S(2)}) collective-permute-start(bf16[3,1024,256]{2,1,0:T(8,128)(2,1)} %slice_bitcast_fusion.2), channel_id=1, source_target_pairs={{0,16},{16,0},{1,17},{17,1},{2,18},{18,2},{3,19},{19,3},{4,20},{20... | collective-permute-start | bytes 4718600 | tf_op jit(solution)/shard_map/ppermute | solution.py:908
  744.9 81.5 %all-to-all-start.3 = ((bf16[4,3,1,512,128]{3,4,2,1,0:T(8,128)(2,1)}), bf16[4,3,1,512,128]{3,4,2,1,0:T(8,128)(2,1)}, u32[]{:S(2)}, u32[]{:S(2)}) async-start(bf16[4,3,1,512,128]{3,4,2,1,0:T(8,128)(2,1)} %maximum_bitcast_fusion.1), calls=%async_computation.3 | async-start | bytes 3145728 | tf_op jit(solution)/shard_map/all_to_all | solution.py:152
  751.3 323.8 %all-gather.24.cloned.1.call-start = ((), (), s32[]{:S(2)}) async-start(), calls=%async_computation.11 | async-start | bytes 7864320 | tf_op jit(solution)/shard_map/all_gather | solution.py:1010
  756.1 384.3 %reduce-scatter.2.cloned.1.call-start = ((), (), s32[]{:S(2)}) async-start(), calls=%async_computation.7 | async-start | bytes 5324800 | tf_op jit(solution)/shard_map/reduce_scatter | solution.py:1101
  884.0 94.5 %collective-permute-start.11 = (bf16[4160,512]{1,0:T(8,128)(2,1)}, bf16[4160,512]{1,0:T(8,128)(2,1)}, u32[]{:S(2)}, u32[]{:S(2)}) collective-permute-start(bf16[4160,512]{1,0:T(8,128)(2,1)} %pad_dynamic-update-slice_fusion.1), channel_id=1, source_target_pairs={{0,16},{16,0},{1,17},{17,1},{2,18},{18,2},{3,19},{19,3},{4,20},{20... | collective-permute-start | bytes 12779528 | tf_op jit(solution)/shard_map/ppermute | solution.py:908
  984.3 90.8 %copy-start.12 = (f32[512,512]{1,0:T(8,128)S(1)}, f32[512,512]{1,0:T(8,128)}, u32[]{:S(2)}) copy-start(f32[512,512]{1,0:T(8,128)} %copy-done.10) | copy-start | bytes 3145732
  984.3 249.0 %all-gather.18.cloned.1.call-start = ((), (), s32[]{:S(2)}) async-start(), calls=%async_computation.8 | async-start | bytes 5324800 | tf_op jit(solution)/shard_map/all_gather | solution.py:1102
  (85 other events, 867.3 us)
Sparse Core Ops, SparseCore 0:
  24.3 56.5 all-gather.13
  122.3 59.5 all-gather.15
  392.6 114.3 all-gather.19
  524.9 145.7 all-gather.25
  672.7 162.4 all-gather.21
  837.1 113.4 all-gather.23
  984.4 109.7 reduce-scatter.1
  1140.6 92.6 all-gather.17

commit v2 on v1

--- a/solution.py
+++ b/solution.py
@@ -14,7 +14,7 @@
 BF16 = jnp.bfloat16
 F32 = jnp.float32
 MESH = pl.DeviceIdType.MESH
-MICRO = 1 << 30
+MICRO = 1 << 26
 
 
 def dot(a, b):
@@ -127,7 +127,8 @@
         attend_back_kernel,
         cost_estimate=pl.CostEstimate(flops=10 * MICRO, bytes_accessed=0, transcendentals=0),
         grid=(heads,),
-        out_shape=(jax.ShapeDtypeStruct((heads, rows, HEAD), BF16),) * 3,
+        out_shape=(jax.ShapeDtypeStruct((heads, rows, HEAD), F32),) * 2
+        + (jax.ShapeDtypeStruct((heads, rows, HEAD), BF16),),
         in_specs=[pl.BlockSpec(memory_space=pltpu.SMEM), spec, spec, spec, spec, column],
         out_specs=(spec,) * 3,
         scratch_shapes=[pltpu.VMEM((rows, HEAD), F32)] * 2,
@@ -154,12 +155,62 @@
     return turned.reshape(len(parts), pack // count, count * mine, HEAD)
 
 
-def expert_kernel(blocks, at_ref, hidden_ref, up_ref, chosen_ref, router_ref, *refs):
-    gate_w, up_w, down_w = (refs[i * blocks : (i + 1) * blocks] for i in range(3))
-    inner_ref, dgate_ref, dup_ref, dots_ref, grads_ref = refs[3 * blocks : 3 * blocks + 5]
-    gate_sum, up_sum, down_sum = refs[3 * blocks + 5 :]
+def carried(pairs, sems):
+    d, count = lax.axis_index("dp"), lax.axis_size("dp")
+    copies, partners = [], []
+    for axis, source, target in pairs:
+        send, recv = sems[axis]
+        if axis == "z":
+            partner = {"ctx": jnp.bitwise_xor(lax.axis_index("ctx"), 1)}
+            copies.append(remote(source, target, (send, recv), 0, partner))
+            partners.append((partner, d >= 0))
+            continue
+        for s in range(1, count):
+            partner = {"dp": lax.rem(d + s, count)}
+            copies.append(remote(source.at[s - 1], target.at[s - 1], (send, recv), s - 1, partner))
+            partners.append((partner, d >= 0))
+    return copies, partners
+
+
+def carry_operands(carry):
+    dma = pltpu.SemaphoreType.DMA
+    shapes, sems = [], []
+    for axis, v in carry:
+        shapes.append(jax.ShapeDtypeStruct(v.shape, v.dtype))
+        sems += [dma((v.shape[0] if axis == "x" else 1,))] * 2
+    return [v for _, v in carry], shapes, sems
+
+
+def expert_kernel(blocks, number, far, mine, full, axes, *refs):
+    refs = list(refs)
+
+    def take(count):
+        return [refs.pop(0) for _ in range(count)]
+
+    hidden_ref, up_ref, chosen_ref, router_ref = take(4)
+    gate_w, up_w, down_w = take(blocks), take(blocks), take(blocks)
+    sources = take(len(axes))
+    if full:
+        inner_ref, dgate_ref, dup_ref, dots_ref = take(4)
+    near_ref, others_ref = take(2)
+    targets = take(len(axes))
+    gate_sum, up_sum, down_sum = take(3)
+    sems = {axis: take(2) for axis in axes}
     turn, last = pl.program_id(0), pl.num_programs(0) - 1
     wide = gate_w[0].shape[0]
+
+    def transfers():
+        return carried(list(zip(axes, sources, targets)), sems)
+
+    if axes:
+
+        @pl.when(turn == 0)
+        def _():
+            copies, partners = transfers()
+            signal_all(partners)
+            for copy in copies:
+                copy.start()
+
     hidden, upstream = hidden_ref[...], up_ref[...]
 
     def over(v, ws, f):
@@ -170,76 +221,97 @@
     logits = dot_t(hidden, router_ref[...])
     odds = jnp.exp(logits - jnp.max(logits, axis=1, keepdims=True))
     probs = odds / jnp.sum(odds, axis=1, keepdims=True) * chosen_ref[...]
-    named = lax.broadcasted_iota(jnp.int32, probs.shape, 1) == at_ref[0]
+    plane = lax.axis_index("ctx")
+    if far:
+        plane = jnp.bitwise_xor(plane, 2)
+    named = lax.broadcasted_iota(jnp.int32, probs.shape, 1) == plane * mine + number
     weight = jnp.sum(jnp.where(named, probs, 0.0), axis=1, keepdims=True)
     sigma = jax.nn.sigmoid(gate)
     active = gate * sigma
     inner = (active * up).astype(BF16).astype(F32)
-    dots = jnp.sum(inner * pulled, axis=1, keepdims=True)
-    dots_ref[...] = jnp.where(weight > 0.0, dots, 0.0)
+    if full:
+        dots = jnp.sum(inner * pulled, axis=1, keepdims=True)
+        dots_ref[...] = jnp.where(weight > 0.0, dots, 0.0)
     inner = (weight * inner).astype(BF16)
     pulled = weight * pulled
     d_gate = (pulled * up * sigma * (1.0 + gate * (1.0 - sigma))).astype(BF16)
     d_up = (pulled * active).astype(BF16)
-    inner_ref[...], dgate_ref[...], dup_ref[...] = inner, d_gate, d_up
+    if full:
+        inner_ref[...], dgate_ref[...], dup_ref[...] = inner, d_gate, d_up
 
     @pl.when(turn == 0)
     def _():
-        for total in (gate_sum, up_sum, down_sum):
-            total[...] = jnp.zeros_like(total)
-
-    gate_sum[...] += t_dot(d_gate, hidden)
-    up_sum[...] += t_dot(d_up, hidden)
-    down_sum[...] += t_dot(inner, upstream)
+        gate_sum[...] = t_dot(d_gate, hidden)
+        up_sum[...] = t_dot(d_up, hidden)
+        down_sum[...] = t_dot(inner, upstream)
+
+    @pl.when(turn > 0)
+    def _():
+        gate_sum[...] += t_dot(d_gate, hidden)
+        up_sum[...] += t_dot(d_up, hidden)
+        down_sum[...] += t_dot(inner, upstream)
 
     @pl.when(turn == last)
     def _():
         fine = down_sum.shape[0]
         for s in range(blocks):
+            target = near_ref if s == 0 else others_ref.at[s - 1]
             own = pl.ds(s * wide, wide)
-            grads_ref[s, 0] = gate_sum[:, own].T.astype(BF16)
-            grads_ref[s, 1] = up_sum[:, own].T.astype(BF16)
+            target[0] = gate_sum[:, own].T.astype(BF16)
+            target[1] = up_sum[:, own].T.astype(BF16)
             for j in range(wide // fine):
-                grads_ref[s, 2, pl.ds(j * fine, fine), :] = down_sum[
+                target[2, pl.ds(j * fine, fine), :] = down_sum[
                     :, pl.ds(s * wide + j * fine, fine)
                 ].astype(BF16)
-
-
-def expert(at, hidden, upstream, chosen, router, gate_w, up_w, down_w, tile=512):
-    blocks = len(gate_w)
+        if axes:
+            for copy in transfers()[0]:
+                copy.wait()
+
+
+def expert(e, hidden, upstream, chosen, router, weights, far, full, carry, ident, tile=512):
+    both_w, down_w = weights
+    blocks = len(both_w)
     pack, width = hidden.shape
-    _, wide, fine = gate_w[0].shape
-
-    def weight_spec(which, shape):
-        return pl.BlockSpec((None,) + shape, lambda i, at_ref: (at_ref[which], 0, 0))
-
-    ups = [weight_spec(0 if s == 0 else 1, (wide, fine)) for s in range(blocks)]
-    downs = [weight_spec(0 if s == 0 else 1, (fine, wide)) for s in range(blocks)]
+    mine, fine, wide = down_w[0].shape
+    operands, shapes, sems = carry_operands(carry)
+    hbm = pl.BlockSpec(memory_space=pl.ANY)
+
     def token(n):
-        return pl.BlockSpec((tile, n), lambda i, at_ref: (i, 0))
-
-    whole = pl.BlockSpec((blocks, 3, wide, fine), lambda i, at_ref: (0, 0, 0, 0))
+        return pl.BlockSpec((tile, n), lambda i: (i, 0))
+
+    def weight(first, *shape):
+        return pl.BlockSpec((None,) + shape, lambda i: (first + e, 0, 0))
+
+    near = pl.BlockSpec((3, wide, fine), lambda i: (0, 0, 0))
+    others = pl.BlockSpec((blocks - 1, 3, wide, fine), lambda i: (0, 0, 0, 0))
+    out_specs, out_shape = [near, others], [
+        jax.ShapeDtypeStruct((3, wide, fine), BF16),
+        jax.ShapeDtypeStruct((blocks - 1, 3, wide, fine), BF16),
+    ]
+    if full:
+        out_specs = [token(fine)] * 3 + [token(1)] + out_specs
+        out_shape = (
+            [jax.ShapeDtypeStruct((pack, fine), BF16)] * 3
+            + [jax.ShapeDtypeStruct((pack, 1), F32)]
+            + out_shape
+        )
+    remote_params = dict(collective_id=ident, has_side_effects=True) if carry else {}
     return pl.pallas_call(
-        functools.partial(expert_kernel, blocks),
+        functools.partial(expert_kernel, blocks, e, far, mine, full, [axis for axis, _ in carry]),
         cost_estimate=pl.CostEstimate(flops=27 * MICRO, bytes_accessed=0, transcendentals=0),
-        grid_spec=pltpu.PrefetchScalarGridSpec(
-            num_scalar_prefetch=1,
-            grid=(pack // tile,),
-            in_specs=[token(width), token(width), token(chosen.shape[1])]
-            + [pl.BlockSpec(router.shape, lambda i, at_ref: (0, 0))]
-            + ups
-            + ups
-            + downs,
-            out_specs=[token(fine)] * 3 + [token(1), whole],
-            scratch_shapes=[pltpu.VMEM((fine, width), F32)] * 3,
-        ),
-        out_shape=[jax.ShapeDtypeStruct((pack, fine), BF16)] * 3
-        + [
-            jax.ShapeDtypeStruct((pack, 1), F32),
-            jax.ShapeDtypeStruct((blocks, 3, wide, fine), BF16),
-        ],
-        compiler_params=pltpu.CompilerParams(vmem_limit_bytes=56 << 20),
-    )(at, hidden, upstream, chosen, router, *gate_w, *up_w, *down_w)
+        grid=(pack // tile,),
+        in_specs=[token(width), token(width), token(chosen.shape[1])]
+        + [pl.BlockSpec(router.shape, lambda i: (0, 0))]
+        + [weight(0, wide, fine)] * blocks
+        + [weight(mine, wide, fine)] * blocks
+        + [weight(0, fine, wide)] * blocks
+        + [hbm] * len(operands),
+        out_specs=out_specs + [hbm] * len(shapes),
+        out_shape=out_shape + shapes,
+        scratch_shapes=[pltpu.VMEM((fine, width), F32)] * 3 + sems,
+        compiler_params=pltpu.CompilerParams(vmem_limit_bytes=56 << 20, **remote_params),
+    )(hidden, upstream, chosen, router, *both_w, *both_w, *down_w, *operands)
+
 
 def signal_all(partners):
     barrier = pltpu.get_barrier_semaphore()
@@ -588,16 +660,24 @@
     )(v)
 
 
-def returns_kernel(kinds, mine, blocks, flipped, with_dots, *refs):
+def returns_kernel(kinds, mine, blocks, flipped, with_dots, axes, *refs):
     refs = list(refs)
-    take = lambda count: [refs.pop(0) for _ in range(count)]
-    lhs_refs, own_refs, other_refs = take(kinds * mine), take(kinds), take(kinds * (blocks - 1))
+
+    def take(count):
+        return [refs.pop(0) for _ in range(count)]
+
+    lhs_refs, own_refs, other_refs = take(kinds * mine), take(1), take(blocks - 1)
     dots_ref = take(1)[0] if with_dots else None
+    sources = take(len(axes))
     out_ref = take(1)[0]
     dots_out = take(1)[0] if with_dots else None
+    targets = take(len(axes))
     lhs, weights, core_out, core_in, keep, near, side_out, side_in, z_out, z_in = take(10)
     ls, ws, cs, cr, ys, yr, zs, zr = take(8)
     dots_in, ds, dr = take(3) if with_dots else (None, None, None)
+    moving, more = carried(
+        list(zip(axes, sources, targets)), {axis: take(2) for axis in axes}
+    )
     c, n, core, side, over_core, over_side = place()
     t, tp = lax.axis_index("tp"), lax.axis_size("tp")
     rows, part = out_ref.shape
@@ -613,7 +693,8 @@
             columns = pl.ds(at * fine, fine)
             loads.append(pltpu.make_async_copy(lhs_refs[at], lhs.at[:, columns], ls.at[at]))
             for s in range(blocks):
-                source = own_refs[k].at[c * mine + e] if s == 0 else other_refs[k * (blocks - 1) + s - 1].at[e]
+                source = own_refs[0] if s == 0 else other_refs[s - 1]
+                source = source.at[at]
                 target = weights.at[s, columns, :] if flipped else weights.at[s, :, columns]
                 loads.append(pltpu.make_async_copy(source, target, ws.at[at * blocks + s]))
     for load in loads:
@@ -623,11 +704,16 @@
         for far_c in range(n):
             for far_t in range(tp):
                 others.append(({"ctx": far_c, "tp": far_t}, (c != far_c) | (t != far_t)))
-        signal_all(others)
     else:
-        signal_all(
-            [(over_core, c >= 0), (over_side, c >= 0), (left, c > 0), (right, c < n - 1)]
-        )
+        others = [(over_core, c >= 0), (over_side, c >= 0), (left, c > 0), (right, c < n - 1)]
+    at = 0
+    for axis in axes:
+        count = 1 if axis == "z" else blocks - 1
+        others += [] if axis == "z" else more[at : at + count]
+        at += count
+    signal_all(others)
+    for copy in moving:
+        copy.start()
 
     def own_rows(owner):
         return pl.ds(pl.multiple_of(owner * rows, rows), rows)
@@ -814,20 +900,22 @@
         return carry
 
     lax.fori_loop(0, n, close, 0)
-
-
-def returns(lhs, own, others, dots, flipped, ident):
+    for copy in moving:
+        copy.wait()
+
+
+def returns(lhs, own, others, dots, flipped, ident, carry=()):
     n, tp = lax.axis_size("ctx"), lax.axis_size("tp")
     kinds, mine = len(lhs), len(lhs[0])
-    blocks = len(others[0]) + 1
+    blocks = len(others) + 1
     pack, fine = lhs[0][0].shape
-    wide = own[0].shape[2 if flipped else 1]
+    wide = own.shape[2 if flipped else 1]
     rows, part = pack // n, wide * blocks // tp
     deep = kinds * mine * fine
     dma, vmem = pltpu.SemaphoreType.DMA, pltpu.VMEM
     hbm = pl.BlockSpec(memory_space=pl.ANY)
     near = pl.BlockSpec(memory_space=pltpu.VMEM)
-    operands = [v for kind in lhs for v in kind] + list(own) + [v for kind in others for v in kind]
+    operands = [v for kind in lhs for v in kind] + [own] + list(others)
     in_specs = [hbm] * len(operands)
     out_shape = [jax.ShapeDtypeStruct((rows, part), F32)]
     extra = []
@@ -836,12 +924,16 @@
         in_specs.append(near)
         out_shape.append(jax.ShapeDtypeStruct((n, mine, rows), F32))
         extra = [vmem((n * tp, mine, rows), F32), dma((n * tp,)), dma((n * tp,))]
+    carried_in, shapes, sems = carry_operands(carry)
+    axes = [axis for axis, _ in carry]
     return pl.pallas_call(
-        functools.partial(returns_kernel, kinds, mine, blocks, flipped, dots is not None),
+        functools.partial(
+            returns_kernel, kinds, mine, blocks, flipped, dots is not None, axes
+        ),
         cost_estimate=pl.CostEstimate(flops=65 * MICRO, bytes_accessed=0, transcendentals=0),
-        out_shape=out_shape,
-        in_specs=in_specs,
-        out_specs=[near] * len(out_shape),
+        out_shape=out_shape + shapes,
+        in_specs=in_specs + [hbm] * len(shapes),
+        out_specs=[near] * len(out_shape) + [hbm] * len(shapes),
         scratch_shapes=[
             vmem((pack, deep), BF16),
             vmem((blocks, deep, wide) if flipped else (blocks, wide, deep), BF16),
@@ -858,11 +950,146 @@
         ]
         + [dma((n,))] * 4
         + [dma((2 * n,))] * 2
-        + extra,
+        + extra
+        + sems,
         compiler_params=pltpu.CompilerParams(
             collective_id=ident, has_side_effects=True, vmem_limit_bytes=56 << 20
         ),
-    )(*operands)
+    )(*operands, *carried_in)
+
+
+def mixture_kernel(blocks, tp, *refs):
+    inner_refs, out_ref = refs[: -1 - blocks], refs[-1]
+    weights = refs[-1 - blocks : -1]
+    wide, part = weights[0].shape[2], out_ref.shape[2]
+    step = min(wide, part)
+    inners = [r[...] for r in inner_refs]
+    for start in range(0, wide * blocks, step):
+        s, here = start // wide, pl.ds(start % wide, step)
+        total = sum(dot(v, weights[s][e, :, here]) for e, v in enumerate(inners))
+        column = start // part
+        out_ref[(column % 2) * 2 + column // 2, :, pl.ds(start % part, step)] = total.astype(BF16)
+
+
+def mixture_parts(inners, weights, tp, tile=512):
+    pack, fine = inners[0].shape
+    mine, blocks = len(inners), len(weights)
+    wide = weights[0].shape[2]
+    part = wide * blocks // tp
+    return pl.pallas_call(
+        functools.partial(mixture_kernel, blocks, tp),
+        cost_estimate=pl.CostEstimate(flops=15 * MICRO, bytes_accessed=0, transcendentals=0),
+        grid=(pack // tile,),
+        in_specs=[pl.BlockSpec((tile, fine), lambda i: (i, 0))] * mine
+        + [pl.BlockSpec((mine, fine, wide), lambda i: (0, 0, 0))] * blocks,
+        out_specs=pl.BlockSpec((tp, tile, part), lambda i: (0, i, 0)),
+        out_shape=jax.ShapeDtypeStruct((tp, pack, part), BF16),
+        compiler_params=pltpu.CompilerParams(vmem_limit_bytes=48 << 20),
+    )(*inners, *weights)
+
+
+def place_kernel(at_ref, near_ref, far_ref, *refs):
+    gate_ref, up_ref, down_ref = refs[-3:]
+    fine, wide = down_ref.shape
+
+    def write(source):
+        gate_ref[...] = source[0].astype(F32)
+        up_ref[...] = source[1].astype(F32)
+        for j in range(wide // fine):
+            down_ref[:, pl.ds(j * fine, fine)] = source[2, pl.ds(j * fine, fine), :].astype(F32)
+
+    pl.when(pl.program_id(0) == 0)(lambda: write(near_ref))
+    pl.when(pl.program_id(0) == 1)(lambda: write(far_ref))
+
+
+def place_grads(at, near, far, experts, held):
+    _, wide, fine = near.shape
+    source = pl.BlockSpec(near.shape, lambda i, at_ref: (0, 0, 0))
+    gate = pl.BlockSpec((None, wide, fine), lambda i, at_ref: (at_ref[i], 0, 0))
+    down = pl.BlockSpec((None, fine, wide), lambda i, at_ref: (at_ref[i], 0, 0))
+    return pl.pallas_call(
+        place_kernel,
+        cost_estimate=pl.CostEstimate(flops=4 * MICRO, bytes_accessed=0, transcendentals=0),
+        grid_spec=pltpu.PrefetchScalarGridSpec(
+            num_scalar_prefetch=1,
+            grid=(2,),
+            in_specs=[source, source] + [pl.BlockSpec(memory_space=pl.ANY)] * len(held),
+            out_specs=[gate, gate, down],
+        ),
+        out_shape=[jax.ShapeDtypeStruct((experts, wide, fine), F32)] * 2
+        + [jax.ShapeDtypeStruct((experts, fine, wide), F32)],
+        input_output_aliases={3 + i: i for i in range(len(held))},
+        compiler_params=pltpu.CompilerParams(vmem_limit_bytes=32 << 20),
+    )(at, near, far, *held)
+
+
+def share_kernel(over_tp, x_ref, out_ref, slots, ss, sr):
+    c, t = lax.axis_index("ctx"), lax.axis_index("tp")
+    n, tp = lax.axis_size("ctx"), lax.axis_size("tp")
+    me = c * tp + t
+    everyone = [(far_c, far_t) for far_c in range(n) for far_t in range(tp)]
+    signal_all(
+        [({"ctx": far_c, "tp": far_t}, (c != far_c) | (t != far_t)) for far_c, far_t in everyone]
+    )
+
+    def copy(far_c, far_t):
+        return pltpu.make_async_remote_copy(
+            src_ref=x_ref,
+            dst_ref=slots.at[me],
+            send_sem=ss.at[far_c * tp + far_t],
+            recv_sem=sr.at[me],
+            device_id={"ctx": far_c, "tp": far_t},
+            device_id_type=MESH,
+        )
+
+    for far_c, far_t in everyone:
+
+        @pl.when((c != far_c) | (t != far_t))
+        def _():
+            copy(far_c, far_t).start()
+
+    slots[me] = x_ref[...]
+    for at in range(n * tp):
+
+        @pl.when(me != at)
+        def _():
+            pltpu.make_async_remote_copy(
+                src_ref=slots.at[at],
+                dst_ref=slots.at[at],
+                send_sem=ss.at[at],
+                recv_sem=sr.at[at],
+                device_id={"tp": lax.rem(t + 1, tp)},
+                device_id_type=MESH,
+            ).wait_recv()
+
+    sums = [sum(slots[far_c * tp + far_t] for far_c in range(n)) for far_t in range(tp)]
+    if over_tp:
+        out_ref[...] = sum(sums)
+    else:
+        for far_t in range(tp):
+            out_ref[far_t] = sums[far_t]
+    for far_c, far_t in everyone:
+
+        @pl.when((c != far_c) | (t != far_t))
+        def _():
+            copy(far_c, far_t).wait_send()
+
+
+def share(v, over_tp, ident):
+    n, tp = lax.axis_size("ctx"), lax.axis_size("tp")
+    dma = pltpu.SemaphoreType.DMA
+    near = pl.BlockSpec(memory_space=pltpu.VMEM)
+    return pl.pallas_call(
+        functools.partial(share_kernel, over_tp),
+        cost_estimate=pl.CostEstimate(flops=8 * MICRO, bytes_accessed=0, transcendentals=0),
+        out_shape=jax.ShapeDtypeStruct(v.shape if over_tp else (tp,) + v.shape, v.dtype),
+        in_specs=[near],
+        out_specs=near,
+        scratch_shapes=[pltpu.VMEM((n * tp,) + v.shape, v.dtype)] + [dma((n * tp,))] * 2,
+        compiler_params=pltpu.CompilerParams(
+            collective_id=ident, has_side_effects=True, vmem_limit_bytes=32 << 20
+        ),
+    )(v)
 
 
 def body(
@@ -908,6 +1135,15 @@
             total = total + lax.ppermute(blocks[s].astype(BF16), "dp", pairs).astype(F32)
         return total
 
+    def swap(blocks):
+        return [
+            lax.ppermute(blocks[s], "dp", [(i, (i + s) % dp_count) for i in range(dp_count)])
+            for s in range(1, dp_count)
+        ]
+
+    def add(blocks, arrived):
+        return sum(v.astype(F32) for v in [blocks[0]] + arrived).astype(BF16)
+
     def columns(v):
         return lax.dynamic_slice_in_dim(v, column_at * part, part, v.ndim - 1)
 
@@ -930,12 +1166,38 @@
         return lax.dynamic_slice_in_dim(back, tp_at * local, local)
 
     gain_q, gain_k = heads_gain(gains[1]), heads_gain(gains[2])
-    query_w, key_w, value_w = fetch(w_query), fetch(w_key), fetch(w_value)
+    own_cols = local // ctx_count
+    head_at = tp_at * local + ctx_at * own_cols
+
+    def own_heads(w):
+        return lax.dynamic_slice_in_dim(w, ctx_at * own_cols, own_cols, 1)
+
+    def natural(v):
+        return jnp.roll(v, dp_at * wide, axis=-1)
+
+    gain_q, gain_k = lax.dynamic_slice_in_dim(natural(gains[1:3]), head_at, own_cols, 1)
+    heads_w = fetch(jnp.concatenate([own_heads(w) for w in (w_query, w_key, w_value)], axis=1))
     out_w = fetch(w_out)
-    gate_others = fetch(own_experts(w_gate))[1:]
-    up_others = fetch(own_experts(w_up))[1:]
-    down_others = fetch(own_experts(w_down))[1:]
+    weights = (w_gate, w_up, w_down)
+    beside = jnp.bitwise_xor(ctx_at, 2)
+
+    def experts_of(w, plane):
+        return lax.dynamic_slice_in_dim(w, plane * mine, mine, 0)
+
+
+    def both(ws, plane):
+        gate, up, down = (experts_of(w, plane) for w in ws)
+        return [jnp.concatenate([gate, up]), down]
+
+    own_slices = both(weights, ctx_at)
     tokens = jnp.roll(tokens, -dp_at * wide, axis=1)
+
+    inputs = tokens.astype(F32)
+    scale_one = lax.rsqrt(jnp.mean(inputs * inputs, axis=1, keepdims=True) + EPS)
+    hidden_one = columns((inputs * scale_one * gain_one).astype(BF16))
+    hidden_one, own_slices = lax.optimization_barrier((hidden_one, own_slices))
+    own_others = [fetch(w)[1:] for w in own_slices]
+    hidden_one = spread(hidden_one, 1)
     cotangent = jnp.roll(cotangent, -dp_at * wide, axis=1)
     chosen = jnp.any(
         routes[:, :, None] == jnp.arange(experts, dtype=jnp.int32)[None, None, :], axis=1
@@ -948,76 +1210,103 @@
         axis=1,
     )
     upstream_all = lax.all_gather(upstream_all, "ctx", axis=0, tiled=True)
+    raw = sum(dot(block(hidden_one, s), w) for s, w in enumerate(heads_w))
+    q_raw, k_raw = raw[:, :own_cols], raw[:, own_cols : 2 * own_cols]
+    values = raw[:, 2 * own_cols :].astype(BF16)
+    pack = raw.shape[0]
+    squares = share(
+        jnp.stack([jnp.sum(q_raw * q_raw, axis=1), jnp.sum(k_raw * k_raw, axis=1)]), True, 5
+    )
+    squares, out_w = lax.optimization_barrier((squares, out_w))
+    q_scale, k_scale = lax.rsqrt(squares / width + EPS)[:, :, None]
+    q_hat, k_hat = q_raw * q_scale, k_raw * k_scale
+    cosine, sine = rotation(lengths[0], 0, pack)
+    mine_heads = own_cols // HEAD
+
+    def turn(v, sine):
+        return rotate(v.reshape(pack, mine_heads, HEAD), cosine, sine)
+
+    def by_head(v):
+        return v.astype(BF16).reshape(pack, mine_heads, HEAD).transpose(1, 0, 2)
+
+    q_all, k_all = by_head(turn(q_hat * gain_q, sine)), by_head(turn(k_hat * gain_k, sine))
+    v_all = by_head(values)
+    attended_all, log = attend(lengths, q_all, k_all, v_all)
+    attended_all, own_others[0] = lax.optimization_barrier((attended_all, own_others[0]))
+    attended = to_rows((attended_all,))[0].reshape(rows, local)
+    branch = jnp.concatenate([dot(attended, w).astype(BF16) for w in out_w], axis=1)
+    branch, upstream_all = lax.optimization_barrier((branch, upstream_all))
     chosen_all = upstream_all[:, part : part + experts].astype(F32)
     upstream_all = lax.all_gather(upstream_all[:, :part], "tp", axis=1, tiled=True)
-
-    inputs = tokens.astype(F32)
-    scale_one = lax.rsqrt(jnp.mean(inputs * inputs, axis=1, keepdims=True) + EPS)
-    hidden_one = (inputs * scale_one * gain_one).astype(BF16)
-
-    def project(blocks):
-        return sum(dot(block(hidden_one, s), w) for s, w in enumerate(blocks))
-
-    q_raw, k_raw = project(query_w), project(key_w)
-    values = project(value_w).astype(BF16)
-    squares = lax.psum(
-        jnp.stack([jnp.sum(q_raw * q_raw, axis=1), jnp.sum(k_raw * k_raw, axis=1)]), "tp"
-    )
-    q_scale, k_scale = lax.rsqrt(squares / width + EPS)[:, :, None]
-    q_hat, k_hat = q_raw * q_scale, k_raw * k_scale
-    cosine, sine = rotation(lengths[0], ctx_at * rows, rows)
-
-    def turn(v):
-        return rotate(v.reshape(rows, heads, HEAD), cosine, sine).astype(BF16)
-
-    q_all, k_all, v_all = to_heads(
-        (turn(q_hat * gain_q), turn(k_hat * gain_k), values), heads
-    )
-    q_all, out_w, gate_others = lax.optimization_barrier((q_all, out_w, gate_others))
-    attended_all, log = attend(lengths, q_all, k_all, v_all)
-    attended = to_rows((attended_all,))[0].reshape(rows, local)
-    branch = jnp.concatenate([dot(attended, w).astype(BF16) for w in out_w], axis=1)
-    branch, up_others = lax.optimization_barrier((branch, up_others))
     branch = collect(branch, 1, 2)
+    branch, late = lax.optimization_barrier((branch, weights))
+    far_slices = both(late, beside)
+    far_others = [fetch(w)[1:] for w in far_slices]
     inputs_c = columns(inputs)
     mixed = inputs_c + branch
     square = lax.psum(jnp.sum(mixed * mixed, axis=1), "tp")
     scale_two = lax.rsqrt(square / width + EPS)[:, None]
     normed_two = mixed * scale_two
     hidden_mine = (normed_two * gain_two).astype(BF16)
+    hidden_mine, own_others[1] = lax.optimization_barrier((hidden_mine, own_others[1]))
     hidden_two = spread(hidden_mine, 3)
-    hidden_two, down_others = lax.optimization_barrier((hidden_two, down_others))
-
-    parts, sums = [], []
+
+    tie = lax.optimization_barrier
+    grads, sums, there = {}, {}, {}
+
+    def run(e):
+        far = e >= mine
+        w = far_w if far else own_w
+        number = e % mine
+        out = expert(
+            number, hidden_two, upstream_all, chosen_all, router_w, w, far, not far, [], 20 + e
+        )
+        grads[e] = [out[-2], out[-1]]
+        return list(out[:-2])
+
+    def start_x(e):
+        grads[e][1] = swap([None] + [grads[e][1][s] for s in range(dp_count - 1)])
+
+    def end_x(e, after):
+        grads[e][1], after = tie((grads[e][1], after))
+        sums[e] = add([grads[e][0]], grads[e][1])
+        return after
+
+    def start_z(e):
+        there[e] = lax.ppermute(sums[e], "ctx", [(i, i ^ 1) for i in range(ctx_count)])
+
+    def end_z(e, after):
+        there[e], after = tie((there[e], after))
+        return after
+
+    own_w = [[w] + o for w, o in zip(own_slices, own_others)]
+    far_w = [[w] + o for w, o in zip(far_slices, far_others)]
+    parts = []
     for e in range(mine):
-        at = ctx_at * mine + e
-        if e > 1:
-            hidden_two, sums[e - 2] = lax.optimization_barrier((hidden_two, sums[e - 2]))
-        parts.append(
-            expert(
-                jnp.stack([at, jnp.int32(e)]).astype(jnp.int32),
-                hidden_two,
-                upstream_all,
-                chosen_all,
-                router_w,
-                [w_gate] + gate_others,
-                [w_up] + up_others,
-                [w_down] + down_others,
-            )
-        )
-        sums.append(hand_over(list(parts[-1][-1])).astype(BF16))
-
-    gathered = [lax.all_gather(v, "ctx", axis=0, tiled=False) for v in sums]
-
+        parts.append(run(e))
+        if e > 0:
+            hidden_two = end_x(e - 1, (hidden_two, grads[e][1]))[0]
+            start_z(e - 1)
+        if e > 2:
+            hidden_two = end_z(e - 3, hidden_two)
+        start_x(e)
+    mixture = mixture_parts([p[0] for p in parts], own_w[1], tp_count)
+    mixture, hidden_two = tie((mixture, hidden_two))
+    mixture = lax.psum_scatter(mixture, "tp", scatter_dimension=0, tiled=False)
     dots = jnp.concatenate([p[3] for p in parts], axis=1).T
+    dots, hidden_two = tie((dots, hidden_two))
     expert_in, dots = returns(
         [[p[1] for p in parts], [p[2] for p in parts]],
-        [w_gate, w_up],
-        [gate_others, up_others],
+        own_w[0][0],
+        own_w[0][1:],
         dots,
         False,
         4,
     )
+    for e in range(1, mine - 1):
+        expert_in = end_z(e, expert_in)
+    expert_in = end_x(mine - 1, expert_in)
+    start_z(mine - 1)
 
     dots = dots.reshape(experts, rows).T
     hidden_rows = lax.dynamic_slice_in_dim(hidden_two, ctx_at * rows, rows, 0)
@@ -1035,111 +1324,126 @@
     )
 
     d_branch = join(d_mixed.astype(BF16), 7)
+    d_branch = end_z(mine - 1, d_branch)
+    hidden_two, d_branch = tie((hidden_two, d_branch))
     d_attended = sum(dot_t(block(d_branch, s), w) for s, w in enumerate(out_w)).astype(BF16)
+    out_grad = swap([t_dot(block(d_branch, s), attended).astype(BF16) for s in range(dp_count)])
+    out_mine = t_dot(block(d_branch, 0), attended)
     d_all = to_heads((d_attended,), heads)[0]
-    d_all, gathered[0] = lax.optimization_barrier((d_all, gathered[0]))
+    run(mine)
+    start_x(mine)
+    mixture, grads[mine][0] = tie((mixture, grads[mine][0]))
+    mixture = lax.psum_scatter(mixture, "ctx", scatter_dimension=0, tiled=True)
+    d_all, grads[mine][0] = tie((d_all, grads[mine][0]))
     dq_all, dk_all, dv_all = attend_back(lengths, q_all, k_all, v_all, d_all, log)
-    d_query, d_key, d_value = to_rows((dq_all, dk_all, dv_all))
-    d_values_raw = d_value.reshape(rows, local)
-    d_q_normed = rotate(d_query.astype(F32), cosine, -sine).reshape(rows, local)
-    d_k_normed = rotate(d_key.astype(F32), cosine, -sine).reshape(rows, local)
+    def by_token(v):
+        return v.transpose(1, 0, 2).reshape(pack, own_cols)
+
+    d_q_normed = turn(by_token(dq_all), -sine).reshape(pack, own_cols)
+    d_k_normed = turn(by_token(dk_all), -sine).reshape(pack, own_cols)
     q_pull, k_pull = d_q_normed * gain_q, d_k_normed * gain_k
-    totals = lax.psum(
-        jnp.stack([jnp.sum(q_pull * q_raw, axis=1), jnp.sum(k_pull * k_raw, axis=1)]), "tp"
+    totals = share(
+        jnp.stack([jnp.sum(q_pull * q_raw, axis=1), jnp.sum(k_pull * k_raw, axis=1)]), True, 6
     )
     q_mean, k_mean = totals[:, :, None] / width
     d_q_raw = (q_scale * q_pull - q_raw * q_scale**3 * q_mean).astype(BF16)
     d_k_raw = (k_scale * k_pull - k_raw * k_scale**3 * k_mean).astype(BF16)
-    d_hidden = jnp.concatenate(
-        [
-            (
-                dot_t(d_q_raw, query_w[s])
-                + dot_t(d_k_raw, key_w[s])
-                + dot_t(d_values_raw, value_w[s])
-            ).astype(BF16)
-            for s in range(dp_count)
-        ],
-        axis=1,
-    )
-    d_hidden, gathered[1] = lax.optimization_barrier((d_hidden, gathered[1]))
-    d_hidden = collect(d_hidden, 1, 8)
+    d_raw = jnp.concatenate([d_q_raw, d_k_raw, by_token(dv_all)], axis=1)
+    heads_mine = t_dot(block(hidden_one, 0), d_raw)
+    heads_grads = swap([t_dot(block(hidden_one, s), d_raw).astype(BF16) for s in range(dp_count)])
+    d_raw, hidden_two = tie((d_raw, hidden_two))
+    for e in range(mine + 1, 2 * mine):
+        run(e)
+        hidden_two, d_raw = end_x(e - 1, (hidden_two, d_raw, grads[e][1]))[:2]
+        start_z(e - 1)
+        if e > mine + 1:
+            hidden_two, d_raw = end_z(e - 2, (hidden_two, d_raw))
+        start_x(e)
+        if e == mine + 1:
+            mixture, d_raw = tie((mixture, d_raw))
+            output = lax.all_gather(mixed + mixture.astype(F32), "tp", axis=0, tiled=False)
+        if e == mine + 2:
+            heads_grads, output, d_raw = tie((heads_grads, output, d_raw))
+            heads_grads = add([heads_mine], heads_grads)
+            heads_grads = lax.all_gather(heads_grads, "ctx", axis=0, tiled=False)
+        if e == mine + 3:
+            out_grad, heads_grads, d_raw = tie((out_grad, heads_grads, d_raw))
+            out_grad = add([out_mine], out_grad)
+            out_grad = lax.psum_scatter(out_grad, "ctx", scatter_dimension=0, tiled=True)
+            out_grad = lax.all_gather(out_grad, "ctx", axis=0, tiled=True)
+    d_raw, far = tie((d_raw, grads[2 * mine - 1][0]))
+    (d_hidden,) = returns(
+        [[d_raw]],
+        heads_w[0][None],
+        [w[None] for w in heads_w[1:]],
+        None,
+        False,
+        8,
+    )
+    d_hidden = end_z(2 * mine - 2, end_x(2 * mine - 1, d_hidden))
+    start_z(2 * mine - 1)
     gain_one_grad = jnp.sum(d_hidden * inputs_c * scale_one, axis=0)
     pull_one = d_hidden * columns(gain_one)
     mean_one = lax.psum(jnp.sum(pull_one * inputs_c, axis=1), "tp")[:, None] / width
     d_inputs = d_mixed + scale_one * pull_one - inputs_c * scale_one**3 * mean_one
-    d_inputs = jnp.roll(join(d_inputs, 9), dp_at * wide, axis=1)
-
-    def in_order(v):
-        return jnp.roll(v, dp_at * wide, axis=-1)
-
+
+    def whole(every):
+        every = [every[(p % 2) * 2 + p // 2] for p in range(tp_count)]
+        return natural(jnp.concatenate(every, axis=1))
+
+    output = whole(output)
+    d_inputs = join(d_inputs, 10)
+    gain_one_grad, d_inputs = tie((gain_one_grad, d_inputs))
+    d_inputs = natural(d_inputs)
+    heads_gains = lax.dynamic_update_slice_in_dim(
+        jnp.zeros((2, local), F32),
+        jnp.stack([jnp.sum(d_q_normed * q_hat, axis=0), jnp.sum(d_k_normed * k_hat, axis=0)]),
+        ctx_at * own_cols,
+        1,
+    )
     small_grads = jnp.concatenate(
-        [
-            gain_one_grad[None],
-            gain_two_grad[None],
-            router_grad,
-            jnp.sum(d_q_normed * q_hat, axis=0)[None],
-            jnp.sum(d_k_normed * k_hat, axis=0)[None],
-        ]
-    )
-    small_grads = lax.all_gather(small_grads, "tp", axis=0, tiled=False)
+        [gain_one_grad[None], gain_two_grad[None], router_grad, heads_gains]
+    )
+    small_grads = jnp.pad(small_grads, ((0, -small_grads.shape[0] % 8), (0, 0)))
+    small_grads = share(small_grads, False, 9)
+
     turned = [small_grads[(p % 2) * 2 + p // 2, : 2 + experts] for p in range(tp_count)]
-    heads_grads = small_grads[:, 2 + experts :].transpose(1, 0, 2).reshape(2, width)
-    heads_grads = jnp.roll(heads_grads, -dp_at * wide, axis=1)
-    small_grads = jnp.concatenate([jnp.concatenate(turned, axis=1), heads_grads])
-    small_rows = small_grads.shape[0] * wide // local
-    filler = -small_rows % (16 * ctx_count)
-
-    def grad_blocks(s):
-        hidden, grads = block(hidden_one, s), (d_q_raw, d_k_raw, d_values_raw)
-        small = block(small_grads, s).reshape(small_rows, local)
-        return jnp.concatenate(
-            [t_dot(hidden, d) for d in grads]
-            + [t_dot(block(d_branch, s), attended), jnp.pad(small, ((0, filler), (0, 0)))]
+    heads_gains = small_grads[:, 2 + experts : 4 + experts].transpose(1, 0, 2).reshape(2, width)
+    small_grads = jnp.concatenate([natural(jnp.concatenate(turned, axis=1)), heads_gains])
+    small_grads = hand_over(
+        [small_grads if s == 0 else small_grads for s in range(dp_count)]
+    )
+    small_grads = lax.dynamic_slice_in_dim(small_grads, dp_at * wide, wide, 1)
+
+    def heads_grad(i):
+        v = heads_grads[:, :, i * own_cols : (i + 1) * own_cols].astype(F32)
+        return v.transpose(1, 0, 2).reshape(wide, local)
+
+    held = []
+    for e in range(2 * mine - 1):
+        there[e], d_hidden = tie((there[e], d_hidden))
+    for e in range(2 * mine):
+        plane = ctx_at if e < mine else beside
+        at = plane * mine + e % mine
+        other = jnp.bitwise_xor(plane, 1) * mine + e % mine
+        held = place_grads(
+            jnp.stack([at, other]).astype(jnp.int32), sums[e], there[e], experts, held
         )
-
-    grads = hand_over([grad_blocks(s) for s in range(dp_count)]).astype(BF16)
-    grads = lax.psum_scatter(grads, "ctx", scatter_dimension=0, tiled=True)
-    grads = lax.all_gather(grads, "ctx", axis=0, tiled=True).astype(F32)
-    grad_query, grad_key, grad_value, grad_out = (
-        grads[i * wide : (i + 1) * wide] for i in range(4)
-    )
-    small_grads = grads[4 * wide : 4 * wide + small_rows].reshape(-1, wide)
-
-    inners = [p[0] for p in parts]
-    inners, d_inputs = lax.optimization_barrier((inners, d_inputs))
-    (mixture,) = returns([inners], [w_down], [down_others], None, True, 5)
-    mixture, gathered[2] = lax.optimization_barrier((mixture, gathered[2]))
-    output = jnp.roll(join(mixed + mixture, 6), dp_at * wide, axis=1)
-
-    fine = w_gate.shape[2]
-
-    def assemble(which):
-        each = [v[:, which].astype(F32) for v in gathered]
-        if which == 2:
-            each = [
-                v.reshape(ctx_count, wide // fine, fine, fine)
-                .transpose(0, 2, 1, 3)
-                .reshape(ctx_count, fine, wide)
-                for v in each
-            ]
-        stacked = jnp.stack(each, axis=1)
-        return stacked.reshape((experts,) + stacked.shape[2:])
-
     return (
         output,
         d_inputs,
         small_grads[0],
-        grad_query,
-        grad_key,
-        grad_value,
+        heads_grad(0),
+        heads_grad(1),
+        heads_grad(2),
         small_grads[2 + experts],
         small_grads[3 + experts],
-        grad_out.T,
+        out_grad.astype(F32).T,
         small_grads[1],
         small_grads[2 : 2 + experts].T,
-        assemble(0),
-        assemble(1),
-        assemble(2),
+        held[0],
+        held[1],
+        held[2],
     )
 
 

time: 1270 us -> 1090 us (0.86)
  waiting for transfers between devices: 380 us -> 88.6 us
  Pallas kernels: 491 us -> 700 us
  local copies, waits for them, and re-layouts: 120 us -> 63.2 us
  other arithmetic: 121 us -> 77.8 us
    pallas_call x4 -> x20, Pallas kernels: 104 us -> 284 us  [the longest x8 197 us: expert(): pl.pallas_call(functools.partial(expert_kernel, blocks, e, far, mine, ful...]
    ppermute x5 -> x1, waiting for transfers between devices: 143 us -> 0.01 us  [hand_over(): lax.ppermute(blocks[s].astype(BF16), 'dp', pairs).astype(F32)]
    pallas_call x1 -> x2, Pallas kernels: 62.1 us -> 160 us  [spread(): pl.pallas_call(spread_kernel, cost_estimate=pl.CostEstimate(flops=60 * MI...]
    ppermute x8 -> x7, waiting for transfers between devices: 90.6 us -> 11.3 us  [fetch(): lax.ppermute(v, 'dp', [((i + s) % dp_count, i) for i in range(dp_count)])]
    ppermute x0 -> x18, waiting for transfers between devices: none -> 77.1 us  [the longest x8 50.6 us: start_z(): lax.ppermute(sums[e], 'ctx', [(i, i ^ 1) for i in range(ctx_count)])]
    all_to_all x2 -> x0, waiting for transfers between devices: 59.1 us -> none  [to_rows(): got = lax.all_to_all(sent, 'ctx', 0, 0, tiled=True)]
    all_gather x5 -> x3, waiting for transfers between devices: 46.3 us -> 0.01 us  [the longest x1 0.01 us: body(): lax.all_gather(mixed + mixture.astype(F32), 'tp', axis=0, tiled=False)]
    ppermute x0 -> x18, starting transfers between devices: none -> 41.8 us  [the longest x8 33.1 us: start_z(): lax.ppermute(sums[e], 'ctx', [(i, i ^ 1) for i in range(ctx_count)])]
  transfers between devices with their start and end apart: 25 -> 35, of which waited for: 14 -> 6; matrix products, arithmetic and copies ran while one was open for 20% -> 13% of each run, Pallas kernels for 37% -> 63%
where the time goes in v2:
time: 1090 us; the launch traced here: 1080 us
  Pallas kernels  700 us (64%)
  waiting for transfers between devices  88.6 us (8%)
  other arithmetic  77.8 us (7%)
  local copies, waits for them, and re-layouts  63.2 us (6%)
  starting transfers between devices  57 us (5%)
  blocking collectives  40.5 us (4%)
  matrix products  35.5 us (3%)
  between operations  15.8 us (1%)
    pallas_call x8, Pallas kernels, expert(): pl.pallas_call(functools.partial(expert_kernel, blocks, e, far, mine, ful...  197 us
    pallas_call x2, Pallas kernels, returns(): pl.pallas_call(functools.partial(returns_kernel, kinds, mine, blocks, fli...  160 us
    pallas_call x2, Pallas kernels, spread(): pl.pallas_call(spread_kernel, cost_estimate=pl.CostEstimate(flops=60 * MI...  160 us
    pallas_call x2, Pallas kernels, join(): pl.pallas_call(join_kernel, cost_estimate=pl.CostEstimate(flops=25 * MICR...  53 us
    ppermute x8, waiting for transfers between devices, start_z(): lax.ppermute(sums[e], 'ctx', [(i, i ^ 1) for i in range(ctx_count)])  50.6 us
    pallas_call x8, Pallas kernels, place_grads(): pl.pallas_call(place_kernel, cost_estimate=pl.CostEstimate(flops=4 * MICR...  36.6 us
    pallas_call x3, Pallas kernels, share(): pl.pallas_call(functools.partial(share_kernel, over_tp), cost_estimate=pl...  36.6 us
    ppermute x8, starting transfers between devices, start_z(): lax.ppermute(sums[e], 'ctx', [(i, i ^ 1) for i in range(ctx_count)])  33.1 us
  transfers between devices with their start and end apart: 35, of which 6 were waited for; matrix products, arithmetic and copies ran while one was open for 13% of the time, Pallas kernels for 63%

profile of v2, /device:TPU:0, one launch (start us, length us, event | category | flops | bytes accessed | tf_op | source)
XLA Modules:
  0.0 1077.8 jit_solution(16137581895650042238)
XLA Ops:
  44.9 83.9 %shard_map.263 = bf16[2048,2048]{1,0:T(8,128)(2,1)} custom-call(bf16[512,512]{1,0:T(8,128)(2,1)} %multiply_convert_fusion.1.x_ref), custom_call_target="tpu_custom_call" | custom-call | flops 4026531840 | tf_op jit(solution)/shard_map/pallas_call | solution.py:453
  137.9 7.3 shard_map.264
  149.9 7.1 shard_map.265
  158.3 20.4 %all_to_all.10 = bf16[4,1,1,512,128]{3,4,2,1,0:T(8,128)(2,1)S(1)} all-to-all(bf16[4,1,1,512,128]{3,4,2,1,0:T(8,128)(2,1)S(1)} %copy.92), channel_id=1, replica_groups=mesh['dp'=2,'ctx'=4,'tp'=4] {'ctx'}, dimensions={0} | all-to-all | bytes 1048576 | tf_op jit(solution)/shard_map/all_to_all | solution.py:153
  187.2 25.2 %shard_map.266 = f32[512,512]{1,0:T(8,128)S(1)} custom-call(bf16[512,2048]{1,0:T(8,128)(2,1)S(1)} %pad_maximum_fusion.2.x_ref), custom_call_target="tpu_custom_call" | custom-call | flops 1140850688 | tf_op jit(solution)/shard_map/pallas_call | solution.py:642
  213.8 8.0 psum.21
  222.8 9.1 collective-permute-done.4.refs_9_.refs_5_
  231.9 75.8 %shard_map.267.refs_0_ = bf16[2048,2048]{1,0:T(8,128)(2,1)} custom-call(bf16[512,512]{1,0:T(8,128)(2,1)} %multiply_convert_fusion.x_ref), custom_call_target="tpu_custom_call" | custom-call | flops 4026531840 | tf_op jit(solution)/shard_map/pallas_call | solution.py:453
  309.8 24.9 %shard_map.268 = (bf16[2048,256]{1,0:T(8,128)(2,1)}, bf16[2048,256]{1,0:T(8,128)(2,1)}, bf16[2048,256]{1,0:T(8,128)(2,1)}, f32[2048,1]{1,0:T(8,128)}, bf16[3,102...) custom-call(bf16[2048,2048]{1,0:T(8,128)(2,1)} %shard_map.267.refs_0_, ...), custom_call_target="tpu_custom_call" | custom-call | flops 1811939328 | tf_op jit(solution)/shard_map/pallas_call | solution.py:299
  334.8 24.9 %shard_map.269 = (bf16[2048,256]{1,0:T(8,128)(2,1)}, bf16[2048,256]{1,0:T(8,128)(2,1)}, bf16[2048,256]{1,0:T(8,128)(2,1)}, f32[2048,1]{1,0:T(8,128)}, bf16[3,102...) custom-call(bf16[2048,2048]{1,0:T(8,128)(2,1)} %shard_map.267.refs_0_, ...), custom_call_target="tpu_custom_call" | custom-call | flops 1811939328 | tf_op jit(solution)/shard_map/pallas_call | solution.py:299
  361.8 10.4 collective-permute-done.5
  372.2 25.1 %shard_map.270 = (bf16[2048,256]{1,0:T(8,128)(2,1)}, bf16[2048,256]{1,0:T(8,128)(2,1)}, bf16[2048,256]{1,0:T(8,128)(2,1)}, f32[2048,1]{1,0:T(8,128)}, bf16[3,102...) custom-call(bf16[2048,2048]{1,0:T(8,128)(2,1)} %shard_map.267.refs_0_, ...), custom_call_target="tpu_custom_call" | custom-call | flops 1811939328 | tf_op jit(solution)/shard_map/pallas_call | solution.py:299
  397.9 8.0 collective-permute-done.6
  405.9 25.4 %shard_map.271 = (bf16[2048,256]{1,0:T(8,128)(2,1)}, bf16[2048,256]{1,0:T(8,128)(2,1)}, bf16[2048,256]{1,0:T(8,128)(2,1)}, f32[2048,1]{1,0:T(8,128)}, bf16[3,102...) custom-call(bf16[2048,2048]{1,0:T(8,128)(2,1)} %shard_map.267.refs_0_, ...), custom_call_target="tpu_custom_call" | custom-call | flops 1811939328 | tf_op jit(solution)/shard_map/pallas_call | solution.py:299
  432.6 13.3 %shard_map.272 = bf16[4,2048,512]{2,1,0:T(8,128)(2,1)} custom-call(bf16[2048,256]{1,0:T(8,128)(2,1)S(1)} %copy-done.20, bf16[2048,256]{1,0:T(8,128)(2,1)S(1)} %copy-done.21, bf16[2048,256]{1,0:T(8,128)(2,1)S(1)} %copy-done.22, bf16[2048,256]{1,0:T(8,128)(2,1)S(1)} %copy-done.23, bf16[4,256,1024]{2,1,0:T(8,128)(2,1)} %constant_dynamic-slice_fusion.11.refs_8_.refs_4_, ...), custom_call_target="tpu_custom_call" | custom-call | flops 1006632960 | tf_op jit(solution)/shard_map/pallas_call | solution.py:979
  471.6 91.8 %shard_map.273 = (f32[512,512]{1,0:T(8,128)}, f32[4,4,512]{2,1,0:T(4,128)}) custom-call(bf16[2048,256]{1,0:T(8,128)(2,1)} %get-tuple-element.191.refs_0_, bf16[2048,256]{1,0:T(8,128)(2,1)} %get-tuple-element.192.refs_1_, bf16[2048,256]{1,0:T(8,128)(2,1)} %get-tuple-element.193.refs_2_, bf16[2048,256]{1,0:T(8,128)(2,1)} %get-tuple-element.194.refs_3_, ...), custom_call_target="tpu_custom_call" | custom-call | flops 4362076160 | tf_op jit(solution)/shard_map/pallas_call | solution.py:929
  566.5 9.6 collective-permute-start.12
  581.4 6.0 psum.22
  591.3 18.9 %shard_map.274 = bf16[512,2048]{1,0:T(8,128)(2,1)} custom-call(bf16[512,512]{1,0:T(8,128)(2,1)} %get-tuple-element.358.x_ref), custom_call_target="tpu_custom_call" | custom-call | flops 1677721600 | tf_op jit(solution)/shard_map/pallas_call | solution.py:492
  622.7 24.3 %shard_map.275 = (bf16[3,1024,256]{2,1,0:T(8,128)(2,1)}, bf16[1,3,1024,256]{3,2,1,0:T(8,128)(2,1)}) custom-call(bf16[2048,2048]{1,0:T(8,128)(2,1)} %shard_map.267.refs_0_, bf16[2048,2048]{1,0:T(8,128)(2,1)} %all-gather.10.cloned.1.call-done.refs_1_, f32[2048,16]{1,0:T(8,128)} %slice_convert_fusion.1.refs_2_, bf16[16,2048]{1,0:T(8,128)(2,1)} %pad_maximum_fusion.9.refs_3_, ...), custom_call_target="tpu_custom_call" | custom-call | flops 1811939328 | tf_op jit(solution)/shard_map/pallas_call | solution.py:299
  652.0 10.3 shard_map.276
  667.2 13.4 %shard_map.277 = f32[2,2048]{1,0:T(2,128)S(1)} custom-call(f32[2,2048]{1,0:T(2,128)S(1)} %pad_maximum_fusion.11.x_ref), custom_call_target="tpu_custom_call" | custom-call | flops 536870912 | tf_op jit(solution)/shard_map/pallas_call | solution.py:1082
  684.3 24.2 %shard_map.278 = (bf16[3,1024,256]{2,1,0:T(8,128)(2,1)}, bf16[1,3,1024,256]{3,2,1,0:T(8,128)(2,1)}) custom-call(bf16[2048,2048]{1,0:T(8,128)(2,1)} %shard_map.267.refs_0_, bf16[2048,2048]{1,0:T(8,128)(2,1)} %all-gather.10.cloned.1.call-done.refs_1_, f32[2048,16]{1,0:T(8,128)} %slice_convert_fusion.1.refs_2_, bf16[16,2048]{1,0:T(8,128)(2,1)} %pad_maximum_fusion.9.refs_3_, ...), custom_call_target="tpu_custom_call" | custom-call | flops 1811939328 | tf_op jit(solution)/shard_map/pallas_call | solution.py:299
  726.3 24.2 %shard_map.279 = (bf16[3,1024,256]{2,1,0:T(8,128)(2,1)}, bf16[1,3,1024,256]{3,2,1,0:T(8,128)(2,1)}) custom-call(bf16[2048,2048]{1,0:T(8,128)(2,1)} %shard_map.267.refs_0_, bf16[2048,2048]{1,0:T(8,128)(2,1)} %all-gather.10.cloned.1.call-done.refs_1_, f32[2048,16]{1,0:T(8,128)} %slice_convert_fusion.1.refs_2_, bf16[16,2048]{1,0:T(8,128)(2,1)} %pad_maximum_fusion.9.refs_3_, ...), custom_call_target="tpu_custom_call" | custom-call | flops 1811939328 | tf_op jit(solution)/shard_map/pallas_call | solution.py:299
  757.3 8.1 collective-permute-done.15
  782.9 24.3 %shard_map.280 = (bf16[3,1024,256]{2,1,0:T(8,128)(2,1)}, bf16[1,3,1024,256]{3,2,1,0:T(8,128)(2,1)}) custom-call(bf16[2048,2048]{1,0:T(8,128)(2,1)} %shard_map.267.refs_0_, bf16[2048,2048]{1,0:T(8,128)(2,1)} %all-gather.10.cloned.1.call-done.refs_1_, f32[2048,16]{1,0:T(8,128)} %slice_convert_fusion.1.refs_2_, bf16[16,2048]{1,0:T(8,128)(2,1)} %pad_maximum_fusion.9.refs_3_, ...), custom_call_target="tpu_custom_call" | custom-call | flops 1811939328 | tf_op jit(solution)/shard_map/pallas_call | solution.py:299
  811.8 50.5 %collective-permute-done.23.far_ref = bf16[3,1024,256]{2,1,0:T(8,128)(2,1)S(1)} collective-permute-done((bf16[3,1024,256]{2,1,0:T(8,128)(2,1)S(1)}, bf16[3,1024,256]{2,1,0:T(8,128)(2,1)S(1)}, u32[]{:S(2)}, u32[]{:S(2)}) %collective-permute-start.23) | collective-permute-done | bytes 1572896 | tf_op jit(solution)/shard_map/ppermute | solution.py:1276
  868.1 68.4 %shard_map.281 = f32[512,512]{1,0:T(8,128)} custom-call(bf16[2048,384]{1,0:T(8,128)(2,1)} %pad_maximum_fusion.3.refs_0_, bf16[1,1024,384]{2,1,0:T(8,128)(2,1)} %get-tuple-element.384.refs_1_, bf16[1,1024,384]{2,1,0:T(8,128)(2,1)} %bitcast.60.refs_2_), custom_call_target="tpu_custom_call" | custom-call | flops 4362076160 | tf_op jit(solution)/shard_map/pallas_call | solution.py:929
  942.7 12.5 %collective-permute-start.25 = (bf16[3,1024,256]{2,1,0:T(8,128)(2,1)}, bf16[3,1024,256]{2,1,0:T(8,128)(2,1)}, u32[]{:S(2)}, u32[]{:S(2)}) collective-permute-start(bf16[3,1024,256]{2,1,0:T(8,128)(2,1)} %add_convert_fusion.near_ref), channel_id=1, source_target_pairs={{0,4},{4,0},{8,12},{12,8},{1,5},{5,1},{9,13},{13,9},{2,6},{6,2},{1... | collective-permute-start | bytes 4718600 | tf_op jit(solution)/shard_map/ppermute | solution.py:1276
  956.9 6.1 psum.23
  966.1 34.2 %shard_map.282 = f32[512,2048]{1,0:T(8,128)} custom-call(f32[512,512]{1,0:T(8,128)} %multiply_subtract_fusion.x_ref), custom_call_target="tpu_custom_call" | custom-call | flops 1677721600 | tf_op jit(solution)/shard_map/pallas_call | solution.py:492
  1000.3 15.9 %shard_map.283 = f32[4,24,512]{2,1,0:T(8,128)S(1)} custom-call(f32[24,512]{1,0:T(8,128)S(1)} %select_maximum_fusion.x_ref), custom_call_target="tpu_custom_call" | custom-call | flops 536870912 | tf_op jit(solution)/shard_map/pallas_call | solution.py:1082
  (369 shorter events, 250.4 us)
Async XLA Ops:
  7.2 174.5 %all-gather.8.cloned.1.call-start = ((), (), s32[]{:S(2)}) async-start(), calls=%async_computation.5 | async-start | bytes 3276800 | tf_op jit(solution)/shard_map/all_gather | solution.py:1212
  14.1 131.1 %collective-permute-start.2 = (bf16[512,1024]{1,0:T(8,128)(2,1)}, bf16[512,1024]{1,0:T(8,128)(2,1)}, u32[]{:S(2)}, u32[]{:S(2)}) collective-permute-start(bf16[512,1024]{1,0:T(8,128)(2,1)} %param.30), channel_id=1, source_target_pairs={{16,0},{0,16},{17,1},{1,17},{18,2},{2,18},{19,3},{3,19},{20,4},{4,... | collective-permute-start | bytes 3145736 | tf_op jit(solution)/shard_map/ppermute | solution.py:1126
  16.8 117.0 %collective-permute-start.1 = (bf16[1024,384]{1,0:T(8,128)(2,1)}, bf16[1024,384]{1,0:T(8,128)(2,1)}, u32[]{:S(2)}, u32[]{:S(2)}) collective-permute-start(bf16[1024,384]{1,0:T(8,128)(2,1)} %get-tuple-element.385), channel_id=1, source_target_pairs={{16,0},{0,16},{17,1},{1,17},{18,2},{2,18},{19,3},{3,19},{20,4},{4,... | collective-permute-start | bytes 2359304 | tf_op jit(solution)/shard_map/ppermute | solution.py:1126
  24.3 285.5 %all-gather.10.cloned.1.call-start = ((), (), s32[]{:S(2)}) async-start(), calls=%async_computation.6 | async-start | bytes 10485760 | tf_op jit(solution)/shard_map/all_gather | solution.py:1240
  44.6 113.4 %collective-permute-start.3 = (bf16[8,1024,256]{2,1,0:T(8,128)(2,1)}, bf16[8,1024,256]{2,1,0:T(8,128)(2,1)}, u32[]{:S(2)}, u32[]{:S(2)}) collective-permute-start(bf16[8,1024,256]{2,1,0:T(8,128)(2,1)} %pad_maximum_fusion.refs_4_.refs_6_.refs_8_), channel_id=1, source_target_pairs={{16,0},{0,16},{17,1},{1,17},{18,2},{2,18},{19,3},{3,19},{20,4},{4,... | collective-permute-start | bytes 12582920 | tf_op jit(solution)/shard_map/ppermute | solution.py:1126
  184.8 462.1 %reduce-scatter.4.cloned.1.call-start = ((), (), s32[]{:S(2)}) async-start(), calls=%async_computation.7 | async-start | bytes 10485760 | tf_op jit(solution)/shard_map/reduce_scatter | solution.py:1295
  184.9 47.0 %collective-permute-start.4 = (bf16[4,256,1024]{2,1,0:T(8,128)(2,1)}, bf16[4,256,1024]{2,1,0:T(8,128)(2,1)}, u32[]{:S(2)}, u32[]{:S(2)}) collective-permute-start(bf16[4,256,1024]{2,1,0:T(8,128)(2,1)} %constant_dynamic-slice_fusion.11.refs_8_.refs_4_), channel_id=1, source_target_pairs={{16,0},{0,16},{17,1},{1,17},{18,2},{2,18},{19,3},{3,19},{20,4},{4,... | collective-permute-start | bytes 6291464 | tf_op jit(solution)/shard_map/ppermute | solution.py:1126
  359.7 46.2 %collective-permute-start.6 = (bf16[3,1024,256]{2,1,0:T(8,128)(2,1)}, bf16[3,1024,256]{2,1,0:T(8,128)(2,1)S(1)}, u32[]{:S(2)}, u32[]{:S(2)}) collective-permute-start(bf16[3,1024,256]{2,1,0:T(8,128)(2,1)} %bitcast.231), channel_id=1, source_target_pairs={{0,16},{16,0},{1,17},{17,1},{2,18},{18,2},{3,19},{19,3},{4,20},{20... | collective-permute-start | bytes 4718600 | tf_op jit(solution)/shard_map/ppermute | solution.py:1140
  397.3 48.6 %collective-permute-start.8 = (bf16[3,1024,256]{2,1,0:T(8,128)(2,1)}, bf16[3,1024,256]{2,1,0:T(8,128)(2,1)}, u32[]{:S(2)}, u32[]{:S(2)}) collective-permute-start(bf16[3,1024,256]{2,1,0:T(8,128)(2,1)} %bitcast.230), channel_id=1, source_target_pairs={{0,16},{16,0},{1,17},{17,1},{2,18},{18,2},{3,19},{19,3},{4,20},{20... | collective-permute-start | bytes 4718600 | tf_op jit(solution)/shard_map/ppermute | solution.py:1140
  397.8 48.1 %collective-permute-start.7 = (bf16[3,1024,256]{2,1,0:T(8,128)(2,1)S(1)}, bf16[3,1024,256]{2,1,0:T(8,128)(2,1)S(1)}, u32[]{:S(2)}, u32[]{:S(2)}) collective-permute-start(bf16[3,1024,256]{2,1,0:T(8,128)(2,1)S(1)} %add_convert_fusion.7.near_ref), channel_id=1, source_target_pairs={{0,4},{4,0},{8,12},{12,8},{1,5},{5,1},{9,13},{13,9},{2,6},{6,2},{1... | collective-permute-start | bytes 4718600 | tf_op jit(solution)/shard_map/ppermute | solution.py:1276
  452.5 110.9 %collective-permute-start.11 = (bf16[3,1024,256]{2,1,0:T(8,128)(2,1)S(1)}, bf16[3,1024,256]{2,1,0:T(8,128)(2,1)}, u32[]{:S(2)}, u32[]{:S(2)}) collective-permute-start(bf16[3,1024,256]{2,1,0:T(8,128)(2,1)S(1)} %add_convert_fusion.5.near_ref), channel_id=1, source_target_pairs={{0,4},{4,0},{8,12},{12,8},{1,5},{5,1},{9,13},{13,9},{2,6},{6,2},{1... | collective-permute-start | bytes 4718600 | tf_op jit(solution)/shard_map/ppermute | solution.py:1276
  452.6 110.9 %collective-permute-start.9 = (bf16[3,1024,256]{2,1,0:T(8,128)(2,1)}, bf16[3,1024,256]{2,1,0:T(8,128)(2,1)}, u32[]{:S(2)}, u32[]{:S(2)}) collective-permute-start(bf16[3,1024,256]{2,1,0:T(8,128)(2,1)} %bitcast.30), channel_id=1, source_target_pairs={{0,16},{16,0},{1,17},{17,1},{2,18},{18,2},{3,19},{19,3},{4,20},{20... | collective-permute-start | bytes 4718600 | tf_op jit(solution)/shard_map/ppermute | solution.py:1140
  455.5 108.0 %collective-permute-start.10 = (bf16[3,1024,256]{2,1,0:T(8,128)(2,1)S(1)}, bf16[3,1024,256]{2,1,0:T(8,128)(2,1)}, u32[]{:S(2)}, u32[]{:S(2)}) collective-permute-start(bf16[3,1024,256]{2,1,0:T(8,128)(2,1)S(1)} %add_convert_fusion.6.near_ref), channel_id=1, source_target_pairs={{0,4},{4,0},{8,12},{12,8},{1,5},{5,1},{9,13},{13,9},{2,6},{6,2},{1... | collective-permute-start | bytes 4718600 | tf_op jit(solution)/shard_map/ppermute | solution.py:1276
  459.2 163.5 %collective-permute-start.13 = (bf16[8,1024,256]{2,1,0:T(8,128)(2,1)}, bf16[8,1024,256]{2,1,0:T(8,128)(2,1)}, u32[]{:S(2)}, u32[]{:S(2)}) collective-permute-start(bf16[8,1024,256]{2,1,0:T(8,128)(2,1)} %pad_maximum_fusion.1.refs_4_.refs_6_), channel_id=1, source_target_pairs={{16,0},{0,16},{17,1},{1,17},{18,2},{2,18},{19,3},{3,19},{20,4},{4,... | collective-permute-start | bytes 12582920 | tf_op jit(solution)/shard_map/ppermute | solution.py:1126
  464.2 158.5 %collective-permute-start.14 = (bf16[4,256,1024]{2,1,0:T(8,128)(2,1)}, bf16[4,256,1024]{2,1,0:T(8,128)(2,1)}, u32[]{:S(2)}, u32[]{:S(2)}) collective-permute-start(bf16[4,256,1024]{2,1,0:T(8,128)(2,1)} %constant_dynamic-slice_fusion.4.refs_8_), channel_id=1, source_target_pairs={{16,0},{0,16},{17,1},{1,17},{18,2},{2,18},{19,3},{3,19},{20,4},{4,... | collective-permute-start | bytes 6291464 | tf_op jit(solution)/shard_map/ppermute | solution.py:1126
  566.5 43.7 %collective-permute-start.12 = (bf16[3,1024,256]{2,1,0:T(8,128)(2,1)}, bf16[3,1024,256]{2,1,0:T(8,128)(2,1)}, u32[]{:S(2)}, u32[]{:S(2)}) collective-permute-start(bf16[3,1024,256]{2,1,0:T(8,128)(2,1)} %add_convert_fusion.4.near_ref), channel_id=1, source_target_pairs={{0,4},{4,0},{8,12},{12,8},{1,5},{5,1},{9,13},{13,9},{2,6},{6,2},{1... | collective-permute-start | bytes 4718600 | tf_op jit(solution)/shard_map/ppermute | solution.py:1276
  620.4 88.1 %reduce-scatter.6.cloned.1.call-start = ((), (), s32[]{:S(2)}) async-start(), calls=%async_computation.8 | async-start | bytes 2621440 | tf_op jit(solution)/shard_map/reduce_scatter | solution.py:1336
  647.0 118.5 %all-gather.14.cloned.1.call-start = ((), (), s32[]{:S(2)}) async-start(), calls=%async_computation.11 | async-start | bytes 5242880 | tf_op jit(solution)/shard_map/all_gather | solution.py:1364
  647.3 61.3 %collective-permute-start.16 = (bf16[3,1024,256]{2,1,0:T(8,128)(2,1)}, bf16[3,1024,256]{2,1,0:T(8,128)(2,1)}, u32[]{:S(2)}, u32[]{:S(2)}) collective-permute-start(bf16[3,1024,256]{2,1,0:T(8,128)(2,1)} %bitcast.227), channel_id=1, source_target_pairs={{0,16},{16,0},{1,17},{17,1},{2,18},{18,2},{3,19},{19,3},{4,20},{20... | collective-permute-start | bytes 4718600 | tf_op jit(solution)/shard_map/ppermute | solution.py:1140
  711.1 157.0 %all-gather.16.cloned.1.call-start = ((), (), s32[]{:S(2)}) async-start(), calls=%async_computation.12 | async-start | bytes 3932160 | tf_op jit(solution)/shard_map/all_gather | solution.py:1368
  711.7 44.5 %collective-permute-start.18 = (bf16[3,1024,256]{2,1,0:T(8,128)(2,1)}, bf16[3,1024,256]{2,1,0:T(8,128)(2,1)}, u32[]{:S(2)}, u32[]{:S(2)}) collective-permute-start(bf16[3,1024,256]{2,1,0:T(8,128)(2,1)} %bitcast.229), channel_id=1, source_target_pairs={{0,16},{16,0},{1,17},{17,1},{2,18},{18,2},{3,19},{19,3},{4,20},{20... | collective-permute-start | bytes 4718600 | tf_op jit(solution)/shard_map/ppermute | solution.py:1140
  715.8 40.4 %collective-permute-start.17 = (bf16[3,1024,256]{2,1,0:T(8,128)(2,1)S(1)}, bf16[3,1024,256]{2,1,0:T(8,128)(2,1)S(1)}, u32[]{:S(2)}, u32[]{:S(2)}) collective-permute-start(bf16[3,1024,256]{2,1,0:T(8,128)(2,1)S(1)} %add_convert_fusion.3.near_ref), channel_id=1, source_target_pairs={{0,4},{4,0},{8,12},{12,8},{1,5},{5,1},{9,13},{13,9},{2,6},{6,2},{1... | collective-permute-start | bytes 4718600 | tf_op jit(solution)/shard_map/ppermute | solution.py:1276
  725.8 39.6 %collective-permute-start.15 = (bf16[1024,384]{1,0:T(8,128)(2,1)}, bf16[1024,384]{1,0:T(8,128)(2,1)}, u32[]{:S(2)}, u32[]{:S(2)}) collective-permute-start(bf16[1024,384]{1,0:T(8,128)(2,1)} %fusion.23), channel_id=1, source_target_pairs={{0,16},{16,0},{1,17},{17,1},{2,18},{18,2},{3,19},{19,3},{4,20},{20... | collective-permute-start | bytes 2359304 | tf_op jit(solution)/shard_map/ppermute | solution.py:1140
  768.2 248.2 %reduce-scatter.8.cloned.1.call-start = ((), (), s32[]{:S(2)}) async-start(), calls=%async_computation.9 | async-start | bytes 1310720 | tf_op jit(solution)/shard_map/reduce_scatter | solution.py:1372
  768.8 40.0 %collective-permute-start.19 = (bf16[3,1024,256]{2,1,0:T(8,128)(2,1)}, bf16[3,1024,256]{2,1,0:T(8,128)(2,1)}, u32[]{:S(2)}, u32[]{:S(2)}) collective-permute-start(bf16[3,1024,256]{2,1,0:T(8,128)(2,1)} %bitcast.226), channel_id=1, source_target_pairs={{0,16},{16,0},{1,17},{17,1},{2,18},{18,2},{3,19},{19,3},{4,20},{20... | collective-permute-start | bytes 4718600 | tf_op jit(solution)/shard_map/ppermute | solution.py:1140
  772.8 89.6 %collective-permute-start.23 = (bf16[3,1024,256]{2,1,0:T(8,128)(2,1)S(1)}, bf16[3,1024,256]{2,1,0:T(8,128)(2,1)S(1)}, u32[]{:S(2)}, u32[]{:S(2)}) collective-permute-start(bf16[3,1024,256]{2,1,0:T(8,128)(2,1)S(1)} %add_convert_fusion.1.near_ref), channel_id=1, source_target_pairs={{0,4},{4,0},{8,12},{12,8},{1,5},{5,1},{9,13},{13,9},{2,6},{6,2},{1... | collective-permute-start | bytes 4718600 | tf_op jit(solution)/shard_map/ppermute | solution.py:1276
  780.3 87.8 %collective-permute-start.22 = (bf16[1024,512]{1,0:T(8,128)(2,1)}, bf16[1024,512]{1,0:T(8,128)(2,1)}, u32[]{:S(2)}, u32[]{:S(2)}) collective-permute-start(bf16[1024,512]{1,0:T(8,128)(2,1)} %convolution_convert_fusion), channel_id=1, source_target_pairs={{0,16},{16,0},{1,17},{17,1},{2,18},{18,2},{3,19},{19,3},{4,20},{20... | collective-permute-start | bytes 3145736 | tf_op jit(solution)/shard_map/ppermute | solution.py:1140
  807.3 129.3 %collective-permute-start.21 = (bf16[3,1024,256]{2,1,0:T(8,128)(2,1)}, bf16[3,1024,256]{2,1,0:T(8,128)(2,1)}, u32[]{:S(2)}, u32[]{:S(2)}) collective-permute-start(bf16[3,1024,256]{2,1,0:T(8,128)(2,1)} %bitcast.228), channel_id=1, source_target_pairs={{0,16},{16,0},{1,17},{17,1},{2,18},{18,2},{3,19},{19,3},{4,20},{20... | collective-permute-start | bytes 4718600 | tf_op jit(solution)/shard_map/ppermute | solution.py:1140
  862.3 92.9 %collective-permute-start.20 = (bf16[3,1024,256]{2,1,0:T(8,128)(2,1)}, bf16[3,1024,256]{2,1,0:T(8,128)(2,1)}, u32[]{:S(2)}, u32[]{:S(2)}) collective-permute-start(bf16[3,1024,256]{2,1,0:T(8,128)(2,1)} %add_convert_fusion.2.near_ref), channel_id=1, source_target_pairs={{0,4},{4,0},{8,12},{12,8},{1,5},{5,1},{9,13},{13,9},{2,6},{6,2},{1... | collective-permute-start | bytes 4718600 | tf_op jit(solution)/shard_map/ppermute | solution.py:1276
  939.2 128.2 %all-gather.12.cloned.1.call-start = ((), (), s32[]{:S(2)}) async-start(), calls=%async_computation.10 | async-start | bytes 1310720 | tf_op jit(solution)/shard_map/all_gather | solution.py:1373
  942.7 119.3 %collective-permute-start.25 = (bf16[3,1024,256]{2,1,0:T(8,128)(2,1)}, bf16[3,1024,256]{2,1,0:T(8,128)(2,1)}, u32[]{:S(2)}, u32[]{:S(2)}) collective-permute-start(bf16[3,1024,256]{2,1,0:T(8,128)(2,1)} %add_convert_fusion.near_ref), channel_id=1, source_target_pairs={{0,4},{4,0},{8,12},{12,8},{1,5},{5,1},{9,13},{13,9},{2,6},{6,2},{1... | collective-permute-start | bytes 4718600 | tf_op jit(solution)/shard_map/ppermute | solution.py:1276
  1016.4 44.3 %collective-permute-start.24 = (bf16[20,2048]{1,0:T(8,128)(2,1)S(1)}, bf16[20,2048]{1,0:T(8,128)(2,1)S(1)}, u32[]{:S(2)}, u32[]{:S(2)}) collective-permute-start(bf16[20,2048]{1,0:T(8,128)(2,1)S(1)} %fusion.44), channel_id=1, source_target_pairs={{0,16},{16,0},{1,17},{17,1},{2,18},{18,2},{3,19},{19,3},{4,20},{20... | collective-permute-start | bytes 245768 | tf_op jit(solution)/shard_map/ppermute | solution.py:1135
  (80 other events, 1527.6 us)
Sparse Core Ops, SparseCore 0:
  24.4 68.6 all-gather.7
  185.0 77.8 all-gather.9
  446.1 94.2 reduce-scatter.3
  647.1 47.4 reduce-scatter.5
  711.3 39.8 all-gather.13
  768.3 93.4 all-gather.15
  939.3 52.8 reduce-scatter.7
  1016.5 31.8 all-gather.11

commit v3 on v2

--- a/solution.py
+++ b/solution.py
@@ -155,29 +155,36 @@
     return turned.reshape(len(parts), pack // count, count * mine, HEAD)
 
 
-def carried(pairs, sems):
+def carried(axes, sources, targets, sems):
     d, count = lax.axis_index("dp"), lax.axis_size("dp")
-    copies, partners = [], []
-    for axis, source, target in pairs:
-        send, recv = sems[axis]
+    copies = []
+    for i, axis in enumerate(axes):
+        pair = (sems[2 * i], sems[2 * i + 1])
         if axis == "z":
             partner = {"ctx": jnp.bitwise_xor(lax.axis_index("ctx"), 1)}
-            copies.append(remote(source, target, (send, recv), 0, partner))
-            partners.append((partner, d >= 0))
+            copies.append(remote(sources[i], targets[i], pair, 0, partner))
             continue
         for s in range(1, count):
-            partner = {"dp": lax.rem(d + s, count)}
-            copies.append(remote(source.at[s - 1], target.at[s - 1], (send, recv), s - 1, partner))
-            partners.append((partner, d >= 0))
+            source = sources[i].at[s - 1] if axis == "x" else sources[i]
+            partner = {"dp": lax.rem(d + (s if axis == "x" else count - s), count)}
+            copies.append(remote(source, targets[i].at[s - 1], pair, s - 1, partner))
+    partners = []
+    if any(axis != "z" for axis in axes):
+        partners = [({"dp": lax.rem(d + s, count)}, d >= 0) for s in range(1, count)]
     return copies, partners
 
 
+def beside():
+    return [({"ctx": jnp.bitwise_xor(lax.axis_index("ctx"), 1)}, lax.axis_index("ctx") >= 0)]
+
+
 def carry_operands(carry):
-    dma = pltpu.SemaphoreType.DMA
+    dma, count = pltpu.SemaphoreType.DMA, lax.axis_size("dp")
     shapes, sems = [], []
     for axis, v in carry:
-        shapes.append(jax.ShapeDtypeStruct(v.shape, v.dtype))
-        sems += [dma((v.shape[0] if axis == "x" else 1,))] * 2
+        shape = (count - 1,) + v.shape if axis == "w" else v.shape
+        shapes.append(jax.ShapeDtypeStruct(shape, v.dtype))
+        sems += [dma((1 if axis == "z" else count - 1,))] * 2
     return [v for _, v in carry], shapes, sems
 
 
@@ -195,19 +202,19 @@
     near_ref, others_ref = take(2)
     targets = take(len(axes))
     gate_sum, up_sum, down_sum = take(3)
-    sems = {axis: take(2) for axis in axes}
+    sems = take(2 * len(axes))
     turn, last = pl.program_id(0), pl.num_programs(0) - 1
     wide = gate_w[0].shape[0]
 
     def transfers():
-        return carried(list(zip(axes, sources, targets)), sems)
+        return carried(axes, sources, targets, sems)
 
     if axes:
 
         @pl.when(turn == 0)
         def _():
             copies, partners = transfers()
-            signal_all(partners)
+            signal_all(partners + (beside() if "z" in axes else []))
             for copy in copies:
                 copy.start()
 
@@ -269,10 +276,11 @@
 
 
 def expert(e, hidden, upstream, chosen, router, weights, far, full, carry, ident, tile=512):
-    both_w, down_w = weights
-    blocks = len(both_w)
+    gate_w, up_w, down_w = weights
+    blocks = len(gate_w)
     pack, width = hidden.shape
     mine, fine, wide = down_w[0].shape
+    first = up_w[0].shape[0] - mine
     operands, shapes, sems = carry_operands(carry)
     hbm = pl.BlockSpec(memory_space=pl.ANY)
 
@@ -303,14 +311,14 @@
         in_specs=[token(width), token(width), token(chosen.shape[1])]
         + [pl.BlockSpec(router.shape, lambda i: (0, 0))]
         + [weight(0, wide, fine)] * blocks
-        + [weight(mine, wide, fine)] * blocks
+        + [weight(first, wide, fine)] * blocks
         + [weight(0, fine, wide)] * blocks
         + [hbm] * len(operands),
         out_specs=out_specs + [hbm] * len(shapes),
         out_shape=out_shape + shapes,
         scratch_shapes=[pltpu.VMEM((fine, width), F32)] * 3 + sems,
         compiler_params=pltpu.CompilerParams(vmem_limit_bytes=56 << 20, **remote_params),
-    )(hidden, upstream, chosen, router, *both_w, *both_w, *down_w, *operands)
+    )(hidden, upstream, chosen, router, *gate_w, *up_w, *down_w, *operands)
 
 
 def signal_all(partners):
@@ -346,11 +354,19 @@
     )
 
 
-def spread_kernel(x_ref, out_ref, local, zs, zr, ys, yr, cs, cr):
+def spread_kernel(axes, x_ref, *refs):
+    count = len(axes)
+    sources, out_ref, targets = refs[:count], refs[count], refs[count + 1 : 2 * count + 1]
+    local, zs, zr, ys, yr, cs, cr = refs[2 * count + 1 : 2 * count + 8]
+    moving, more = carried(axes, sources, targets, refs[2 * count + 8 :])
     c, n, core, side, over_core, over_side = place()
     rows, part = x_ref.shape
     left, right = {"ctx": c - 1}, {"ctx": c + 1}
-    signal_all([(left, c > 0), (right, c < n - 1), (over_core, c >= 0), (over_side, c >= 0)])
+    signal_all(
+        [(left, c > 0), (right, c < n - 1), (over_core, c >= 0), (over_side, c >= 0)] + more
+    )
+    for copy in moving:
+        copy.start()
     mine = core * 2 + side
     other = core * 2 + 1 - side
 
@@ -444,21 +460,29 @@
         for which, column in ((0, (1 - core) * 2 + side), (1, (1 - core) * 2 + 1 - side)):
             here = tile(owner, column)
             remote(here, here, (cs, cr), which * n + owner, over_core).wait_recv()
-
-
-def spread(v, ident):
+    for copy in moving:
+        copy.wait()
+
+
+def spread(v, ident, carry=()):
+    operands, shapes, sems = carry_operands(carry)
+    hbm = pl.BlockSpec(memory_space=pl.ANY)
     n, tp = lax.axis_size("ctx"), lax.axis_size("tp")
     rows, part = v.shape
     dma = pltpu.SemaphoreType.DMA
     return pl.pallas_call(
-        spread_kernel,
+        functools.partial(spread_kernel, [axis for axis, _ in carry]),
         cost_estimate=pl.CostEstimate(flops=60 * MICRO, bytes_accessed=0, transcendentals=0),
-        out_shape=jax.ShapeDtypeStruct((n * rows, tp * part), v.dtype),
-        in_specs=[pl.BlockSpec(memory_space=pl.ANY)],
-        out_specs=pl.BlockSpec(memory_space=pl.ANY),
-        scratch_shapes=[dma] + [dma((2 * n,))] * 2 + [dma((n,))] * 2 + [dma((2 * n,))] * 2,
+        out_shape=[jax.ShapeDtypeStruct((n * rows, tp * part), v.dtype)] + shapes,
+        in_specs=[hbm] * (1 + len(shapes)),
+        out_specs=[hbm] * (1 + len(shapes)),
+        scratch_shapes=[dma]
+        + [dma((2 * n,))] * 2
+        + [dma((n,))] * 2
+        + [dma((2 * n,))] * 2
+        + sems,
         compiler_params=pltpu.CompilerParams(collective_id=ident, has_side_effects=True),
-    )(v)
+    )(v, *operands)
 
 
 def join_kernel(x_ref, out_ref, local, ss, sr):
@@ -666,7 +690,7 @@
     def take(count):
         return [refs.pop(0) for _ in range(count)]
 
-    lhs_refs, own_refs, other_refs = take(kinds * mine), take(1), take(blocks - 1)
+    lhs_refs, weight_refs = take(kinds * mine), take(kinds * blocks)
     dots_ref = take(1)[0] if with_dots else None
     sources = take(len(axes))
     out_ref = take(1)[0]
@@ -675,9 +699,7 @@
     lhs, weights, core_out, core_in, keep, near, side_out, side_in, z_out, z_in = take(10)
     ls, ws, cs, cr, ys, yr, zs, zr = take(8)
     dots_in, ds, dr = take(3) if with_dots else (None, None, None)
-    moving, more = carried(
-        list(zip(axes, sources, targets)), {axis: take(2) for axis in axes}
-    )
+    moving, more = carried(axes, sources, targets, take(2 * len(axes)))
     c, n, core, side, over_core, over_side = place()
     t, tp = lax.axis_index("tp"), lax.axis_size("tp")
     rows, part = out_ref.shape
@@ -693,8 +715,7 @@
             columns = pl.ds(at * fine, fine)
             loads.append(pltpu.make_async_copy(lhs_refs[at], lhs.at[:, columns], ls.at[at]))
             for s in range(blocks):
-                source = own_refs[0] if s == 0 else other_refs[s - 1]
-                source = source.at[at]
+                source = weight_refs[k * blocks + s].at[e]
                 target = weights.at[s, columns, :] if flipped else weights.at[s, :, columns]
                 loads.append(pltpu.make_async_copy(source, target, ws.at[at * blocks + s]))
     for load in loads:
@@ -706,11 +727,7 @@
                 others.append(({"ctx": far_c, "tp": far_t}, (c != far_c) | (t != far_t)))
     else:
         others = [(over_core, c >= 0), (over_side, c >= 0), (left, c > 0), (right, c < n - 1)]
-    at = 0
-    for axis in axes:
-        count = 1 if axis == "z" else blocks - 1
-        others += [] if axis == "z" else more[at : at + count]
-        at += count
+    others += more
     signal_all(others)
     for copy in moving:
         copy.start()
@@ -904,18 +921,18 @@
         copy.wait()
 
 
-def returns(lhs, own, others, dots, flipped, ident, carry=()):
+def returns(lhs, weights, dots, flipped, ident, carry=()):
     n, tp = lax.axis_size("ctx"), lax.axis_size("tp")
     kinds, mine = len(lhs), len(lhs[0])
-    blocks = len(others) + 1
+    blocks = len(weights[0])
     pack, fine = lhs[0][0].shape
-    wide = own.shape[2 if flipped else 1]
+    wide = weights[0][0].shape[2 if flipped else 1]
     rows, part = pack // n, wide * blocks // tp
     deep = kinds * mine * fine
     dma, vmem = pltpu.SemaphoreType.DMA, pltpu.VMEM
     hbm = pl.BlockSpec(memory_space=pl.ANY)
     near = pl.BlockSpec(memory_space=pltpu.VMEM)
-    operands = [v for kind in lhs for v in kind] + [own] + list(others)
+    operands = [v for kind in lhs for v in kind] + [w for kind in weights for w in kind]
     in_specs = [hbm] * len(operands)
     out_shape = [jax.ShapeDtypeStruct((rows, part), F32)]
     extra = []
@@ -1176,40 +1193,51 @@
         return jnp.roll(v, dp_at * wide, axis=-1)
 
     gain_q, gain_k = lax.dynamic_slice_in_dim(natural(gains[1:3]), head_at, own_cols, 1)
-    heads_w = fetch(jnp.concatenate([own_heads(w) for w in (w_query, w_key, w_value)], axis=1))
-    out_w = fetch(w_out)
+    heads_w = jnp.concatenate([own_heads(w) for w in (w_query, w_key, w_value)], axis=1)
     weights = (w_gate, w_up, w_down)
-    beside = jnp.bitwise_xor(ctx_at, 2)
+    beside_at = jnp.bitwise_xor(ctx_at, 2)
 
     def experts_of(w, plane):
         return lax.dynamic_slice_in_dim(w, plane * mine, mine, 0)
 
 
-    def both(ws, plane):
-        gate, up, down = (experts_of(w, plane) for w in ws)
-        return [jnp.concatenate([gate, up]), down]
-
-    own_slices = both(weights, ctx_at)
+    own_slices = [experts_of(w, ctx_at) for w in weights]
     tokens = jnp.roll(tokens, -dp_at * wide, axis=1)
 
     inputs = tokens.astype(F32)
     scale_one = lax.rsqrt(jnp.mean(inputs * inputs, axis=1, keepdims=True) + EPS)
     hidden_one = columns((inputs * scale_one * gain_one).astype(BF16))
     hidden_one, own_slices = lax.optimization_barrier((hidden_one, own_slices))
-    own_others = [fetch(w)[1:] for w in own_slices]
-    hidden_one = spread(hidden_one, 1)
-    cotangent = jnp.roll(cotangent, -dp_at * wide, axis=1)
+    hidden_one, *got = spread(
+        hidden_one, 1, [("w", heads_w), ("w", w_out), ("w", own_slices[0])]
+    )
+
+    def listed(w, received):
+        return [w] + [received[s] for s in range(dp_count - 1)]
+
+    heads_w, out_w = listed(heads_w, got[0]), listed(w_out, got[1])
+    own_w = [listed(own_slices[0], got[2]), fetch(own_slices[1]), None]
+    if wide % part == 0:
+
+        def upstream_columns(at):
+            return lax.dynamic_slice_in_dim(
+                cotangent, lax.rem(at * part + dp_at * wide, width), part, 1
+            )
+
+    else:
+        turned_cotangent = jnp.roll(cotangent, -dp_at * wide, axis=1)
+
+        def upstream_columns(at):
+            return lax.dynamic_slice_in_dim(turned_cotangent, at * part, part, 1)
+
     chosen = jnp.any(
         routes[:, :, None] == jnp.arange(experts, dtype=jnp.int32)[None, None, :], axis=1
     )
-    upstream_all = jnp.concatenate(
-        [
-            lax.dynamic_slice_in_dim(cotangent, tp_at * part, part, 1),
-            jnp.pad(chosen.astype(BF16), ((0, 0), (0, HEAD - experts))),
-        ],
-        axis=1,
-    )
-    upstream_all = lax.all_gather(upstream_all, "ctx", axis=0, tiled=True)
+    upstream_all = jnp.concatenate([upstream_columns(tp_at), chosen.astype(BF16).T])
+    upstream_all = lax.all_gather(upstream_all, "ctx", axis=0, tiled=False)
+    chosen_all = upstream_all[:, rows:].transpose(0, 2, 1).reshape(-1, experts).astype(F32)
+    hidden_one, upstream_all = lax.optimization_barrier((hidden_one, upstream_all))
+    upstream_all = lax.all_gather(upstream_all[:, :rows].reshape(-1, part), "tp", axis=1, tiled=True)
     raw = sum(dot(block(hidden_one, s), w) for s, w in enumerate(heads_w))
     q_raw, k_raw = raw[:, :own_cols], raw[:, own_cols : 2 * own_cols]
     values = raw[:, 2 * own_cols :].astype(BF16)
@@ -1217,7 +1245,6 @@
     squares = share(
         jnp.stack([jnp.sum(q_raw * q_raw, axis=1), jnp.sum(k_raw * k_raw, axis=1)]), True, 5
     )
-    squares, out_w = lax.optimization_barrier((squares, out_w))
     q_scale, k_scale = lax.rsqrt(squares / width + EPS)[:, :, None]
     q_hat, k_hat = q_raw * q_scale, k_raw * k_scale
     cosine, sine = rotation(lengths[0], 0, pack)
@@ -1232,24 +1259,21 @@
     q_all, k_all = by_head(turn(q_hat * gain_q, sine)), by_head(turn(k_hat * gain_k, sine))
     v_all = by_head(values)
     attended_all, log = attend(lengths, q_all, k_all, v_all)
-    attended_all, own_others[0] = lax.optimization_barrier((attended_all, own_others[0]))
     attended = to_rows((attended_all,))[0].reshape(rows, local)
     branch = jnp.concatenate([dot(attended, w).astype(BF16) for w in out_w], axis=1)
-    branch, upstream_all = lax.optimization_barrier((branch, upstream_all))
-    chosen_all = upstream_all[:, part : part + experts].astype(F32)
-    upstream_all = lax.all_gather(upstream_all[:, :part], "tp", axis=1, tiled=True)
+    branch, own_w[1] = lax.optimization_barrier((branch, own_w[1]))
     branch = collect(branch, 1, 2)
-    branch, late = lax.optimization_barrier((branch, weights))
-    far_slices = both(late, beside)
-    far_others = [fetch(w)[1:] for w in far_slices]
     inputs_c = columns(inputs)
     mixed = inputs_c + branch
     square = lax.psum(jnp.sum(mixed * mixed, axis=1), "tp")
     scale_two = lax.rsqrt(square / width + EPS)[:, None]
     normed_two = mixed * scale_two
     hidden_mine = (normed_two * gain_two).astype(BF16)
-    hidden_mine, own_others[1] = lax.optimization_barrier((hidden_mine, own_others[1]))
-    hidden_two = spread(hidden_mine, 3)
+    hidden_two, got = spread(hidden_mine, 3, [("w", own_slices[2])])
+    own_w[2] = listed(own_slices[2], got)
+    hidden_two, late = lax.optimization_barrier((hidden_two, weights))
+    far_slices = [experts_of(w, beside_at) for w in late]
+    far_slices = [jnp.concatenate(far_slices[:2]), far_slices[2]]
 
     tie = lax.optimization_barrier
     grads, sums, there = {}, {}, {}
@@ -1279,8 +1303,6 @@
         there[e], after = tie((there[e], after))
         return after
 
-    own_w = [[w] + o for w, o in zip(own_slices, own_others)]
-    far_w = [[w] + o for w, o in zip(far_slices, far_others)]
     parts = []
     for e in range(mine):
         parts.append(run(e))
@@ -1290,23 +1312,25 @@
         if e > 2:
             hidden_two = end_z(e - 3, hidden_two)
         start_x(e)
-    mixture = mixture_parts([p[0] for p in parts], own_w[1], tp_count)
+    mixture = mixture_parts([p[0] for p in parts], own_w[2], tp_count)
     mixture, hidden_two = tie((mixture, hidden_two))
     mixture = lax.psum_scatter(mixture, "tp", scatter_dimension=0, tiled=False)
     dots = jnp.concatenate([p[3] for p in parts], axis=1).T
     dots, hidden_two = tie((dots, hidden_two))
+    far_both = fetch(far_slices[0])
     expert_in, dots = returns(
         [[p[1] for p in parts], [p[2] for p in parts]],
-        own_w[0][0],
-        own_w[0][1:],
+        own_w[:2],
         dots,
         False,
         4,
     )
+    far_both, expert_in, late_down = tie((far_both, expert_in, far_slices[1]))
+    far_down = fetch(late_down)
     for e in range(1, mine - 1):
         expert_in = end_z(e, expert_in)
-    expert_in = end_x(mine - 1, expert_in)
-    start_z(mine - 1)
+    expert_in, mixture = tie((expert_in, mixture))
+    mixture = lax.psum_scatter(mixture, "ctx", scatter_dimension=0, tiled=True)
 
     dots = dots.reshape(experts, rows).T
     hidden_rows = lax.dynamic_slice_in_dim(hidden_two, ctx_at * rows, rows, 0)
@@ -1319,22 +1343,27 @@
     gain_two_grad = jnp.sum(d_hidden_two * normed_two, axis=0)
     pull_two = d_hidden_two * gain_two
     mean_two = lax.psum(jnp.sum(pull_two * mixed, axis=1), "tp")[:, None] / width
+    mean_two = end_x(mine - 1, mean_two)
+    sums[mine - 1], mean_two = tie((sums[mine - 1], mean_two))
+    start_z(mine - 1)
     d_mixed = (
-        columns(cotangent).astype(F32) + scale_two * pull_two - mixed * scale_two**3 * mean_two
+        upstream_columns(column_at).astype(F32) + scale_two * pull_two - mixed * scale_two**3 * mean_two
     )
 
     d_branch = join(d_mixed.astype(BF16), 7)
     d_branch = end_z(mine - 1, d_branch)
-    hidden_two, d_branch = tie((hidden_two, d_branch))
+    hidden_two, d_branch, far_down, mixture = tie((hidden_two, d_branch, far_down, mixture))
+    output = lax.all_gather(mixed + mixture.astype(F32), "tp", axis=0, tiled=False)
+    far_w = [far_both, far_both, far_down]
     d_attended = sum(dot_t(block(d_branch, s), w) for s, w in enumerate(out_w)).astype(BF16)
     out_grad = swap([t_dot(block(d_branch, s), attended).astype(BF16) for s in range(dp_count)])
     out_mine = t_dot(block(d_branch, 0), attended)
     d_all = to_heads((d_attended,), heads)[0]
     run(mine)
     start_x(mine)
-    mixture, grads[mine][0] = tie((mixture, grads[mine][0]))
-    mixture = lax.psum_scatter(mixture, "ctx", scatter_dimension=0, tiled=True)
-    d_all, grads[mine][0] = tie((d_all, grads[mine][0]))
+    d_all, grads[mine][0], out_grad, output = tie((d_all, grads[mine][0], out_grad, output))
+    out_grad = add([out_mine], out_grad)
+    out_grad = lax.psum_scatter(out_grad, "ctx", scatter_dimension=0, tiled=True)
     dq_all, dk_all, dv_all = attend_back(lengths, q_all, k_all, v_all, d_all, log)
     def by_token(v):
         return v.transpose(1, 0, 2).reshape(pack, own_cols)
@@ -1350,51 +1379,52 @@
     d_k_raw = (k_scale * k_pull - k_raw * k_scale**3 * k_mean).astype(BF16)
     d_raw = jnp.concatenate([d_q_raw, d_k_raw, by_token(dv_all)], axis=1)
     heads_mine = t_dot(block(hidden_one, 0), d_raw)
-    heads_grads = swap([t_dot(block(hidden_one, s), d_raw).astype(BF16) for s in range(dp_count)])
-    d_raw, hidden_two = tie((d_raw, hidden_two))
+    heads_grads = [t_dot(block(hidden_one, s), d_raw).astype(BF16) for s in range(dp_count)]
+    heads_mine, heads_grads, d_raw, hidden_two, out_grad = tie(
+        (heads_mine, heads_grads, d_raw, hidden_two, out_grad)
+    )
+    out_grad = lax.all_gather(out_grad, "ctx", axis=0, tiled=True)
+    held = []
+
+    def put(e):
+        nonlocal held
+        plane = ctx_at if e < mine else beside_at
+        at = plane * mine + e % mine
+        other = jnp.bitwise_xor(plane, 1) * mine + e % mine
+        held = place_grads(
+            jnp.stack([at, other]).astype(jnp.int32), sums[e], there[e], experts, held
+        )
+
     for e in range(mine + 1, 2 * mine):
         run(e)
-        hidden_two, d_raw = end_x(e - 1, (hidden_two, d_raw, grads[e][1]))[:2]
+        if e > mine + 1:
+            for i in range(2 * (e - mine - 2), 2 * (e - mine - 1)):
+                there[i], grads[e] = tie((there[i], grads[e]))
+                put(i)
+        step = (hidden_two, d_raw, grads[e], held)
+        if e > mine + 1:
+            step = end_z(e - 2, step)
+        step = end_x(e - 1, step)
+        if e == mine + 1:
+            out_grad, step = tie((out_grad, step))
+        sums[e - 1], step = tie((sums[e - 1], step))
+        hidden_two, d_raw, grads[e], held = step
         start_z(e - 1)
-        if e > mine + 1:
-            hidden_two, d_raw = end_z(e - 2, (hidden_two, d_raw))
-        start_x(e)
-        if e == mine + 1:
-            mixture, d_raw = tie((mixture, d_raw))
-            output = lax.all_gather(mixed + mixture.astype(F32), "tp", axis=0, tiled=False)
-        if e == mine + 2:
-            heads_grads, output, d_raw = tie((heads_grads, output, d_raw))
-            heads_grads = add([heads_mine], heads_grads)
-            heads_grads = lax.all_gather(heads_grads, "ctx", axis=0, tiled=False)
-        if e == mine + 3:
-            out_grad, heads_grads, d_raw = tie((out_grad, heads_grads, d_raw))
-            out_grad = add([out_mine], out_grad)
-            out_grad = lax.psum_scatter(out_grad, "ctx", scatter_dimension=0, tiled=True)
-            out_grad = lax.all_gather(out_grad, "ctx", axis=0, tiled=True)
-    d_raw, far = tie((d_raw, grads[2 * mine - 1][0]))
+        if e < 2 * mine - 1:
+            start_x(e)
+    heads_grads, grads[2 * mine - 1] = tie((heads_grads, grads[2 * mine - 1]))
+    start_x(2 * mine - 1)
+    heads_grads = swap(heads_grads)
     (d_hidden,) = returns(
         [[d_raw]],
-        heads_w[0][None],
-        [w[None] for w in heads_w[1:]],
+        [[w[None] for w in heads_w]],
         None,
         False,
         8,
     )
     d_hidden = end_z(2 * mine - 2, end_x(2 * mine - 1, d_hidden))
-    start_z(2 * mine - 1)
+    heads_grads, out_grad, d_hidden = tie((heads_grads, out_grad, d_hidden))
     gain_one_grad = jnp.sum(d_hidden * inputs_c * scale_one, axis=0)
-    pull_one = d_hidden * columns(gain_one)
-    mean_one = lax.psum(jnp.sum(pull_one * inputs_c, axis=1), "tp")[:, None] / width
-    d_inputs = d_mixed + scale_one * pull_one - inputs_c * scale_one**3 * mean_one
-
-    def whole(every):
-        every = [every[(p % 2) * 2 + p // 2] for p in range(tp_count)]
-        return natural(jnp.concatenate(every, axis=1))
-
-    output = whole(output)
-    d_inputs = join(d_inputs, 10)
-    gain_one_grad, d_inputs = tie((gain_one_grad, d_inputs))
-    d_inputs = natural(d_inputs)
     heads_gains = lax.dynamic_update_slice_in_dim(
         jnp.zeros((2, local), F32),
         jnp.stack([jnp.sum(d_q_normed * q_hat, axis=0), jnp.sum(d_k_normed * k_hat, axis=0)]),
@@ -1407,6 +1437,23 @@
     small_grads = jnp.pad(small_grads, ((0, -small_grads.shape[0] % 8), (0, 0)))
     small_grads = share(small_grads, False, 9)
 
+    d_hidden, small_grads, heads_grads, sums[2 * mine - 1] = tie(
+        (d_hidden, small_grads, heads_grads, sums[2 * mine - 1])
+    )
+    start_z(2 * mine - 1)
+    heads_grads = add([heads_mine], heads_grads)
+    heads_grads = lax.all_gather(heads_grads, "ctx", axis=0, tiled=False)
+    pull_one = d_hidden * columns(gain_one)
+    mean_one = lax.psum(jnp.sum(pull_one * inputs_c, axis=1), "tp")[:, None] / width
+    d_inputs = d_mixed + scale_one * pull_one - inputs_c * scale_one**3 * mean_one
+
+    def whole(every):
+        every = [every[(p % 2) * 2 + p // 2] for p in range(tp_count)]
+        return natural(jnp.concatenate(every, axis=1))
+
+    output = whole(output)
+    d_inputs = join(d_inputs, 10)
+    d_inputs = natural(d_inputs)
     turned = [small_grads[(p % 2) * 2 + p // 2, : 2 + experts] for p in range(tp_count)]
     heads_gains = small_grads[:, 2 + experts : 4 + experts].transpose(1, 0, 2).reshape(2, width)
     small_grads = jnp.concatenate([natural(jnp.concatenate(turned, axis=1)), heads_gains])
@@ -1419,16 +1466,10 @@
         v = heads_grads[:, :, i * own_cols : (i + 1) * own_cols].astype(F32)
         return v.transpose(1, 0, 2).reshape(wide, local)
 
-    held = []
-    for e in range(2 * mine - 1):
+    for e in range(mine, 2 * mine - 1):
         there[e], d_hidden = tie((there[e], d_hidden))
-    for e in range(2 * mine):
-        plane = ctx_at if e < mine else beside
-        at = plane * mine + e % mine
-        other = jnp.bitwise_xor(plane, 1) * mine + e % mine
-        held = place_grads(
-            jnp.stack([at, other]).astype(jnp.int32), sums[e], there[e], experts, held
-        )
+    for e in range(mine, 2 * mine):
+        put(e)
     return (
         output,
         d_inputs,

time: 1090 us -> 1040 us (0.954)
  blocking collectives: 40.5 us -> 20.2 us
  waiting for transfers between devices: 88.6 us -> 76.3 us
    ppermute x8, waiting for transfers between devices: 50.6 us -> 20 us  [start_z(): lax.ppermute(sums[e], 'ctx', [(i, i ^ 1) for i in range(ctx_count)])]
    all_to_all x1 -> x0, blocking collectives: 20.4 us -> none  [to_rows(): got = lax.all_to_all(sent, 'ctx', 0, 0, tiled=True)]
    ppermute x10, waiting for transfers between devices: 26.5 us -> 42.4 us  [swap(): lax.ppermute(blocks[s], 'dp', [(i, (i + s) % dp_count) for i in range(dp_...]
    ppermute x8, starting transfers between devices: 33.1 us -> 19.6 us  [start_z(): lax.ppermute(sums[e], 'ctx', [(i, i ^ 1) for i in range(ctx_count)])]
    all_to_all x0 -> x1, waiting for transfers between devices: none -> 12.2 us  [to_rows(): got = lax.all_to_all(sent, 'ctx', 0, 0, tiled=True)]
    pallas_call x3, Pallas kernels: 36.6 us -> 48.5 us  [share(): pl.pallas_call(functools.partial(share_kernel, over_tp), cost_estimate=pl...]
    ppermute x7 -> x4, waiting for transfers between devices: 11.3 us -> 0.01 us  [fetch(): lax.ppermute(v, 'dp', [((i + s) % dp_count, i) for i in range(dp_count)])]
    pallas_call x2, Pallas kernels: 160 us -> 149 us  [spread(): pl.pallas_call(functools.partial(spread_kernel, [axis for axis, _ in carr...]
  transfers between devices with their start and end apart: 35 -> 33, of which waited for: 6 -> 9; matrix products, arithmetic and copies ran while one was open for 13% -> 13% of each run, Pallas kernels for 63% -> 62%
where the time goes in v3:
time: 1040 us; the launch traced here: 1030 us
  Pallas kernels  691 us (66%)
  waiting for transfers between devices  76.3 us (7%)
  other arithmetic  75.6 us (7%)
  local copies, waits for them, and re-layouts  60.2 us (6%)
  starting transfers between devices  53.3 us (5%)
  matrix products  35.6 us (3%)
  blocking collectives  20.2 us (2%)
  between operations  15.6 us (2%)
    pallas_call x8, Pallas kernels, expert(): pl.pallas_call(functools.partial(expert_kernel, blocks, e, far, mine, ful...  198 us
    pallas_call x2, Pallas kernels, returns(): pl.pallas_call(functools.partial(returns_kernel, kinds, mine, blocks, fli...  158 us
    pallas_call x2, Pallas kernels, spread(): pl.pallas_call(functools.partial(spread_kernel, [axis for axis, _ in carr...  149 us
    pallas_call x2, Pallas kernels, join(): pl.pallas_call(join_kernel, cost_estimate=pl.CostEstimate(flops=25 * MICR...  51.8 us
    pallas_call x3, Pallas kernels, share(): pl.pallas_call(functools.partial(share_kernel, over_tp), cost_estimate=pl...  48.5 us
    ppermute x10, waiting for transfers between devices, swap(): lax.ppermute(blocks[s], 'dp', [(i, (i + s) % dp_count) for i in range(dp_...  42.4 us
    pallas_call x8, Pallas kernels, place_grads(): pl.pallas_call(place_kernel, cost_estimate=pl.CostEstimate(flops=4 * MICR...  38.8 us
  transfers between devices with their start and end apart: 33, of which 9 were waited for; matrix products, arithmetic and copies ran while one was open for 13% of the time, Pallas kernels for 62%

profile of v3, /device:TPU:0, one launch (start us, length us, event | category | flops | bytes accessed | tf_op | source)
XLA Modules:
  0.0 1028.2 jit_solution(83755408335342051)
XLA Ops:
  32.5 87.1 %shard_map.263 = (bf16[2048,2048]{1,0:T(8,128)(2,1)}, bf16[1,1024,384]{2,1,0:T(8,128)(2,1)}, bf16[1,512,1024]{2,1,0:T(8,128)(2,1)}, bf16[1,4,1024,256]{3,2,1,0:T(8,128)(2,1)}) custom-call(bf16[512,512]{1,0:T(8,128)(2,1)} %multiply_convert_fusion.1.x_ref, bf16[1024,384]{1,0:T(8,128)(2,1)} %get-tuple-element.532.refs_0_, bf16[512,1024]{1,0:T(8,128)(2,1)} %refs_1_.1, ...), custom_call_target="tpu_custom_call" | custom-call | flops 4026531840 | tf_op jit(solution)/shard_map/pallas_call | solution.py:473
  137.2 9.8 shard_map.264
  150.6 7.1 shard_map.265
  167.6 12.2 %all-to-all-done = bf16[4,1,1,512,128]{3,4,2,1,0:T(8,128)(2,1)S(1)} async-done(((bf16[4,1,1,512,128]{3,4,2,1,0:T(8,128)(2,1)}), bf16[4,1,1,512,128]{3,4,2,1,0:T(8,128)(2,1)S(1)}, u32[]{:S(2)}, u32[]{:S(2)}) %all-to-all-start) | async-done | bytes 524320 | tf_op jit(solution)/shard_map/all_to_all | solution.py:153
  184.1 17.2 %shard_map.266 = f32[512,512]{1,0:T(8,128)S(1)} custom-call(bf16[512,2048]{1,0:T(8,128)(2,1)S(1)} %pad_maximum_fusion.1.x_ref), custom_call_target="tpu_custom_call" | custom-call | flops 1140850688 | tf_op jit(solution)/shard_map/pallas_call | solution.py:666
  209.5 61.5 %shard_map.267 = (bf16[2048,2048]{1,0:T(8,128)(2,1)}, bf16[1,4,256,1024]{3,2,1,0:T(8,128)(2,1)}) custom-call(bf16[512,512]{1,0:T(8,128)(2,1)} %multiply_convert_fusion.x_ref, bf16[4,256,1024]{2,1,0:T(8,128)(2,1)} %constant_dynamic-slice_fusion.11.refs_0_.refs_8_.refs_4_), custom_call_target="tpu_custom_call" | custom-call | flops 4026531840 | tf_op jit(solution)/shard_map/pallas_call | solution.py:473
  271.0 24.9 %shard_map.268 = (bf16[2048,256]{1,0:T(8,128)(2,1)}, bf16[2048,256]{1,0:T(8,128)(2,1)}, bf16[2048,256]{1,0:T(8,128)(2,1)}, f32[2048,1]{1,0:T(8,128)}, bf16[3,102...) custom-call(bf16[2048,2048]{1,0:T(8,128)(2,1)} %get-tuple-element.365.refs_0_, ...), custom_call_target="tpu_custom_call" | custom-call | flops 1811939328 | tf_op jit(solution)/shard_map/pallas_call | solution.py:307
  296.8 24.9 %shard_map.269 = (bf16[2048,256]{1,0:T(8,128)(2,1)}, bf16[2048,256]{1,0:T(8,128)(2,1)}, bf16[2048,256]{1,0:T(8,128)(2,1)}, f32[2048,1]{1,0:T(8,128)}, bf16[3,102...) custom-call(bf16[2048,2048]{1,0:T(8,128)(2,1)} %get-tuple-element.365.refs_0_, ...), custom_call_target="tpu_custom_call" | custom-call | flops 1811939328 | tf_op jit(solution)/shard_map/pallas_call | solution.py:307
  323.0 10.4 %collective-permute-done.2 = bf16[3,1024,256]{2,1,0:T(8,128)(2,1)S(1)} collective-permute-done((bf16[3,1024,256]{2,1,0:T(8,128)(2,1)}, bf16[3,1024,256]{2,1,0:T(8,128)(2,1)S(1)}, u32[]{:S(2)}, u32[]{:S(2)}) %collective-permute-start.2) | collective-permute-done | bytes 1572896 | tf_op jit(solution)/shard_map/ppermute | solution.py:1157
  333.4 25.3 %shard_map.270 = (bf16[2048,256]{1,0:T(8,128)(2,1)}, bf16[2048,256]{1,0:T(8,128)(2,1)}, bf16[2048,256]{1,0:T(8,128)(2,1)}, f32[2048,1]{1,0:T(8,128)}, bf16[3,102...) custom-call(bf16[2048,2048]{1,0:T(8,128)(2,1)} %get-tuple-element.365.refs_0_, ...), custom_call_target="tpu_custom_call" | custom-call | flops 1811939328 | tf_op jit(solution)/shard_map/pallas_call | solution.py:307
  360.0 7.1 collective-permute-done.3
  367.1 25.4 %shard_map.271 = (bf16[2048,256]{1,0:T(8,128)(2,1)}, bf16[2048,256]{1,0:T(8,128)(2,1)}, bf16[2048,256]{1,0:T(8,128)(2,1)}, f32[2048,1]{1,0:T(8,128)}, bf16[3,102...) custom-call(bf16[2048,2048]{1,0:T(8,128)(2,1)} %get-tuple-element.365.refs_0_, ...), custom_call_target="tpu_custom_call" | custom-call | flops 1811939328 | tf_op jit(solution)/shard_map/pallas_call | solution.py:307
  393.9 13.1 %shard_map.272 = bf16[4,2048,512]{2,1,0:T(8,128)(2,1)} custom-call(bf16[2048,256]{1,0:T(8,128)(2,1)S(1)} %copy-done.15, bf16[2048,256]{1,0:T(8,128)(2,1)S(1)} %copy-done.16, bf16[2048,256]{1,0:T(8,128)(2,1)S(1)} %copy-done.17, bf16[2048,256]{1,0:T(8,128)(2,1)S(1)} %copy-done.18, bf16[4,256,1024]{2,1,0:T(8,128)(2,1)} %constant_dynamic-slice_fusion.11.refs_0_.refs_8_.refs_4_, ...), custom_call_target="tpu_custom_call" | custom-call | flops 1006632960 | tf_op jit(solution)/shard_map/pallas_call | solution.py:996
  430.1 95.9 %shard_map.273 = (f32[512,512]{1,0:T(8,128)}, f32[4,4,512]{2,1,0:T(4,128)}) custom-call(bf16[2048,256]{1,0:T(8,128)(2,1)} %get-tuple-element.270.refs_0_, bf16[2048,256]{1,0:T(8,128)(2,1)} %get-tuple-element.271.refs_1_, bf16[2048,256]{1,0:T(8,128)(2,1)} %get-tuple-element.272.refs_2_, bf16[2048,256]{1,0:T(8,128)(2,1)} %get-tuple-element.273.refs_3_, ...), custom_call_target="tpu_custom_call" | custom-call | flops 4362076160 | tf_op jit(solution)/shard_map/pallas_call | solution.py:946
  534.5 6.0 psum.22
  540.5 23.4 %collective-permute-done.6 = bf16[3,1024,256]{2,1,0:T(8,128)(2,1)} collective-permute-done((bf16[3,1024,256]{2,1,0:T(8,128)(2,1)}, bf16[3,1024,256]{2,1,0:T(8,128)(2,1)}, u32[]{:S(2)}, u32[]{:S(2)}) %collective-permute-start.6) | collective-permute-done | bytes 1572896 | tf_op jit(solution)/shard_map/ppermute | solution.py:1157
  567.3 9.5 collective-permute-start.10
  579.9 18.3 %shard_map.274 = bf16[512,2048]{1,0:T(8,128)(2,1)} custom-call(bf16[512,512]{1,0:T(8,128)(2,1)} %get-tuple-element.505.x_ref), custom_call_target="tpu_custom_call" | custom-call | flops 1677721600 | tf_op jit(solution)/shard_map/pallas_call | solution.py:516
  598.2 9.8 collective-permute-done.10.far_ref
  621.0 6.7 all-to-all-start.1
  627.6 24.3 %shard_map.275 = (bf16[3,1024,256]{2,1,0:T(8,128)(2,1)}, bf16[1,3,1024,256]{3,2,1,0:T(8,128)(2,1)}) custom-call(bf16[2048,2048]{1,0:T(8,128)(2,1)} %get-tuple-element.365.refs_0_, bf16[2048,2048]{1,0:T(8,128)(2,1)} %all-gather.9.cloned.1.call-done.refs_1_, f32[2048,16]{1,0:T(8,128)} %bitcast.199, bf16[16,2048]{1,0:T(8,128)(2,1)} %pad_maximum_fusion.8.refs_3_, ...), custom_call_target="tpu_custom_call" | custom-call | flops 1811939328 | tf_op jit(solution)/shard_map/pallas_call | solution.py:307
  661.9 10.2 shard_map.276
  676.9 10.2 shard_map.277
  697.7 24.4 %shard_map.278 = (bf16[3,1024,256]{2,1,0:T(8,128)(2,1)}, bf16[1,3,1024,256]{3,2,1,0:T(8,128)(2,1)}) custom-call(bf16[2048,2048]{1,0:T(8,128)(2,1)} %get-tuple-element.365.refs_0_, bf16[2048,2048]{1,0:T(8,128)(2,1)} %all-gather.9.cloned.1.call-done.refs_1_, f32[2048,16]{1,0:T(8,128)} %bitcast.200, bf16[16,2048]{1,0:T(8,128)(2,1)} %pad_maximum_fusion.8.refs_3_, ...), custom_call_target="tpu_custom_call" | custom-call | flops 1811939328 | tf_op jit(solution)/shard_map/pallas_call | solution.py:307
  729.4 24.3 %shard_map.279 = (bf16[3,1024,256]{2,1,0:T(8,128)(2,1)}, bf16[1,3,1024,256]{3,2,1,0:T(8,128)(2,1)}) custom-call(bf16[2048,2048]{1,0:T(8,128)(2,1)} %get-tuple-element.365.refs_0_, bf16[2048,2048]{1,0:T(8,128)(2,1)} %all-gather.9.cloned.1.call-done.refs_1_, f32[2048,16]{1,0:T(8,128)} %bitcast.201, bf16[16,2048]{1,0:T(8,128)(2,1)} %pad_maximum_fusion.8.refs_3_, ...), custom_call_target="tpu_custom_call" | custom-call | flops 1811939328 | tf_op jit(solution)/shard_map/pallas_call | solution.py:307
  767.9 24.2 %shard_map.282 = (bf16[3,1024,256]{2,1,0:T(8,128)(2,1)}, bf16[1,3,1024,256]{3,2,1,0:T(8,128)(2,1)}) custom-call(bf16[2048,2048]{1,0:T(8,128)(2,1)} %get-tuple-element.365.refs_0_, bf16[2048,2048]{1,0:T(8,128)(2,1)} %all-gather.9.cloned.1.call-done.refs_1_, f32[2048,16]{1,0:T(8,128)} %bitcast.202, bf16[16,2048]{1,0:T(8,128)(2,1)} %pad_maximum_fusion.8.refs_3_, ...), custom_call_target="tpu_custom_call" | custom-call | flops 1811939328 | tf_op jit(solution)/shard_map/pallas_call | solution.py:307
  814.2 62.4 %shard_map.285 = f32[512,512]{1,0:T(8,128)} custom-call(bf16[2048,384]{1,0:T(8,128)(2,1)} %pad_maximum_fusion.2.refs_0_, bf16[1,1024,384]{2,1,0:T(8,128)(2,1)} %get-tuple-element.531.refs_1_, bf16[1,1024,384]{2,1,0:T(8,128)(2,1)} %get-tuple-element.230.refs_2_), custom_call_target="tpu_custom_call" | custom-call | flops 4362076160 | tf_op jit(solution)/shard_map/pallas_call | solution.py:946
  878.5 28.5 %shard_map.286 = f32[4,24,512]{2,1,0:T(8,128)S(1)} custom-call(f32[24,512]{1,0:T(8,128)S(1)} %select_maximum_fusion.x_ref), custom_call_target="tpu_custom_call" | custom-call | flops 536870912 | tf_op jit(solution)/shard_map/pallas_call | solution.py:1099
  911.1 6.4 fusion.4
  927.1 8.4 psum.23
  938.3 33.4 %shard_map.287 = f32[512,2048]{1,0:T(8,128)} custom-call(f32[512,512]{1,0:T(8,128)} %multiply_subtract_fusion.x_ref), custom_call_target="tpu_custom_call" | custom-call | flops 1677721600 | tf_op jit(solution)/shard_map/pallas_call | solution.py:516
  998.7 9.8 collective-permute-done.22.far_ref
  (324 shorter events, 250.3 us)
Async XLA Ops:
  7.2 112.5 %all-gather.13.cloned.1.call-start = ((), (), s32[]{:S(2)}) async-start(), calls=%async_computation.10 | async-start | bytes 2703360 | tf_op jit(solution)/shard_map/all_gather | solution.py:1237
  10.1 260.9 %all-gather.9.cloned.1.call-start = ((), (), s32[]{:S(2)}) async-start(), calls=%async_computation.5 | async-start | bytes 10485760 | tf_op jit(solution)/shard_map/all_gather | solution.py:1240
  126.9 57.2 %collective-permute-start.1 = (bf16[4,1024,256]{2,1,0:T(8,128)(2,1)S(1)}, bf16[4,1024,256]{2,1,0:T(8,128)(2,1)}, u32[]{:S(2)}, u32[]{:S(2)}) collective-permute-start(bf16[4,1024,256]{2,1,0:T(8,128)(2,1)S(1)} %get-tuple-element.240.refs_6_.refs_10_), channel_id=1, source_target_pairs={{16,0},{0,16},{17,1},{1,17},{18,2},{2,18},{19,3},{3,19},{20,4},{4,... | collective-permute-start | bytes 6291464 | tf_op jit(solution)/shard_map/ppermute | solution.py:1143
  159.7 20.1 %all-to-all-start = ((bf16[4,1,1,512,128]{3,4,2,1,0:T(8,128)(2,1)}), bf16[4,1,1,512,128]{3,4,2,1,0:T(8,128)(2,1)S(1)}, u32[]{:S(2)}, u32[]{:S(2)}) async-start(bf16[4,1,1,512,128]{3,4,2,1,0:T(8,128)(2,1)} %copy.95), calls=%async_computation | async-start | bytes 1048576 | tf_op jit(solution)/shard_map/all_to_all | solution.py:153
  164.6 361.5 %reduce-scatter.4.cloned.1.call-start = ((), (), s32[]{:S(2)}) async-start(), calls=%async_computation.6 | async-start | bytes 10485760 | tf_op jit(solution)/shard_map/reduce_scatter | solution.py:1317
  295.9 37.5 %collective-permute-start.2 = (bf16[3,1024,256]{2,1,0:T(8,128)(2,1)}, bf16[3,1024,256]{2,1,0:T(8,128)(2,1)S(1)}, u32[]{:S(2)}, u32[]{:S(2)}) collective-permute-start(bf16[3,1024,256]{2,1,0:T(8,128)(2,1)} %bitcast.267), channel_id=1, source_target_pairs={{0,16},{16,0},{1,17},{17,1},{2,18},{18,2},{3,19},{19,3},{4,20},{20... | collective-permute-start | bytes 4718600 | tf_op jit(solution)/shard_map/ppermute | solution.py:1157
  321.7 45.5 %collective-permute-start.3 = (bf16[3,1024,256]{2,1,0:T(8,128)(2,1)}, bf16[3,1024,256]{2,1,0:T(8,128)(2,1)S(1)}, u32[]{:S(2)}, u32[]{:S(2)}) collective-permute-start(bf16[3,1024,256]{2,1,0:T(8,128)(2,1)} %bitcast.266), channel_id=1, source_target_pairs={{0,16},{16,0},{1,17},{17,1},{2,18},{18,2},{3,19},{19,3},{4,20},{20... | collective-permute-start | bytes 4718600 | tf_op jit(solution)/shard_map/ppermute | solution.py:1157
  358.7 48.3 %collective-permute-start.5 = (bf16[3,1024,256]{2,1,0:T(8,128)(2,1)}, bf16[3,1024,256]{2,1,0:T(8,128)(2,1)}, u32[]{:S(2)}, u32[]{:S(2)}) collective-permute-start(bf16[3,1024,256]{2,1,0:T(8,128)(2,1)} %bitcast.265), channel_id=1, source_target_pairs={{0,16},{16,0},{1,17},{17,1},{2,18},{18,2},{3,19},{19,3},{4,20},{20... | collective-permute-start | bytes 4718600 | tf_op jit(solution)/shard_map/ppermute | solution.py:1157
  359.9 47.0 %collective-permute-start.4 = (bf16[3,1024,256]{2,1,0:T(8,128)(2,1)S(1)}, bf16[3,1024,256]{2,1,0:T(8,128)(2,1)S(1)}, u32[]{:S(2)}, u32[]{:S(2)}) collective-permute-start(bf16[3,1024,256]{2,1,0:T(8,128)(2,1)S(1)} %add_convert_fusion.7.near_ref), channel_id=1, source_target_pairs={{0,4},{4,0},{8,12},{12,8},{1,5},{5,1},{9,13},{13,9},{2,6},{6,2},{1... | collective-permute-start | bytes 4718600 | tf_op jit(solution)/shard_map/ppermute | solution.py:1300
  408.1 199.9 %reduce-scatter.6.cloned.1.call-start = ((), (), s32[]{:S(2)}) async-start(), calls=%async_computation.7 | async-start | bytes 2621440 | tf_op jit(solution)/shard_map/reduce_scatter | solution.py:1333
  414.4 111.6 %collective-permute-start.9 = (bf16[8,1024,256]{2,1,0:T(8,128)(2,1)}, bf16[8,1024,256]{2,1,0:T(8,128)(2,1)}, u32[]{:S(2)}, u32[]{:S(2)}) collective-permute-start(bf16[8,1024,256]{2,1,0:T(8,128)(2,1)} %pad_maximum_fusion.refs_4_.refs_6_), channel_id=1, source_target_pairs={{16,0},{0,16},{17,1},{1,17},{18,2},{2,18},{19,3},{3,19},{20,4},{4,... | collective-permute-start | bytes 12582920 | tf_op jit(solution)/shard_map/ppermute | solution.py:1143
  415.7 110.4 %collective-permute-start.8 = (bf16[3,1024,256]{2,1,0:T(8,128)(2,1)S(1)}, bf16[3,1024,256]{2,1,0:T(8,128)(2,1)}, u32[]{:S(2)}, u32[]{:S(2)}) collective-permute-start(bf16[3,1024,256]{2,1,0:T(8,128)(2,1)S(1)} %add_convert_fusion.5.near_ref), channel_id=1, source_target_pairs={{0,4},{4,0},{8,12},{12,8},{1,5},{5,1},{9,13},{13,9},{2,6},{6,2},{1... | collective-permute-start | bytes 4718600 | tf_op jit(solution)/shard_map/ppermute | solution.py:1300
  418.4 107.7 %collective-permute-start.7 = (bf16[3,1024,256]{2,1,0:T(8,128)(2,1)S(1)}, bf16[3,1024,256]{2,1,0:T(8,128)(2,1)}, u32[]{:S(2)}, u32[]{:S(2)}) collective-permute-start(bf16[3,1024,256]{2,1,0:T(8,128)(2,1)S(1)} %add_convert_fusion.6.near_ref), channel_id=1, source_target_pairs={{0,4},{4,0},{8,12},{12,8},{1,5},{5,1},{9,13},{13,9},{2,6},{6,2},{1... | collective-permute-start | bytes 4718600 | tf_op jit(solution)/shard_map/ppermute | solution.py:1300
  526.1 127.4 %all-gather.15.cloned.1.call-start = ((), (), s32[]{:S(2)}) async-start(), calls=%async_computation.11 | async-start | bytes 5242880 | tf_op jit(solution)/shard_map/all_gather | solution.py:1356
  526.2 37.7 %collective-permute-start.6 = (bf16[3,1024,256]{2,1,0:T(8,128)(2,1)}, bf16[3,1024,256]{2,1,0:T(8,128)(2,1)}, u32[]{:S(2)}, u32[]{:S(2)}) collective-permute-start(bf16[3,1024,256]{2,1,0:T(8,128)(2,1)} %bitcast.262), channel_id=1, source_target_pairs={{0,16},{16,0},{1,17},{17,1},{2,18},{18,2},{3,19},{19,3},{4,20},{20... | collective-permute-start | bytes 4718600 | tf_op jit(solution)/shard_map/ppermute | solution.py:1157
  528.6 79.4 %collective-permute-start.11 = (bf16[4,256,1024]{2,1,0:T(8,128)(2,1)}, bf16[4,256,1024]{2,1,0:T(8,128)(2,1)}, u32[]{:S(2)}, u32[]{:S(2)}) collective-permute-start(bf16[4,256,1024]{2,1,0:T(8,128)(2,1)} %constant_dynamic-slice_fusion.3.refs_8_), channel_id=1, source_target_pairs={{16,0},{0,16},{17,1},{1,17},{18,2},{2,18},{19,3},{3,19},{20,4},{4,... | collective-permute-start | bytes 6291464 | tf_op jit(solution)/shard_map/ppermute | solution.py:1143
  567.3 40.8 %collective-permute-start.10 = (bf16[3,1024,256]{2,1,0:T(8,128)(2,1)}, bf16[3,1024,256]{2,1,0:T(8,128)(2,1)}, u32[]{:S(2)}, u32[]{:S(2)}) collective-permute-start(bf16[3,1024,256]{2,1,0:T(8,128)(2,1)} %add_convert_fusion.4.near_ref), channel_id=1, source_target_pairs={{0,4},{4,0},{8,12},{12,8},{1,5},{5,1},{9,13},{13,9},{2,6},{6,2},{1... | collective-permute-start | bytes 4718600 | tf_op jit(solution)/shard_map/ppermute | solution.py:1300
  613.8 39.7 %collective-permute-start.12 = (bf16[1024,512]{1,0:T(8,128)(2,1)}, bf16[1024,512]{1,0:T(8,128)(2,1)}, u32[]{:S(2)}, u32[]{:S(2)}) collective-permute-start(bf16[1024,512]{1,0:T(8,128)(2,1)} %convolution_convert_fusion), channel_id=1, source_target_pairs={{0,16},{16,0},{1,17},{17,1},{2,18},{18,2},{3,19},{19,3},{4,20},{20... | collective-permute-start | bytes 3145736 | tf_op jit(solution)/shard_map/ppermute | solution.py:1157
  621.0 32.5 %all-to-all-start.1 = ((bf16[4,1,1,512,128]{4,3,2,1,0:T(8,128)(2,1)}), bf16[4,1,1,512,128]{4,3,2,1,0:T(8,128)(2,1)}, u32[]{:S(2)}, u32[]{:S(2)}) async-start(bf16[4,1,1,512,128]{4,3,2,1,0:T(8,128)(2,1)} %bitcast.222), calls=%async_computation.3 | async-start | bytes 1048576 | tf_op jit(solution)/shard_map/all_to_all | solution.py:144
  627.6 69.9 %reduce-scatter.8.cloned.1.call-start = ((), (), s32[]{:S(2)}) async-start(), calls=%async_computation.8 | async-start | bytes 1310720 | tf_op jit(solution)/shard_map/reduce_scatter | solution.py:1366
  652.0 70.1 %collective-permute-start.13 = (bf16[3,1024,256]{2,1,0:T(8,128)(2,1)}, bf16[3,1024,256]{2,1,0:T(8,128)(2,1)}, u32[]{:S(2)}, u32[]{:S(2)}) collective-permute-start(bf16[3,1024,256]{2,1,0:T(8,128)(2,1)} %bitcast.263), channel_id=1, source_target_pairs={{0,16},{16,0},{1,17},{17,1},{2,18},{18,2},{3,19},{19,3},{4,20},{20... | collective-permute-start | bytes 4718600 | tf_op jit(solution)/shard_map/ppermute | solution.py:1157
  657.0 69.5 %all-gather.11.cloned.1.call-start = ((), (), s32[]{:S(2)}) async-start(), calls=%async_computation.9 | async-start | bytes 1310720 | tf_op jit(solution)/shard_map/all_gather | solution.py:1386
  697.5 316.3 %all-gather.17.cloned.1.call-start = ((), (), s32[]{:S(2)}) async-start(), calls=%async_computation.12 | async-start | bytes 3932160 | tf_op jit(solution)/shard_map/all_gather | solution.py:1445
  726.5 36.3 %collective-permute-start.15 = (bf16[3,1024,256]{2,1,0:T(8,128)(2,1)}, bf16[3,1024,256]{2,1,0:T(8,128)(2,1)}, u32[]{:S(2)}, u32[]{:S(2)}) collective-permute-start(bf16[3,1024,256]{2,1,0:T(8,128)(2,1)} %add_convert_fusion.3.near_ref), channel_id=1, source_target_pairs={{0,4},{4,0},{8,12},{12,8},{1,5},{5,1},{9,13},{13,9},{2,6},{6,2},{1... | collective-permute-start | bytes 4718600 | tf_op jit(solution)/shard_map/ppermute | solution.py:1300
  727.9 36.3 %collective-permute-start.14 = (bf16[3,1024,256]{2,1,0:T(8,128)(2,1)}, bf16[3,1024,256]{2,1,0:T(8,128)(2,1)}, u32[]{:S(2)}, u32[]{:S(2)}) collective-permute-start(bf16[3,1024,256]{2,1,0:T(8,128)(2,1)} %bitcast.264), channel_id=1, source_target_pairs={{0,16},{16,0},{1,17},{17,1},{2,18},{18,2},{3,19},{19,3},{4,20},{20... | collective-permute-start | bytes 4718600 | tf_op jit(solution)/shard_map/ppermute | solution.py:1157
  766.0 36.3 %collective-permute-start.17 = (bf16[3,1024,256]{2,1,0:T(8,128)(2,1)S(1)}, bf16[3,1024,256]{2,1,0:T(8,128)(2,1)}, u32[]{:S(2)}, u32[]{:S(2)}) collective-permute-start(bf16[3,1024,256]{2,1,0:T(8,128)(2,1)S(1)} %add_convert_fusion.2.near_ref), channel_id=1, source_target_pairs={{0,4},{4,0},{8,12},{12,8},{1,5},{5,1},{9,13},{13,9},{2,6},{6,2},{1... | collective-permute-start | bytes 4718600 | tf_op jit(solution)/shard_map/ppermute | solution.py:1300
  766.4 36.0 %collective-permute-start.16 = (bf16[3,1024,256]{2,1,0:T(8,128)(2,1)}, bf16[3,1024,256]{2,1,0:T(8,128)(2,1)}, u32[]{:S(2)}, u32[]{:S(2)}) collective-permute-start(bf16[3,1024,256]{2,1,0:T(8,128)(2,1)} %bitcast.72), channel_id=1, source_target_pairs={{0,16},{16,0},{1,17},{17,1},{2,18},{18,2},{3,19},{19,3},{4,20},{20... | collective-permute-start | bytes 4718600 | tf_op jit(solution)/shard_map/ppermute | solution.py:1157
  804.2 72.5 %collective-permute-start.20 = (bf16[3,1024,256]{2,1,0:T(8,128)(2,1)}, bf16[3,1024,256]{2,1,0:T(8,128)(2,1)}, u32[]{:S(2)}, u32[]{:S(2)}) collective-permute-start(bf16[3,1024,256]{2,1,0:T(8,128)(2,1)} %bitcast.77), channel_id=1, source_target_pairs={{0,16},{16,0},{1,17},{17,1},{2,18},{18,2},{3,19},{19,3},{4,20},{20... | collective-permute-start | bytes 4718600 | tf_op jit(solution)/shard_map/ppermute | solution.py:1157
  804.8 71.8 %collective-permute-start.19 = (bf16[3,1024,256]{2,1,0:T(8,128)(2,1)S(1)}, bf16[3,1024,256]{2,1,0:T(8,128)(2,1)}, u32[]{:S(2)}, u32[]{:S(2)}) collective-permute-start(bf16[3,1024,256]{2,1,0:T(8,128)(2,1)S(1)} %add_convert_fusion.1.near_ref), channel_id=1, source_target_pairs={{0,4},{4,0},{8,12},{12,8},{1,5},{5,1},{9,13},{13,9},{2,6},{6,2},{1... | collective-permute-start | bytes 4718600 | tf_op jit(solution)/shard_map/ppermute | solution.py:1300
  808.7 68.0 %collective-permute-start.18 = (bf16[1024,384]{1,0:T(8,128)(2,1)}, bf16[1024,384]{1,0:T(8,128)(2,1)S(1)}, u32[]{:S(2)}, u32[]{:S(2)}) collective-permute-start(bf16[1024,384]{1,0:T(8,128)(2,1)} %fusion.23), channel_id=1, source_target_pairs={{0,16},{16,0},{1,17},{17,1},{2,18},{18,2},{3,19},{19,3},{4,20},{20... | collective-permute-start | bytes 2359304 | tf_op jit(solution)/shard_map/ppermute | solution.py:1157
  917.5 91.0 %collective-permute-start.22 = (bf16[3,1024,256]{2,1,0:T(8,128)(2,1)}, bf16[3,1024,256]{2,1,0:T(8,128)(2,1)}, u32[]{:S(2)}, u32[]{:S(2)}) collective-permute-start(bf16[3,1024,256]{2,1,0:T(8,128)(2,1)} %add_convert_fusion.near_ref), channel_id=1, source_target_pairs={{0,4},{4,0},{8,12},{12,8},{1,5},{5,1},{9,13},{13,9},{2,6},{6,2},{1... | collective-permute-start | bytes 4718600 | tf_op jit(solution)/shard_map/ppermute | solution.py:1300
  922.5 74.0 %collective-permute-start.21 = (bf16[20,2048]{1,0:T(8,128)(2,1)S(1)}, bf16[20,2048]{1,0:T(8,128)(2,1)}, u32[]{:S(2)}, u32[]{:S(2)}) collective-permute-start(bf16[20,2048]{1,0:T(8,128)(2,1)S(1)} %fusion.46), channel_id=1, source_target_pairs={{0,16},{16,0},{1,17},{17,1},{2,18},{18,2},{3,19},{19,3},{4,20},{20... | collective-permute-start | bytes 245768 | tf_op jit(solution)/shard_map/ppermute | solution.py:1152
  (58 other events, 1133.5 us)
Sparse Core Ops, SparseCore 0:
  10.2 60.8 all-gather.12
  122.9 62.0 all-gather.8
  407.1 96.8 reduce-scatter.3
  526.2 53.1 reduce-scatter.5
  610.7 37.2 all-gather.14
  657.1 27.4 reduce-scatter.7
  697.6 28.8 all-gather.10
  911.2 96.4 all-gather.16

commit v4 on v3

--- a/solution.py
+++ b/solution.py
@@ -1308,6 +1308,8 @@
         parts.append(run(e))
         if e > 0:
             hidden_two = end_x(e - 1, (hidden_two, grads[e][1]))[0]
+            if e == 1:
+                hidden_two, far_slices = tie((hidden_two, far_slices))
             start_z(e - 1)
         if e > 2:
             hidden_two = end_z(e - 3, hidden_two)
@@ -1434,15 +1436,18 @@
     small_grads = jnp.concatenate(
         [gain_one_grad[None], gain_two_grad[None], router_grad, heads_gains]
     )
-    small_grads = jnp.pad(small_grads, ((0, -small_grads.shape[0] % 8), (0, 0)))
-    small_grads = share(small_grads, False, 9)
-
-    d_hidden, small_grads, heads_grads, sums[2 * mine - 1] = tie(
-        (d_hidden, small_grads, heads_grads, sums[2 * mine - 1])
-    )
+    small_shape, across = small_grads.shape, 3 * own_cols
+    small_count = small_grads.size
+    small_rows = -(-small_count // (16 * across)) * 16
+    small_grads = jnp.pad(
+        small_grads.astype(BF16).reshape(-1), (0, small_rows * across - small_count)
+    )
+    heads_grads = add([heads_mine], heads_grads)
+    heads_grads = jnp.concatenate([heads_grads, small_grads.reshape(small_rows, across)])
+    heads_grads = lax.all_gather(heads_grads, "ctx", axis=0, tiled=False)
     start_z(2 * mine - 1)
-    heads_grads = add([heads_mine], heads_grads)
-    heads_grads = lax.all_gather(heads_grads, "ctx", axis=0, tiled=False)
+    small_grads = heads_grads[:, wide:].astype(F32).sum(axis=0).reshape(-1)[:small_count]
+    small_grads = lax.all_gather(small_grads.reshape(small_shape), "tp", axis=0, tiled=False)
     pull_one = d_hidden * columns(gain_one)
     mean_one = lax.psum(jnp.sum(pull_one * inputs_c, axis=1), "tp")[:, None] / width
     d_inputs = d_mixed + scale_one * pull_one - inputs_c * scale_one**3 * mean_one
@@ -1463,7 +1468,7 @@
     small_grads = lax.dynamic_slice_in_dim(small_grads, dp_at * wide, wide, 1)
 
     def heads_grad(i):
-        v = heads_grads[:, :, i * own_cols : (i + 1) * own_cols].astype(F32)
+        v = heads_grads[:, :wide, i * own_cols : (i + 1) * own_cols].astype(F32)
         return v.transpose(1, 0, 2).reshape(wide, local)
 
     for e in range(mine, 2 * mine - 1):

time: 1040 us -> 1020 us (0.981)
  Pallas kernels: 691 us -> 675 us
    pallas_call x3 -> x2, Pallas kernels: 48.5 us -> 20.1 us  [share(): pl.pallas_call(functools.partial(share_kernel, over_tp), cost_estimate=pl...]
    pallas_call x2, Pallas kernels: 158 us -> 173 us  [returns(): pl.pallas_call(functools.partial(returns_kernel, kinds, mine, blocks, fli...]
    ppermute x8, starting transfers between devices: 19.6 us -> 30.8 us  [start_z(): lax.ppermute(sums[e], 'ctx', [(i, i ^ 1) for i in range(ctx_count)])]
  transfers between devices with their start and end apart: 33 -> 33, of which waited for: 9 -> 9; matrix products, arithmetic and copies ran while one was open for 13% -> 14% of each run, Pallas kernels for 62% -> 64%
where the time goes in v4:
time: 1020 us; the launch traced here: 1010 us
  Pallas kernels  675 us (66%)
  other arithmetic  75.8 us (7%)
  waiting for transfers between devices  67.5 us (7%)
  starting transfers between devices  60.8 us (6%)
  local copies, waits for them, and re-layouts  59.8 us (6%)
  matrix products  34.5 us (3%)
  blocking collectives  23.4 us (2%)
  between operations  15.7 us (2%)
    pallas_call x8, Pallas kernels, expert(): pl.pallas_call(functools.partial(expert_kernel, blocks, e, far, mine, ful...  198 us
    pallas_call x2, Pallas kernels, returns(): pl.pallas_call(functools.partial(returns_kernel, kinds, mine, blocks, fli...  173 us
    pallas_call x2, Pallas kernels, spread(): pl.pallas_call(functools.partial(spread_kernel, [axis for axis, _ in carr...  148 us
    pallas_call x2, Pallas kernels, join(): pl.pallas_call(join_kernel, cost_estimate=pl.CostEstimate(flops=25 * MICR...  50.3 us
    pallas_call x8, Pallas kernels, place_grads(): pl.pallas_call(place_kernel, cost_estimate=pl.CostEstimate(flops=4 * MICR...  37.8 us
    ppermute x10, waiting for transfers between devices, swap(): lax.ppermute(blocks[s], 'dp', [(i, (i + s) % dp_count) for i in range(dp_...  32.3 us
    ppermute x8, starting transfers between devices, start_z(): lax.ppermute(sums[e], 'ctx', [(i, i ^ 1) for i in range(ctx_count)])  30.8 us
    ppermute x8, waiting for transfers between devices, start_z(): lax.ppermute(sums[e], 'ctx', [(i, i ^ 1) for i in range(ctx_count)])  20.4 us
  transfers between devices with their start and end apart: 33, of which 9 were waited for; matrix products, arithmetic and copies ran while one was open for 14% of the time, Pallas kernels for 64%

profile of v4, /device:TPU:0, one launch (start us, length us, event | category | flops | bytes accessed | tf_op | source)
XLA Modules:
  0.0 1012.4 jit_solution(10784943219276903583)
XLA Ops:
  32.5 87.2 %shard_map.263 = (bf16[2048,2048]{1,0:T(8,128)(2,1)}, bf16[1,1024,384]{2,1,0:T(8,128)(2,1)}, bf16[1,512,1024]{2,1,0:T(8,128)(2,1)}, bf16[1,4,1024,256]{3,2,1,0:T(8,128)(2,1)}) custom-call(bf16[512,512]{1,0:T(8,128)(2,1)} %multiply_convert_fusion.1.x_ref, bf16[1024,384]{1,0:T(8,128)(2,1)} %get-tuple-element.532.refs_0_, bf16[512,1024]{1,0:T(8,128)(2,1)} %refs_1_.1, ...), custom_call_target="tpu_custom_call" | custom-call | flops 4026531840 | tf_op jit(solution)/shard_map/pallas_call | solution.py:473
  137.2 9.8 shard_map.264
  150.7 7.1 shard_map.265
  167.7 12.2 %all-to-all-done = bf16[4,1,1,512,128]{3,4,2,1,0:T(8,128)(2,1)S(1)} async-done(((bf16[4,1,1,512,128]{3,4,2,1,0:T(8,128)(2,1)}), bf16[4,1,1,512,128]{3,4,2,1,0:T(8,128)(2,1)S(1)}, u32[]{:S(2)}, u32[]{:S(2)}) %all-to-all-start) | async-done | bytes 524320 | tf_op jit(solution)/shard_map/all_to_all | solution.py:153
  184.2 17.2 %shard_map.266 = f32[512,512]{1,0:T(8,128)S(1)} custom-call(bf16[512,2048]{1,0:T(8,128)(2,1)S(1)} %pad_maximum_fusion.1.x_ref), custom_call_target="tpu_custom_call" | custom-call | flops 1140850688 | tf_op jit(solution)/shard_map/pallas_call | solution.py:666
  202.8 5.8 psum.21
  209.6 61.0 %shard_map.267 = (bf16[2048,2048]{1,0:T(8,128)(2,1)}, bf16[1,4,256,1024]{3,2,1,0:T(8,128)(2,1)}) custom-call(bf16[512,512]{1,0:T(8,128)(2,1)} %multiply_convert_fusion.x_ref, bf16[4,256,1024]{2,1,0:T(8,128)(2,1)} %constant_dynamic-slice_fusion.11.refs_0_.refs_8_.refs_4_), custom_call_target="tpu_custom_call" | custom-call | flops 4026531840 | tf_op jit(solution)/shard_map/pallas_call | solution.py:473
  270.6 24.9 %shard_map.268 = (bf16[2048,256]{1,0:T(8,128)(2,1)}, bf16[2048,256]{1,0:T(8,128)(2,1)}, bf16[2048,256]{1,0:T(8,128)(2,1)}, f32[2048,1]{1,0:T(8,128)}, bf16[3,102...) custom-call(bf16[2048,2048]{1,0:T(8,128)(2,1)} %get-tuple-element.367.refs_0_, ...), custom_call_target="tpu_custom_call" | custom-call | flops 1811939328 | tf_op jit(solution)/shard_map/pallas_call | solution.py:307
  305.8 24.9 %shard_map.269 = (bf16[2048,256]{1,0:T(8,128)(2,1)}, bf16[2048,256]{1,0:T(8,128)(2,1)}, bf16[2048,256]{1,0:T(8,128)(2,1)}, f32[2048,1]{1,0:T(8,128)}, bf16[3,102...) custom-call(bf16[2048,2048]{1,0:T(8,128)(2,1)} %get-tuple-element.367.refs_0_, ...), custom_call_target="tpu_custom_call" | custom-call | flops 1811939328 | tf_op jit(solution)/shard_map/pallas_call | solution.py:307
  332.0 25.4 %shard_map.270 = (bf16[2048,256]{1,0:T(8,128)(2,1)}, bf16[2048,256]{1,0:T(8,128)(2,1)}, bf16[2048,256]{1,0:T(8,128)(2,1)}, f32[2048,1]{1,0:T(8,128)}, bf16[3,102...) custom-call(bf16[2048,2048]{1,0:T(8,128)(2,1)} %get-tuple-element.367.refs_0_, ...), custom_call_target="tpu_custom_call" | custom-call | flops 1811939328 | tf_op jit(solution)/shard_map/pallas_call | solution.py:307
  361.1 7.1 collective-permute-done.3
  368.2 25.4 %shard_map.271 = (bf16[2048,256]{1,0:T(8,128)(2,1)}, bf16[2048,256]{1,0:T(8,128)(2,1)}, bf16[2048,256]{1,0:T(8,128)(2,1)}, f32[2048,1]{1,0:T(8,128)}, bf16[3,102...) custom-call(bf16[2048,2048]{1,0:T(8,128)(2,1)} %get-tuple-element.367.refs_0_, ...), custom_call_target="tpu_custom_call" | custom-call | flops 1811939328 | tf_op jit(solution)/shard_map/pallas_call | solution.py:307
  394.9 12.9 %shard_map.272 = bf16[4,2048,512]{2,1,0:T(8,128)(2,1)} custom-call(bf16[2048,256]{1,0:T(8,128)(2,1)S(1)} %copy-done.17, bf16[2048,256]{1,0:T(8,128)(2,1)S(1)} %copy-done.18, bf16[2048,256]{1,0:T(8,128)(2,1)S(1)} %copy-done.19, bf16[2048,256]{1,0:T(8,128)(2,1)S(1)} %copy-done.20, bf16[4,256,1024]{2,1,0:T(8,128)(2,1)} %constant_dynamic-slice_fusion.11.refs_0_.refs_8_.refs_4_, ...), custom_call_target="tpu_custom_call" | custom-call | flops 1006632960 | tf_op jit(solution)/shard_map/pallas_call | solution.py:996
  423.4 104.1 %shard_map.273 = (f32[512,512]{1,0:T(8,128)}, f32[4,4,512]{2,1,0:T(4,128)}) custom-call(bf16[2048,256]{1,0:T(8,128)(2,1)} %get-tuple-element.272.refs_0_, bf16[2048,256]{1,0:T(8,128)(2,1)} %get-tuple-element.273.refs_1_, bf16[2048,256]{1,0:T(8,128)(2,1)} %get-tuple-element.274.refs_2_, bf16[2048,256]{1,0:T(8,128)(2,1)} %get-tuple-element.275.refs_3_, ...), custom_call_target="tpu_custom_call" | custom-call | flops 4362076160 | tf_op jit(solution)/shard_map/pallas_call | solution.py:946
  535.9 6.0 psum.22
  542.0 23.4 %collective-permute-done.6 = bf16[3,1024,256]{2,1,0:T(8,128)(2,1)} collective-permute-done((bf16[3,1024,256]{2,1,0:T(8,128)(2,1)}, bf16[3,1024,256]{2,1,0:T(8,128)(2,1)}, u32[]{:S(2)}, u32[]{:S(2)}) %collective-permute-start.6) | collective-permute-done | bytes 1572896 | tf_op jit(solution)/shard_map/ppermute | solution.py:1157
  568.7 9.8 collective-permute-start.10
  581.6 17.1 %shard_map.274 = bf16[512,2048]{1,0:T(8,128)(2,1)} custom-call(bf16[512,512]{1,0:T(8,128)(2,1)} %get-tuple-element.505.x_ref), custom_call_target="tpu_custom_call" | custom-call | flops 1677721600 | tf_op jit(solution)/shard_map/pallas_call | solution.py:516
  598.7 12.1 %collective-permute-done.10.far_ref = bf16[3,1024,256]{2,1,0:T(8,128)(2,1)} collective-permute-done((bf16[3,1024,256]{2,1,0:T(8,128)(2,1)}, bf16[3,1024,256]{2,1,0:T(8,128)(2,1)}, u32[]{:S(2)}, u32[]{:S(2)}) %collective-permute-start.10) | collective-permute-done | bytes 1572896 | tf_op jit(solution)/shard_map/ppermute | solution.py:1300
  627.9 24.5 %shard_map.275 = (bf16[3,1024,256]{2,1,0:T(8,128)(2,1)}, bf16[1,3,1024,256]{3,2,1,0:T(8,128)(2,1)}) custom-call(bf16[2048,2048]{1,0:T(8,128)(2,1)} %get-tuple-element.367.refs_0_, bf16[2048,2048]{1,0:T(8,128)(2,1)} %all-gather.9.cloned.1.call-done.refs_1_, f32[2048,16]{1,0:T(8,128)} %bitcast.209, bf16[16,2048]{1,0:T(8,128)(2,1)} %pad_maximum_fusion.9.refs_3_, ...), custom_call_target="tpu_custom_call" | custom-call | flops 1811939328 | tf_op jit(solution)/shard_map/pallas_call | solution.py:307
  661.3 10.2 %shard_map.276 = (f32[1,2048,128]{2,1,0:T(8,128)S(1)}, f32[1,2048,128]{2,1,0:T(8,128)S(1)}, bf16[1,2048,128]{2,1,0:T(8,128)(2,1)S(1)}) custom-call(s32[1,3]{1,0:T(1,128)S(1)} %copy-done.23, bf16[1,2048,128]{2,1,0:T(8,128)(2,1)S(1)} %copy-done.10, bf16[1,2048,128]{2,1,0:T(8,128)(2,1)S(1)} %copy-done.8, bf16[1,2048,128]{2,1,0:T(8,128)(2,1)S(1)} %copy-done.12, ...), custom_call_target="tpu_custom_call" | custom-call | flops 671088640 | tf_op jit(solution)/shard_map/pallas_call | solution.py:126
  676.3 10.3 %shard_map.277 = f32[2,2048]{1,0:T(2,128)S(1)} custom-call(f32[2,2048]{1,0:T(2,128)S(1)} %pad_maximum_fusion.12.x_ref), custom_call_target="tpu_custom_call" | custom-call | flops 536870912 | tf_op jit(solution)/shard_map/pallas_call | solution.py:1099
  697.2 24.4 %shard_map.278 = (bf16[3,1024,256]{2,1,0:T(8,128)(2,1)}, bf16[1,3,1024,256]{3,2,1,0:T(8,128)(2,1)}) custom-call(bf16[2048,2048]{1,0:T(8,128)(2,1)} %get-tuple-element.367.refs_0_, bf16[2048,2048]{1,0:T(8,128)(2,1)} %all-gather.9.cloned.1.call-done.refs_1_, f32[2048,16]{1,0:T(8,128)} %bitcast.210, bf16[16,2048]{1,0:T(8,128)(2,1)} %pad_maximum_fusion.9.refs_3_, ...), custom_call_target="tpu_custom_call" | custom-call | flops 1811939328 | tf_op jit(solution)/shard_map/pallas_call | solution.py:307
  730.0 24.4 %shard_map.279 = (bf16[3,1024,256]{2,1,0:T(8,128)(2,1)}, bf16[1,3,1024,256]{3,2,1,0:T(8,128)(2,1)}) custom-call(bf16[2048,2048]{1,0:T(8,128)(2,1)} %get-tuple-element.367.refs_0_, bf16[2048,2048]{1,0:T(8,128)(2,1)} %all-gather.9.cloned.1.call-done.refs_1_, f32[2048,16]{1,0:T(8,128)} %bitcast.211, bf16[16,2048]{1,0:T(8,128)(2,1)} %pad_maximum_fusion.9.refs_3_, ...), custom_call_target="tpu_custom_call" | custom-call | flops 1811939328 | tf_op jit(solution)/shard_map/pallas_call | solution.py:307
  768.4 24.2 %shard_map.282 = (bf16[3,1024,256]{2,1,0:T(8,128)(2,1)}, bf16[1,3,1024,256]{3,2,1,0:T(8,128)(2,1)}) custom-call(bf16[2048,2048]{1,0:T(8,128)(2,1)} %get-tuple-element.367.refs_0_, bf16[2048,2048]{1,0:T(8,128)(2,1)} %all-gather.9.cloned.1.call-done.refs_1_, f32[2048,16]{1,0:T(8,128)} %bitcast.212, bf16[16,2048]{1,0:T(8,128)(2,1)} %pad_maximum_fusion.9.refs_3_, ...), custom_call_target="tpu_custom_call" | custom-call | flops 1811939328 | tf_op jit(solution)/shard_map/pallas_call | solution.py:307
  809.4 68.7 %shard_map.285 = f32[512,512]{1,0:T(8,128)} custom-call(bf16[2048,384]{1,0:T(8,128)(2,1)} %pad_maximum_fusion.2.refs_0_, bf16[1,1024,384]{2,1,0:T(8,128)(2,1)} %get-tuple-element.531.refs_1_, bf16[1,1024,384]{2,1,0:T(8,128)(2,1)} %get-tuple-element.229.refs_2_), custom_call_target="tpu_custom_call" | custom-call | flops 4362076160 | tf_op jit(solution)/shard_map/pallas_call | solution.py:946
  889.5 15.2 %collective-permute-start.22 = (bf16[3,1024,256]{2,1,0:T(8,128)(2,1)}, bf16[3,1024,256]{2,1,0:T(8,128)(2,1)}, u32[]{:S(2)}, u32[]{:S(2)}) collective-permute-start(bf16[3,1024,256]{2,1,0:T(8,128)(2,1)} %add_convert_fusion.near_ref), channel_id=1, source_target_pairs={{0,4},{4,0},{8,12},{12,8},{1,5},{5,1},{9,13},{13,9},{2,6},{6,2},{1... | collective-permute-start | bytes 4718600 | tf_op jit(solution)/shard_map/ppermute | solution.py:1300
  913.9 6.0 psum.23
  936.1 33.2 %shard_map.286 = f32[512,2048]{1,0:T(8,128)} custom-call(f32[512,512]{1,0:T(8,128)} %multiply_subtract_fusion.x_ref), custom_call_target="tpu_custom_call" | custom-call | flops 1677721600 | tf_op jit(solution)/shard_map/pallas_call | solution.py:516
  969.4 5.5 fusion
  974.9 8.0 collective-permute-done.22.far_ref
  989.2 5.6 all_gather.35
  (343 shorter events, 243.0 us)
Async XLA Ops:
  7.2 112.5 %all-gather.13.cloned.1.call-start = ((), (), s32[]{:S(2)}) async-start(), calls=%async_computation.10 | async-start | bytes 2703360 | tf_op jit(solution)/shard_map/all_gather | solution.py:1237
  10.1 260.5 %all-gather.9.cloned.1.call-start = ((), (), s32[]{:S(2)}) async-start(), calls=%async_computation.5 | async-start | bytes 10485760 | tf_op jit(solution)/shard_map/all_gather | solution.py:1240
  13.9 16.3 %collective-permute-start = (bf16[20,1024]{1,0:T(8,128)(2,1)S(1)}, bf16[20,1024]{1,0:T(8,128)(2,1)S(1)}, u32[]{:S(2)}, u32[]{:S(2)}) collective-permute-start(bf16[20,1024]{1,0:T(8,128)(2,1)S(1)} %concatenate.106), channel_id=1, source_target_pairs={{16,0},{0,16},{17,1},{1,17},{18,2},{2,18},{19,3},{3,19},{20,4},{4,... | collective-permute-start | bytes 122888 | tf_op jit(solution)/shard_map/ppermute | solution.py:1143
  126.9 57.3 %collective-permute-start.1 = (bf16[4,1024,256]{2,1,0:T(8,128)(2,1)S(1)}, bf16[4,1024,256]{2,1,0:T(8,128)(2,1)}, u32[]{:S(2)}, u32[]{:S(2)}) collective-permute-start(bf16[4,1024,256]{2,1,0:T(8,128)(2,1)S(1)} %get-tuple-element.239.refs_6_.refs_10_), channel_id=1, source_target_pairs={{16,0},{0,16},{17,1},{1,17},{18,2},{2,18},{19,3},{3,19},{20,4},{4,... | collective-permute-start | bytes 6291464 | tf_op jit(solution)/shard_map/ppermute | solution.py:1143
  159.8 20.0 %all-to-all-start = ((bf16[4,1,1,512,128]{3,4,2,1,0:T(8,128)(2,1)}), bf16[4,1,1,512,128]{3,4,2,1,0:T(8,128)(2,1)S(1)}, u32[]{:S(2)}, u32[]{:S(2)}) async-start(bf16[4,1,1,512,128]{3,4,2,1,0:T(8,128)(2,1)} %copy.95), calls=%async_computation | async-start | bytes 1048576 | tf_op jit(solution)/shard_map/all_to_all | solution.py:153
  164.7 362.8 %reduce-scatter.4.cloned.1.call-start = ((), (), s32[]{:S(2)}) async-start(), calls=%async_computation.6 | async-start | bytes 10485760 | tf_op jit(solution)/shard_map/reduce_scatter | solution.py:1319
  295.5 36.5 %collective-permute-start.2 = (bf16[3,1024,256]{2,1,0:T(8,128)(2,1)}, bf16[3,1024,256]{2,1,0:T(8,128)(2,1)S(1)}, u32[]{:S(2)}, u32[]{:S(2)}) collective-permute-start(bf16[3,1024,256]{2,1,0:T(8,128)(2,1)} %bitcast.274), channel_id=1, source_target_pairs={{0,16},{16,0},{1,17},{17,1},{2,18},{18,2},{3,19},{19,3},{4,20},{20... | collective-permute-start | bytes 4718600 | tf_op jit(solution)/shard_map/ppermute | solution.py:1157
  330.7 37.5 %collective-permute-start.3 = (bf16[3,1024,256]{2,1,0:T(8,128)(2,1)}, bf16[3,1024,256]{2,1,0:T(8,128)(2,1)S(1)}, u32[]{:S(2)}, u32[]{:S(2)}) collective-permute-start(bf16[3,1024,256]{2,1,0:T(8,128)(2,1)} %bitcast.276), channel_id=1, source_target_pairs={{0,16},{16,0},{1,17},{17,1},{2,18},{18,2},{3,19},{19,3},{4,20},{20... | collective-permute-start | bytes 4718600 | tf_op jit(solution)/shard_map/ppermute | solution.py:1157
  357.4 50.4 %collective-permute-start.5 = (bf16[3,1024,256]{2,1,0:T(8,128)(2,1)}, bf16[3,1024,256]{2,1,0:T(8,128)(2,1)}, u32[]{:S(2)}, u32[]{:S(2)}) collective-permute-start(bf16[3,1024,256]{2,1,0:T(8,128)(2,1)} %bitcast.275), channel_id=1, source_target_pairs={{0,16},{16,0},{1,17},{17,1},{2,18},{18,2},{3,19},{19,3},{4,20},{20... | collective-permute-start | bytes 4718600 | tf_op jit(solution)/shard_map/ppermute | solution.py:1157
  361.0 46.8 %collective-permute-start.4 = (bf16[3,1024,256]{2,1,0:T(8,128)(2,1)S(1)}, bf16[3,1024,256]{2,1,0:T(8,128)(2,1)S(1)}, u32[]{:S(2)}, u32[]{:S(2)}) collective-permute-start(bf16[3,1024,256]{2,1,0:T(8,128)(2,1)S(1)} %add_convert_fusion.7.near_ref), channel_id=1, source_target_pairs={{0,4},{4,0},{8,12},{12,8},{1,5},{5,1},{9,13},{13,9},{2,6},{6,2},{1... | collective-permute-start | bytes 4718600 | tf_op jit(solution)/shard_map/ppermute | solution.py:1300
  409.0 201.8 %reduce-scatter.6.cloned.1.call-start = ((), (), s32[]{:S(2)}) async-start(), calls=%async_computation.7 | async-start | bytes 2621440 | tf_op jit(solution)/shard_map/reduce_scatter | solution.py:1335
  409.0 118.5 %collective-permute-start.9 = (bf16[8,1024,256]{2,1,0:T(8,128)(2,1)}, bf16[8,1024,256]{2,1,0:T(8,128)(2,1)}, u32[]{:S(2)}, u32[]{:S(2)}) collective-permute-start(bf16[8,1024,256]{2,1,0:T(8,128)(2,1)} %pad_maximum_fusion.refs_4_.refs_6_), channel_id=1, source_target_pairs={{16,0},{0,16},{17,1},{1,17},{18,2},{2,18},{19,3},{3,19},{20,4},{4,... | collective-permute-start | bytes 12582920 | tf_op jit(solution)/shard_map/ppermute | solution.py:1143
  411.6 115.9 %collective-permute-start.8 = (bf16[3,1024,256]{2,1,0:T(8,128)(2,1)S(1)}, bf16[3,1024,256]{2,1,0:T(8,128)(2,1)}, u32[]{:S(2)}, u32[]{:S(2)}) collective-permute-start(bf16[3,1024,256]{2,1,0:T(8,128)(2,1)S(1)} %add_convert_fusion.5.near_ref), channel_id=1, source_target_pairs={{0,4},{4,0},{8,12},{12,8},{1,5},{5,1},{9,13},{13,9},{2,6},{6,2},{1... | collective-permute-start | bytes 4718600 | tf_op jit(solution)/shard_map/ppermute | solution.py:1300
  413.5 114.0 %collective-permute-start.7 = (bf16[3,1024,256]{2,1,0:T(8,128)(2,1)S(1)}, bf16[3,1024,256]{2,1,0:T(8,128)(2,1)}, u32[]{:S(2)}, u32[]{:S(2)}) collective-permute-start(bf16[3,1024,256]{2,1,0:T(8,128)(2,1)S(1)} %add_convert_fusion.6.near_ref), channel_id=1, source_target_pairs={{0,4},{4,0},{8,12},{12,8},{1,5},{5,1},{9,13},{13,9},{2,6},{6,2},{1... | collective-permute-start | bytes 4718600 | tf_op jit(solution)/shard_map/ppermute | solution.py:1300
  527.6 125.5 %all-gather.15.cloned.1.call-start = ((), (), s32[]{:S(2)}) async-start(), calls=%async_computation.11 | async-start | bytes 5242880 | tf_op jit(solution)/shard_map/all_gather | solution.py:1358
  527.6 37.7 %collective-permute-start.6 = (bf16[3,1024,256]{2,1,0:T(8,128)(2,1)}, bf16[3,1024,256]{2,1,0:T(8,128)(2,1)}, u32[]{:S(2)}, u32[]{:S(2)}) collective-permute-start(bf16[3,1024,256]{2,1,0:T(8,128)(2,1)} %bitcast.271), channel_id=1, source_target_pairs={{0,16},{16,0},{1,17},{17,1},{2,18},{18,2},{3,19},{19,3},{4,20},{20... | collective-permute-start | bytes 4718600 | tf_op jit(solution)/shard_map/ppermute | solution.py:1157
  532.3 78.5 %collective-permute-start.11 = (bf16[4,256,1024]{2,1,0:T(8,128)(2,1)}, bf16[4,256,1024]{2,1,0:T(8,128)(2,1)}, u32[]{:S(2)}, u32[]{:S(2)}) collective-permute-start(bf16[4,256,1024]{2,1,0:T(8,128)(2,1)} %constant_dynamic-slice_fusion.3.refs_8_), channel_id=1, source_target_pairs={{16,0},{0,16},{17,1},{1,17},{18,2},{2,18},{19,3},{3,19},{20,4},{4,... | collective-permute-start | bytes 6291464 | tf_op jit(solution)/shard_map/ppermute | solution.py:1143
  568.7 42.0 %collective-permute-start.10 = (bf16[3,1024,256]{2,1,0:T(8,128)(2,1)}, bf16[3,1024,256]{2,1,0:T(8,128)(2,1)}, u32[]{:S(2)}, u32[]{:S(2)}) collective-permute-start(bf16[3,1024,256]{2,1,0:T(8,128)(2,1)} %add_convert_fusion.4.near_ref), channel_id=1, source_target_pairs={{0,4},{4,0},{8,12},{12,8},{1,5},{5,1},{9,13},{13,9},{2,6},{6,2},{1... | collective-permute-start | bytes 4718600 | tf_op jit(solution)/shard_map/ppermute | solution.py:1300
  616.5 36.5 %collective-permute-start.12 = (bf16[1024,512]{1,0:T(8,128)(2,1)}, bf16[1024,512]{1,0:T(8,128)(2,1)}, u32[]{:S(2)}, u32[]{:S(2)}) collective-permute-start(bf16[1024,512]{1,0:T(8,128)(2,1)} %convolution_convert_fusion), channel_id=1, source_target_pairs={{0,16},{16,0},{1,17},{17,1},{2,18},{18,2},{3,19},{19,3},{4,20},{20... | collective-permute-start | bytes 3145736 | tf_op jit(solution)/shard_map/ppermute | solution.py:1157
  623.6 29.4 %all-to-all-start.1 = ((bf16[4,1,1,512,128]{4,3,2,1,0:T(8,128)(2,1)}), bf16[4,1,1,512,128]{4,3,2,1,0:T(8,128)(2,1)}, u32[]{:S(2)}, u32[]{:S(2)}) async-start(bf16[4,1,1,512,128]{4,3,2,1,0:T(8,128)(2,1)} %bitcast.233), calls=%async_computation.3 | async-start | bytes 1048576 | tf_op jit(solution)/shard_map/all_to_all | solution.py:144
  627.8 69.2 %reduce-scatter.8.cloned.1.call-start = ((), (), s32[]{:S(2)}) async-start(), calls=%async_computation.8 | async-start | bytes 1310720 | tf_op jit(solution)/shard_map/reduce_scatter | solution.py:1368
  652.4 69.2 %collective-permute-start.13 = (bf16[3,1024,256]{2,1,0:T(8,128)(2,1)}, bf16[3,1024,256]{2,1,0:T(8,128)(2,1)}, u32[]{:S(2)}, u32[]{:S(2)}) collective-permute-start(bf16[3,1024,256]{2,1,0:T(8,128)(2,1)} %bitcast.272), channel_id=1, source_target_pairs={{0,16},{16,0},{1,17},{17,1},{2,18},{18,2},{3,19},{19,3},{4,20},{20... | collective-permute-start | bytes 4718600 | tf_op jit(solution)/shard_map/ppermute | solution.py:1157
  656.5 70.5 %all-gather.11.cloned.1.call-start = ((), (), s32[]{:S(2)}) async-start(), calls=%async_computation.9 | async-start | bytes 1310720 | tf_op jit(solution)/shard_map/all_gather | solution.py:1388
  697.0 291.3 %all-gather.17.cloned.1.call-start = ((), (), s32[]{:S(2)}) async-start(), calls=%async_computation.12 | async-start | bytes 4055040 | tf_op jit(solution)/shard_map/all_gather | solution.py:1447
  727.0 36.3 %collective-permute-start.15 = (bf16[3,1024,256]{2,1,0:T(8,128)(2,1)}, bf16[3,1024,256]{2,1,0:T(8,128)(2,1)}, u32[]{:S(2)}, u32[]{:S(2)}) collective-permute-start(bf16[3,1024,256]{2,1,0:T(8,128)(2,1)} %add_convert_fusion.3.near_ref), channel_id=1, source_target_pairs={{0,4},{4,0},{8,12},{12,8},{1,5},{5,1},{9,13},{13,9},{2,6},{6,2},{1... | collective-permute-start | bytes 4718600 | tf_op jit(solution)/shard_map/ppermute | solution.py:1300
  728.5 36.2 %collective-permute-start.14 = (bf16[3,1024,256]{2,1,0:T(8,128)(2,1)}, bf16[3,1024,256]{2,1,0:T(8,128)(2,1)}, u32[]{:S(2)}, u32[]{:S(2)}) collective-permute-start(bf16[3,1024,256]{2,1,0:T(8,128)(2,1)} %bitcast.273), channel_id=1, source_target_pairs={{0,16},{16,0},{1,17},{17,1},{2,18},{18,2},{3,19},{19,3},{4,20},{20... | collective-permute-start | bytes 4718600 | tf_op jit(solution)/shard_map/ppermute | solution.py:1157
  766.4 36.5 %collective-permute-start.17 = (bf16[3,1024,256]{2,1,0:T(8,128)(2,1)S(1)}, bf16[3,1024,256]{2,1,0:T(8,128)(2,1)}, u32[]{:S(2)}, u32[]{:S(2)}) collective-permute-start(bf16[3,1024,256]{2,1,0:T(8,128)(2,1)S(1)} %add_convert_fusion.2.near_ref), channel_id=1, source_target_pairs={{0,4},{4,0},{8,12},{12,8},{1,5},{5,1},{9,13},{13,9},{2,6},{6,2},{1... | collective-permute-start | bytes 4718600 | tf_op jit(solution)/shard_map/ppermute | solution.py:1300
  766.9 36.0 %collective-permute-start.16 = (bf16[3,1024,256]{2,1,0:T(8,128)(2,1)}, bf16[3,1024,256]{2,1,0:T(8,128)(2,1)}, u32[]{:S(2)}, u32[]{:S(2)}) collective-permute-start(bf16[3,1024,256]{2,1,0:T(8,128)(2,1)} %bitcast.72), channel_id=1, source_target_pairs={{0,16},{16,0},{1,17},{17,1},{2,18},{18,2},{3,19},{19,3},{4,20},{20... | collective-permute-start | bytes 4718600 | tf_op jit(solution)/shard_map/ppermute | solution.py:1157
  804.8 73.3 %collective-permute-start.20 = (bf16[3,1024,256]{2,1,0:T(8,128)(2,1)}, bf16[3,1024,256]{2,1,0:T(8,128)(2,1)}, u32[]{:S(2)}, u32[]{:S(2)}) collective-permute-start(bf16[3,1024,256]{2,1,0:T(8,128)(2,1)} %bitcast.77), channel_id=1, source_target_pairs={{0,16},{16,0},{1,17},{17,1},{2,18},{18,2},{3,19},{19,3},{4,20},{20... | collective-permute-start | bytes 4718600 | tf_op jit(solution)/shard_map/ppermute | solution.py:1157
  805.5 72.7 %collective-permute-start.19 = (bf16[3,1024,256]{2,1,0:T(8,128)(2,1)S(1)}, bf16[3,1024,256]{2,1,0:T(8,128)(2,1)S(1)}, u32[]{:S(2)}, u32[]{:S(2)}) collective-permute-start(bf16[3,1024,256]{2,1,0:T(8,128)(2,1)S(1)} %add_convert_fusion.1.near_ref), channel_id=1, source_target_pairs={{0,4},{4,0},{8,12},{12,8},{1,5},{5,1},{9,13},{13,9},{2,6},{6,2},{1... | collective-permute-start | bytes 4718600 | tf_op jit(solution)/shard_map/ppermute | solution.py:1300
  807.0 72.3 %collective-permute-start.18 = (bf16[1024,384]{1,0:T(8,128)(2,1)S(1)}, bf16[1024,384]{1,0:T(8,128)(2,1)}, u32[]{:S(2)}, u32[]{:S(2)}) collective-permute-start(bf16[1024,384]{1,0:T(8,128)(2,1)S(1)} %copy-done.56), channel_id=1, source_target_pairs={{0,16},{16,0},{1,17},{17,1},{2,18},{18,2},{3,19},{19,3},{4,20},{20... | collective-permute-start | bytes 2359304 | tf_op jit(solution)/shard_map/ppermute | solution.py:1157
  889.5 93.4 %collective-permute-start.22 = (bf16[3,1024,256]{2,1,0:T(8,128)(2,1)}, bf16[3,1024,256]{2,1,0:T(8,128)(2,1)}, u32[]{:S(2)}, u32[]{:S(2)}) collective-permute-start(bf16[3,1024,256]{2,1,0:T(8,128)(2,1)} %add_convert_fusion.near_ref), channel_id=1, source_target_pairs={{0,4},{4,0},{8,12},{12,8},{1,5},{5,1},{9,13},{13,9},{2,6},{6,2},{1... | collective-permute-start | bytes 4718600 | tf_op jit(solution)/shard_map/ppermute | solution.py:1300
  (63 other events, 1136.2 us)
Sparse Core Ops, SparseCore 0:
  10.2 60.8 all-gather.12
  122.9 62.0 all-gather.8
  408.0 104.7 reduce-scatter.3
  527.7 58.6 reduce-scatter.5
  613.4 34.6 all-gather.14
  656.6 29.5 reduce-scatter.7
  697.1 29.8 all-gather.10
  883.8 98.4 all-gather.16

commit v5 on v4

--- a/solution.py
+++ b/solution.py
@@ -1457,8 +1457,8 @@
         return natural(jnp.concatenate(every, axis=1))
 
     output = whole(output)
-    d_inputs = join(d_inputs, 10)
-    d_inputs = natural(d_inputs)
+    d_inputs = join(d_inputs.astype(BF16), 10)
+    d_inputs = natural(d_inputs).astype(F32)
     turned = [small_grads[(p % 2) * 2 + p // 2, : 2 + experts] for p in range(tp_count)]
     heads_gains = small_grads[:, 2 + experts : 4 + experts].transpose(1, 0, 2).reshape(2, width)
     small_grads = jnp.concatenate([natural(jnp.concatenate(turned, axis=1)), heads_gains])

time: 1020 us -> 1020 us (level)
  waiting for transfers between devices: 67.5 us -> 87 us
  Pallas kernels: 675 us -> 659 us
    ppermute x8, waiting for transfers between devices: 20.4 us -> 39.9 us  [start_z(): lax.ppermute(sums[e], 'ctx', [(i, i ^ 1) for i in range(ctx_count)])]
    pallas_call x2, Pallas kernels: 50.3 us -> 34.3 us  [join(): pl.pallas_call(join_kernel, cost_estimate=pl.CostEstimate(flops=25 * MICR...]
  transfers between devices with their start and end apart: 33 -> 33, of which waited for: 9 -> 9; matrix products, arithmetic and copies ran while one was open for 14% -> 14% of each run, Pallas kernels for 64% -> 62%
where the time goes in v5:
time: 1020 us; the launch traced here: 1010 us
  Pallas kernels  659 us (65%)
  waiting for transfers between devices  87 us (9%)
  other arithmetic  70 us (7%)
  local copies, waits for them, and re-layouts  63.8 us (6%)
  starting transfers between devices  61 us (6%)
  matrix products  34.5 us (3%)
  blocking collectives  23.4 us (2%)
  between operations  15.8 us (2%)
    pallas_call x8, Pallas kernels, expert(): pl.pallas_call(functools.partial(expert_kernel, blocks, e, far, mine, ful...  198 us
    pallas_call x2, Pallas kernels, returns(): pl.pallas_call(functools.partial(returns_kernel, kinds, mine, blocks, fli...  173 us
    pallas_call x2, Pallas kernels, spread(): pl.pallas_call(functools.partial(spread_kernel, [axis for axis, _ in carr...  148 us
    ppermute x8, waiting for transfers between devices, start_z(): lax.ppermute(sums[e], 'ctx', [(i, i ^ 1) for i in range(ctx_count)])  39.9 us
    pallas_call x8, Pallas kernels, place_grads(): pl.pallas_call(place_kernel, cost_estimate=pl.CostEstimate(flops=4 * MICR...  37.7 us
    pallas_call x2, Pallas kernels, join(): pl.pallas_call(join_kernel, cost_estimate=pl.CostEstimate(flops=25 * MICR...  34.3 us
    ppermute x10, waiting for transfers between devices, swap(): lax.ppermute(blocks[s], 'dp', [(i, (i + s) % dp_count) for i in range(dp_...  32.3 us
    ppermute x8, starting transfers between devices, start_z(): lax.ppermute(sums[e], 'ctx', [(i, i ^ 1) for i in range(ctx_count)])  30.9 us
  transfers between devices with their start and end apart: 33, of which 9 were waited for; matrix products, arithmetic and copies ran while one was open for 14% of the time, Pallas kernels for 62%

profile of v5, /device:TPU:0, one launch (start us, length us, event | category | flops | bytes accessed | tf_op | source)
XLA Modules:
  0.0 1014.2 jit_solution(15809697602371226984)
XLA Ops:
  32.5 87.2 %shard_map.263 = (bf16[2048,2048]{1,0:T(8,128)(2,1)}, bf16[1,1024,384]{2,1,0:T(8,128)(2,1)}, bf16[1,512,1024]{2,1,0:T(8,128)(2,1)}, bf16[1,4,1024,256]{3,2,1,0:T(8,128)(2,1)}) custom-call(bf16[512,512]{1,0:T(8,128)(2,1)} %multiply_convert_fusion.1.x_ref, bf16[1024,384]{1,0:T(8,128)(2,1)} %get-tuple-element.528.refs_0_, bf16[512,1024]{1,0:T(8,128)(2,1)} %refs_1_.1, ...), custom_call_target="tpu_custom_call" | custom-call | flops 4026531840 | tf_op jit(solution)/shard_map/pallas_call | solution.py:473
  128.5 5.5 fusion.2
  137.2 9.8 shard_map.264
  150.7 7.1 shard_map.265
  167.7 12.2 %all-to-all-done = bf16[4,1,1,512,128]{3,4,2,1,0:T(8,128)(2,1)S(1)} async-done(((bf16[4,1,1,512,128]{3,4,2,1,0:T(8,128)(2,1)}), bf16[4,1,1,512,128]{3,4,2,1,0:T(8,128)(2,1)S(1)}, u32[]{:S(2)}, u32[]{:S(2)}) %all-to-all-start) | async-done | bytes 524320 | tf_op jit(solution)/shard_map/all_to_all | solution.py:153
  184.2 17.2 %shard_map.266 = f32[512,512]{1,0:T(8,128)S(1)} custom-call(bf16[512,2048]{1,0:T(8,128)(2,1)S(1)} %pad_maximum_fusion.1.x_ref), custom_call_target="tpu_custom_call" | custom-call | flops 1140850688 | tf_op jit(solution)/shard_map/pallas_call | solution.py:666
  202.8 5.8 psum.21
  209.6 61.0 %shard_map.267 = (bf16[2048,2048]{1,0:T(8,128)(2,1)}, bf16[1,4,256,1024]{3,2,1,0:T(8,128)(2,1)}) custom-call(bf16[512,512]{1,0:T(8,128)(2,1)} %multiply_convert_fusion.x_ref, bf16[4,256,1024]{2,1,0:T(8,128)(2,1)} %constant_dynamic-slice_fusion.10.refs_0_.refs_8_.refs_4_), custom_call_target="tpu_custom_call" | custom-call | flops 4026531840 | tf_op jit(solution)/shard_map/pallas_call | solution.py:473
  270.6 24.9 %shard_map.268 = (bf16[2048,256]{1,0:T(8,128)(2,1)}, bf16[2048,256]{1,0:T(8,128)(2,1)}, bf16[2048,256]{1,0:T(8,128)(2,1)}, f32[2048,1]{1,0:T(8,128)}, bf16[3,102...) custom-call(bf16[2048,2048]{1,0:T(8,128)(2,1)} %get-tuple-element.367.refs_0_, ...), custom_call_target="tpu_custom_call" | custom-call | flops 1811939328 | tf_op jit(solution)/shard_map/pallas_call | solution.py:307
  305.8 24.9 %shard_map.269 = (bf16[2048,256]{1,0:T(8,128)(2,1)}, bf16[2048,256]{1,0:T(8,128)(2,1)}, bf16[2048,256]{1,0:T(8,128)(2,1)}, f32[2048,1]{1,0:T(8,128)}, bf16[3,102...) custom-call(bf16[2048,2048]{1,0:T(8,128)(2,1)} %get-tuple-element.367.refs_0_, ...), custom_call_target="tpu_custom_call" | custom-call | flops 1811939328 | tf_op jit(solution)/shard_map/pallas_call | solution.py:307
  332.0 25.4 %shard_map.270 = (bf16[2048,256]{1,0:T(8,128)(2,1)}, bf16[2048,256]{1,0:T(8,128)(2,1)}, bf16[2048,256]{1,0:T(8,128)(2,1)}, f32[2048,1]{1,0:T(8,128)}, bf16[3,102...) custom-call(bf16[2048,2048]{1,0:T(8,128)(2,1)} %get-tuple-element.367.refs_0_, ...), custom_call_target="tpu_custom_call" | custom-call | flops 1811939328 | tf_op jit(solution)/shard_map/pallas_call | solution.py:307
  361.1 7.1 collective-permute-done.3
  368.2 25.4 %shard_map.271 = (bf16[2048,256]{1,0:T(8,128)(2,1)}, bf16[2048,256]{1,0:T(8,128)(2,1)}, bf16[2048,256]{1,0:T(8,128)(2,1)}, f32[2048,1]{1,0:T(8,128)}, bf16[3,102...) custom-call(bf16[2048,2048]{1,0:T(8,128)(2,1)} %get-tuple-element.367.refs_0_, ...), custom_call_target="tpu_custom_call" | custom-call | flops 1811939328 | tf_op jit(solution)/shard_map/pallas_call | solution.py:307
  394.9 12.9 %shard_map.272 = bf16[4,2048,512]{2,1,0:T(8,128)(2,1)} custom-call(bf16[2048,256]{1,0:T(8,128)(2,1)S(1)} %copy-done.17, bf16[2048,256]{1,0:T(8,128)(2,1)S(1)} %copy-done.18, bf16[2048,256]{1,0:T(8,128)(2,1)S(1)} %copy-done.19, bf16[2048,256]{1,0:T(8,128)(2,1)S(1)} %copy-done.20, bf16[4,256,1024]{2,1,0:T(8,128)(2,1)} %constant_dynamic-slice_fusion.10.refs_0_.refs_8_.refs_4_, ...), custom_call_target="tpu_custom_call" | custom-call | flops 1006632960 | tf_op jit(solution)/shard_map/pallas_call | solution.py:996
  423.4 104.1 %shard_map.273 = (f32[512,512]{1,0:T(8,128)}, f32[4,4,512]{2,1,0:T(4,128)}) custom-call(bf16[2048,256]{1,0:T(8,128)(2,1)} %get-tuple-element.272.refs_0_, bf16[2048,256]{1,0:T(8,128)(2,1)} %get-tuple-element.273.refs_1_, bf16[2048,256]{1,0:T(8,128)(2,1)} %get-tuple-element.274.refs_2_, bf16[2048,256]{1,0:T(8,128)(2,1)} %get-tuple-element.275.refs_3_, ...), custom_call_target="tpu_custom_call" | custom-call | flops 4362076160 | tf_op jit(solution)/shard_map/pallas_call | solution.py:946
  535.9 6.0 psum.22
  542.0 23.4 %collective-permute-done.6 = bf16[3,1024,256]{2,1,0:T(8,128)(2,1)} collective-permute-done((bf16[3,1024,256]{2,1,0:T(8,128)(2,1)}, bf16[3,1024,256]{2,1,0:T(8,128)(2,1)}, u32[]{:S(2)}, u32[]{:S(2)}) %collective-permute-start.6) | collective-permute-done | bytes 1572896 | tf_op jit(solution)/shard_map/ppermute | solution.py:1157
  568.7 9.8 collective-permute-start.10
  581.6 17.1 %shard_map.274 = bf16[512,2048]{1,0:T(8,128)(2,1)} custom-call(bf16[512,512]{1,0:T(8,128)(2,1)} %get-tuple-element.505.x_ref), custom_call_target="tpu_custom_call" | custom-call | flops 1677721600 | tf_op jit(solution)/shard_map/pallas_call | solution.py:516
  598.7 12.1 %collective-permute-done.10.far_ref = bf16[3,1024,256]{2,1,0:T(8,128)(2,1)} collective-permute-done((bf16[3,1024,256]{2,1,0:T(8,128)(2,1)}, bf16[3,1024,256]{2,1,0:T(8,128)(2,1)}, u32[]{:S(2)}, u32[]{:S(2)}) %collective-permute-start.10) | collective-permute-done | bytes 1572896 | tf_op jit(solution)/shard_map/ppermute | solution.py:1300
  627.9 24.5 %shard_map.275 = (bf16[3,1024,256]{2,1,0:T(8,128)(2,1)}, bf16[1,3,1024,256]{3,2,1,0:T(8,128)(2,1)}) custom-call(bf16[2048,2048]{1,0:T(8,128)(2,1)} %get-tuple-element.367.refs_0_, bf16[2048,2048]{1,0:T(8,128)(2,1)} %all-gather.9.cloned.1.call-done.refs_1_, f32[2048,16]{1,0:T(8,128)} %bitcast.213, bf16[16,2048]{1,0:T(8,128)(2,1)} %pad_maximum_fusion.9.refs_3_, ...), custom_call_target="tpu_custom_call" | custom-call | flops 1811939328 | tf_op jit(solution)/shard_map/pallas_call | solution.py:307
  661.3 10.2 %shard_map.276 = (f32[1,2048,128]{2,1,0:T(8,128)S(1)}, f32[1,2048,128]{2,1,0:T(8,128)S(1)}, bf16[1,2048,128]{2,1,0:T(8,128)(2,1)S(1)}) custom-call(s32[1,3]{1,0:T(1,128)S(1)} %copy-done.23, bf16[1,2048,128]{2,1,0:T(8,128)(2,1)S(1)} %copy-done.10, bf16[1,2048,128]{2,1,0:T(8,128)(2,1)S(1)} %copy-done.8, bf16[1,2048,128]{2,1,0:T(8,128)(2,1)S(1)} %copy-done.12, ...), custom_call_target="tpu_custom_call" | custom-call | flops 671088640 | tf_op jit(solution)/shard_map/pallas_call | solution.py:126
  676.3 10.3 %shard_map.277 = f32[2,2048]{1,0:T(2,128)S(1)} custom-call(f32[2,2048]{1,0:T(2,128)S(1)} %pad_maximum_fusion.12.x_ref), custom_call_target="tpu_custom_call" | custom-call | flops 536870912 | tf_op jit(solution)/shard_map/pallas_call | solution.py:1099
  697.2 24.4 %shard_map.278 = (bf16[3,1024,256]{2,1,0:T(8,128)(2,1)}, bf16[1,3,1024,256]{3,2,1,0:T(8,128)(2,1)}) custom-call(bf16[2048,2048]{1,0:T(8,128)(2,1)} %get-tuple-element.367.refs_0_, bf16[2048,2048]{1,0:T(8,128)(2,1)} %all-gather.9.cloned.1.call-done.refs_1_, f32[2048,16]{1,0:T(8,128)} %bitcast.214, bf16[16,2048]{1,0:T(8,128)(2,1)} %pad_maximum_fusion.9.refs_3_, ...), custom_call_target="tpu_custom_call" | custom-call | flops 1811939328 | tf_op jit(solution)/shard_map/pallas_call | solution.py:307
  730.0 24.4 %shard_map.279 = (bf16[3,1024,256]{2,1,0:T(8,128)(2,1)}, bf16[1,3,1024,256]{3,2,1,0:T(8,128)(2,1)}) custom-call(bf16[2048,2048]{1,0:T(8,128)(2,1)} %get-tuple-element.367.refs_0_, bf16[2048,2048]{1,0:T(8,128)(2,1)} %all-gather.9.cloned.1.call-done.refs_1_, f32[2048,16]{1,0:T(8,128)} %bitcast.215, bf16[16,2048]{1,0:T(8,128)(2,1)} %pad_maximum_fusion.9.refs_3_, ...), custom_call_target="tpu_custom_call" | custom-call | flops 1811939328 | tf_op jit(solution)/shard_map/pallas_call | solution.py:307
  768.4 24.2 %shard_map.282 = (bf16[3,1024,256]{2,1,0:T(8,128)(2,1)}, bf16[1,3,1024,256]{3,2,1,0:T(8,128)(2,1)}) custom-call(bf16[2048,2048]{1,0:T(8,128)(2,1)} %get-tuple-element.367.refs_0_, bf16[2048,2048]{1,0:T(8,128)(2,1)} %all-gather.9.cloned.1.call-done.refs_1_, f32[2048,16]{1,0:T(8,128)} %bitcast.216, bf16[16,2048]{1,0:T(8,128)(2,1)} %pad_maximum_fusion.9.refs_3_, ...), custom_call_target="tpu_custom_call" | custom-call | flops 1811939328 | tf_op jit(solution)/shard_map/pallas_call | solution.py:307
  809.4 68.7 %shard_map.285 = f32[512,512]{1,0:T(8,128)} custom-call(bf16[2048,384]{1,0:T(8,128)(2,1)} %pad_maximum_fusion.2.refs_0_, bf16[1,1024,384]{2,1,0:T(8,128)(2,1)} %get-tuple-element.527.refs_1_, bf16[1,1024,384]{2,1,0:T(8,128)(2,1)} %get-tuple-element.229.refs_2_), custom_call_target="tpu_custom_call" | custom-call | flops 4362076160 | tf_op jit(solution)/shard_map/pallas_call | solution.py:946
  891.4 15.4 %collective-permute-start.22 = (bf16[3,1024,256]{2,1,0:T(8,128)(2,1)}, bf16[3,1024,256]{2,1,0:T(8,128)(2,1)}, u32[]{:S(2)}, u32[]{:S(2)}) collective-permute-start(bf16[3,1024,256]{2,1,0:T(8,128)(2,1)} %add_convert_fusion.near_ref), channel_id=1, source_target_pairs={{0,4},{4,0},{8,12},{12,8},{1,5},{5,1},{9,13},{13,9},{2,6},{6,2},{1... | collective-permute-start | bytes 4718600 | tf_op jit(solution)/shard_map/ppermute | solution.py:1300
  913.5 6.0 psum.23
  935.5 17.2 %shard_map.286 = bf16[512,2048]{1,0:T(8,128)(2,1)} custom-call(bf16[512,512]{1,0:T(8,128)(2,1)} %subtract_convert_fusion.x_ref), custom_call_target="tpu_custom_call" | custom-call | flops 1677721600 | tf_op jit(solution)/shard_map/pallas_call | solution.py:516
  957.2 27.5 %collective-permute-done.22.far_ref = bf16[3,1024,256]{2,1,0:T(8,128)(2,1)} collective-permute-done((bf16[3,1024,256]{2,1,0:T(8,128)(2,1)}, bf16[3,1024,256]{2,1,0:T(8,128)(2,1)}, u32[]{:S(2)}, u32[]{:S(2)}) %collective-permute-start.22) | collective-permute-done | bytes 1572896 | tf_op jit(solution)/shard_map/ppermute | solution.py:1300
  991.1 5.6 all_gather.35
  (352 shorter events, 241.2 us)
Async XLA Ops:
  7.2 112.5 %all-gather.13.cloned.1.call-start = ((), (), s32[]{:S(2)}) async-start(), calls=%async_computation.10 | async-start | bytes 2703360 | tf_op jit(solution)/shard_map/all_gather | solution.py:1237
  10.1 260.5 %all-gather.9.cloned.1.call-start = ((), (), s32[]{:S(2)}) async-start(), calls=%async_computation.5 | async-start | bytes 10485760 | tf_op jit(solution)/shard_map/all_gather | solution.py:1240
  13.9 16.3 %collective-permute-start = (bf16[20,1024]{1,0:T(8,128)(2,1)S(1)}, bf16[20,1024]{1,0:T(8,128)(2,1)S(1)}, u32[]{:S(2)}, u32[]{:S(2)}) collective-permute-start(bf16[20,1024]{1,0:T(8,128)(2,1)S(1)} %concatenate.104), channel_id=1, source_target_pairs={{16,0},{0,16},{17,1},{1,17},{18,2},{2,18},{19,3},{3,19},{20,4},{4,... | collective-permute-start | bytes 122888 | tf_op jit(solution)/shard_map/ppermute | solution.py:1143
  126.9 57.3 %collective-permute-start.1 = (bf16[4,1024,256]{2,1,0:T(8,128)(2,1)S(1)}, bf16[4,1024,256]{2,1,0:T(8,128)(2,1)}, u32[]{:S(2)}, u32[]{:S(2)}) collective-permute-start(bf16[4,1024,256]{2,1,0:T(8,128)(2,1)S(1)} %get-tuple-element.239.refs_6_.refs_10_), channel_id=1, source_target_pairs={{16,0},{0,16},{17,1},{1,17},{18,2},{2,18},{19,3},{3,19},{20,4},{4,... | collective-permute-start | bytes 6291464 | tf_op jit(solution)/shard_map/ppermute | solution.py:1143
  159.8 20.0 %all-to-all-start = ((bf16[4,1,1,512,128]{3,4,2,1,0:T(8,128)(2,1)}), bf16[4,1,1,512,128]{3,4,2,1,0:T(8,128)(2,1)S(1)}, u32[]{:S(2)}, u32[]{:S(2)}) async-start(bf16[4,1,1,512,128]{3,4,2,1,0:T(8,128)(2,1)} %copy.95), calls=%async_computation | async-start | bytes 1048576 | tf_op jit(solution)/shard_map/all_to_all | solution.py:153
  164.7 362.8 %reduce-scatter.4.cloned.1.call-start = ((), (), s32[]{:S(2)}) async-start(), calls=%async_computation.6 | async-start | bytes 10485760 | tf_op jit(solution)/shard_map/reduce_scatter | solution.py:1319
  295.5 36.5 %collective-permute-start.2 = (bf16[3,1024,256]{2,1,0:T(8,128)(2,1)}, bf16[3,1024,256]{2,1,0:T(8,128)(2,1)S(1)}, u32[]{:S(2)}, u32[]{:S(2)}) collective-permute-start(bf16[3,1024,256]{2,1,0:T(8,128)(2,1)} %bitcast.285), channel_id=1, source_target_pairs={{0,16},{16,0},{1,17},{17,1},{2,18},{18,2},{3,19},{19,3},{4,20},{20... | collective-permute-start | bytes 4718600 | tf_op jit(solution)/shard_map/ppermute | solution.py:1157
  330.7 37.5 %collective-permute-start.3 = (bf16[3,1024,256]{2,1,0:T(8,128)(2,1)}, bf16[3,1024,256]{2,1,0:T(8,128)(2,1)S(1)}, u32[]{:S(2)}, u32[]{:S(2)}) collective-permute-start(bf16[3,1024,256]{2,1,0:T(8,128)(2,1)} %bitcast.287), channel_id=1, source_target_pairs={{0,16},{16,0},{1,17},{17,1},{2,18},{18,2},{3,19},{19,3},{4,20},{20... | collective-permute-start | bytes 4718600 | tf_op jit(solution)/shard_map/ppermute | solution.py:1157
  357.4 50.4 %collective-permute-start.5 = (bf16[3,1024,256]{2,1,0:T(8,128)(2,1)}, bf16[3,1024,256]{2,1,0:T(8,128)(2,1)}, u32[]{:S(2)}, u32[]{:S(2)}) collective-permute-start(bf16[3,1024,256]{2,1,0:T(8,128)(2,1)} %bitcast.286), channel_id=1, source_target_pairs={{0,16},{16,0},{1,17},{17,1},{2,18},{18,2},{3,19},{19,3},{4,20},{20... | collective-permute-start | bytes 4718600 | tf_op jit(solution)/shard_map/ppermute | solution.py:1157
  361.0 46.8 %collective-permute-start.4 = (bf16[3,1024,256]{2,1,0:T(8,128)(2,1)S(1)}, bf16[3,1024,256]{2,1,0:T(8,128)(2,1)S(1)}, u32[]{:S(2)}, u32[]{:S(2)}) collective-permute-start(bf16[3,1024,256]{2,1,0:T(8,128)(2,1)S(1)} %add_convert_fusion.7.near_ref), channel_id=1, source_target_pairs={{0,4},{4,0},{8,12},{12,8},{1,5},{5,1},{9,13},{13,9},{2,6},{6,2},{1... | collective-permute-start | bytes 4718600 | tf_op jit(solution)/shard_map/ppermute | solution.py:1300
  409.0 201.8 %reduce-scatter.6.cloned.1.call-start = ((), (), s32[]{:S(2)}) async-start(), calls=%async_computation.7 | async-start | bytes 2621440 | tf_op jit(solution)/shard_map/reduce_scatter | solution.py:1335
  409.0 118.5 %collective-permute-start.9 = (bf16[8,1024,256]{2,1,0:T(8,128)(2,1)}, bf16[8,1024,256]{2,1,0:T(8,128)(2,1)}, u32[]{:S(2)}, u32[]{:S(2)}) collective-permute-start(bf16[8,1024,256]{2,1,0:T(8,128)(2,1)} %pad_maximum_fusion.refs_4_.refs_6_), channel_id=1, source_target_pairs={{16,0},{0,16},{17,1},{1,17},{18,2},{2,18},{19,3},{3,19},{20,4},{4,... | collective-permute-start | bytes 12582920 | tf_op jit(solution)/shard_map/ppermute | solution.py:1143
  411.6 115.9 %collective-permute-start.8 = (bf16[3,1024,256]{2,1,0:T(8,128)(2,1)S(1)}, bf16[3,1024,256]{2,1,0:T(8,128)(2,1)}, u32[]{:S(2)}, u32[]{:S(2)}) collective-permute-start(bf16[3,1024,256]{2,1,0:T(8,128)(2,1)S(1)} %add_convert_fusion.5.near_ref), channel_id=1, source_target_pairs={{0,4},{4,0},{8,12},{12,8},{1,5},{5,1},{9,13},{13,9},{2,6},{6,2},{1... | collective-permute-start | bytes 4718600 | tf_op jit(solution)/shard_map/ppermute | solution.py:1300
  413.5 114.0 %collective-permute-start.7 = (bf16[3,1024,256]{2,1,0:T(8,128)(2,1)S(1)}, bf16[3,1024,256]{2,1,0:T(8,128)(2,1)}, u32[]{:S(2)}, u32[]{:S(2)}) collective-permute-start(bf16[3,1024,256]{2,1,0:T(8,128)(2,1)S(1)} %add_convert_fusion.6.near_ref), channel_id=1, source_target_pairs={{0,4},{4,0},{8,12},{12,8},{1,5},{5,1},{9,13},{13,9},{2,6},{6,2},{1... | collective-permute-start | bytes 4718600 | tf_op jit(solution)/shard_map/ppermute | solution.py:1300
  527.6 125.5 %all-gather.15.cloned.1.call-start = ((), (), s32[]{:S(2)}) async-start(), calls=%async_computation.11 | async-start | bytes 5242880 | tf_op jit(solution)/shard_map/all_gather | solution.py:1358
  527.6 37.7 %collective-permute-start.6 = (bf16[3,1024,256]{2,1,0:T(8,128)(2,1)}, bf16[3,1024,256]{2,1,0:T(8,128)(2,1)}, u32[]{:S(2)}, u32[]{:S(2)}) collective-permute-start(bf16[3,1024,256]{2,1,0:T(8,128)(2,1)} %bitcast.282), channel_id=1, source_target_pairs={{0,16},{16,0},{1,17},{17,1},{2,18},{18,2},{3,19},{19,3},{4,20},{20... | collective-permute-start | bytes 4718600 | tf_op jit(solution)/shard_map/ppermute | solution.py:1157
  532.3 78.5 %collective-permute-start.11 = (bf16[4,256,1024]{2,1,0:T(8,128)(2,1)}, bf16[4,256,1024]{2,1,0:T(8,128)(2,1)}, u32[]{:S(2)}, u32[]{:S(2)}) collective-permute-start(bf16[4,256,1024]{2,1,0:T(8,128)(2,1)} %constant_dynamic-slice_fusion.3.refs_8_), channel_id=1, source_target_pairs={{16,0},{0,16},{17,1},{1,17},{18,2},{2,18},{19,3},{3,19},{20,4},{4,... | collective-permute-start | bytes 6291464 | tf_op jit(solution)/shard_map/ppermute | solution.py:1143
  568.7 42.0 %collective-permute-start.10 = (bf16[3,1024,256]{2,1,0:T(8,128)(2,1)}, bf16[3,1024,256]{2,1,0:T(8,128)(2,1)}, u32[]{:S(2)}, u32[]{:S(2)}) collective-permute-start(bf16[3,1024,256]{2,1,0:T(8,128)(2,1)} %add_convert_fusion.4.near_ref), channel_id=1, source_target_pairs={{0,4},{4,0},{8,12},{12,8},{1,5},{5,1},{9,13},{13,9},{2,6},{6,2},{1... | collective-permute-start | bytes 4718600 | tf_op jit(solution)/shard_map/ppermute | solution.py:1300
  616.5 36.5 %collective-permute-start.12 = (bf16[1024,512]{1,0:T(8,128)(2,1)}, bf16[1024,512]{1,0:T(8,128)(2,1)}, u32[]{:S(2)}, u32[]{:S(2)}) collective-permute-start(bf16[1024,512]{1,0:T(8,128)(2,1)} %convolution_convert_fusion), channel_id=1, source_target_pairs={{0,16},{16,0},{1,17},{17,1},{2,18},{18,2},{3,19},{19,3},{4,20},{20... | collective-permute-start | bytes 3145736 | tf_op jit(solution)/shard_map/ppermute | solution.py:1157
  623.6 29.4 %all-to-all-start.1 = ((bf16[4,1,1,512,128]{4,3,2,1,0:T(8,128)(2,1)}), bf16[4,1,1,512,128]{4,3,2,1,0:T(8,128)(2,1)}, u32[]{:S(2)}, u32[]{:S(2)}) async-start(bf16[4,1,1,512,128]{4,3,2,1,0:T(8,128)(2,1)} %bitcast.244), calls=%async_computation.3 | async-start | bytes 1048576 | tf_op jit(solution)/shard_map/all_to_all | solution.py:144
  627.8 69.2 %reduce-scatter.8.cloned.1.call-start = ((), (), s32[]{:S(2)}) async-start(), calls=%async_computation.8 | async-start | bytes 1310720 | tf_op jit(solution)/shard_map/reduce_scatter | solution.py:1368
  652.4 69.2 %collective-permute-start.13 = (bf16[3,1024,256]{2,1,0:T(8,128)(2,1)}, bf16[3,1024,256]{2,1,0:T(8,128)(2,1)}, u32[]{:S(2)}, u32[]{:S(2)}) collective-permute-start(bf16[3,1024,256]{2,1,0:T(8,128)(2,1)} %bitcast.283), channel_id=1, source_target_pairs={{0,16},{16,0},{1,17},{17,1},{2,18},{18,2},{3,19},{19,3},{4,20},{20... | collective-permute-start | bytes 4718600 | tf_op jit(solution)/shard_map/ppermute | solution.py:1157
  656.5 70.5 %all-gather.11.cloned.1.call-start = ((), (), s32[]{:S(2)}) async-start(), calls=%async_computation.9 | async-start | bytes 1310720 | tf_op jit(solution)/shard_map/all_gather | solution.py:1388
  697.0 293.1 %all-gather.17.cloned.1.call-start = ((), (), s32[]{:S(2)}) async-start(), calls=%async_computation.12 | async-start | bytes 4055040 | tf_op jit(solution)/shard_map/all_gather | solution.py:1447
  727.0 36.3 %collective-permute-start.15 = (bf16[3,1024,256]{2,1,0:T(8,128)(2,1)}, bf16[3,1024,256]{2,1,0:T(8,128)(2,1)}, u32[]{:S(2)}, u32[]{:S(2)}) collective-permute-start(bf16[3,1024,256]{2,1,0:T(8,128)(2,1)} %add_convert_fusion.3.near_ref), channel_id=1, source_target_pairs={{0,4},{4,0},{8,12},{12,8},{1,5},{5,1},{9,13},{13,9},{2,6},{6,2},{1... | collective-permute-start | bytes 4718600 | tf_op jit(solution)/shard_map/ppermute | solution.py:1300
  728.5 36.2 %collective-permute-start.14 = (bf16[3,1024,256]{2,1,0:T(8,128)(2,1)}, bf16[3,1024,256]{2,1,0:T(8,128)(2,1)}, u32[]{:S(2)}, u32[]{:S(2)}) collective-permute-start(bf16[3,1024,256]{2,1,0:T(8,128)(2,1)} %bitcast.284), channel_id=1, source_target_pairs={{0,16},{16,0},{1,17},{17,1},{2,18},{18,2},{3,19},{19,3},{4,20},{20... | collective-permute-start | bytes 4718600 | tf_op jit(solution)/shard_map/ppermute | solution.py:1157
  766.4 36.5 %collective-permute-start.17 = (bf16[3,1024,256]{2,1,0:T(8,128)(2,1)S(1)}, bf16[3,1024,256]{2,1,0:T(8,128)(2,1)}, u32[]{:S(2)}, u32[]{:S(2)}) collective-permute-start(bf16[3,1024,256]{2,1,0:T(8,128)(2,1)S(1)} %add_convert_fusion.2.near_ref), channel_id=1, source_target_pairs={{0,4},{4,0},{8,12},{12,8},{1,5},{5,1},{9,13},{13,9},{2,6},{6,2},{1... | collective-permute-start | bytes 4718600 | tf_op jit(solution)/shard_map/ppermute | solution.py:1300
  766.9 36.0 %collective-permute-start.16 = (bf16[3,1024,256]{2,1,0:T(8,128)(2,1)}, bf16[3,1024,256]{2,1,0:T(8,128)(2,1)}, u32[]{:S(2)}, u32[]{:S(2)}) collective-permute-start(bf16[3,1024,256]{2,1,0:T(8,128)(2,1)} %bitcast.72), channel_id=1, source_target_pairs={{0,16},{16,0},{1,17},{17,1},{2,18},{18,2},{3,19},{19,3},{4,20},{20... | collective-permute-start | bytes 4718600 | tf_op jit(solution)/shard_map/ppermute | solution.py:1157
  804.8 73.3 %collective-permute-start.20 = (bf16[3,1024,256]{2,1,0:T(8,128)(2,1)}, bf16[3,1024,256]{2,1,0:T(8,128)(2,1)}, u32[]{:S(2)}, u32[]{:S(2)}) collective-permute-start(bf16[3,1024,256]{2,1,0:T(8,128)(2,1)} %bitcast.77), channel_id=1, source_target_pairs={{0,16},{16,0},{1,17},{17,1},{2,18},{18,2},{3,19},{19,3},{4,20},{20... | collective-permute-start | bytes 4718600 | tf_op jit(solution)/shard_map/ppermute | solution.py:1157
  805.5 72.7 %collective-permute-start.19 = (bf16[3,1024,256]{2,1,0:T(8,128)(2,1)S(1)}, bf16[3,1024,256]{2,1,0:T(8,128)(2,1)S(1)}, u32[]{:S(2)}, u32[]{:S(2)}) collective-permute-start(bf16[3,1024,256]{2,1,0:T(8,128)(2,1)S(1)} %add_convert_fusion.1.near_ref), channel_id=1, source_target_pairs={{0,4},{4,0},{8,12},{12,8},{1,5},{5,1},{9,13},{13,9},{2,6},{6,2},{1... | collective-permute-start | bytes 4718600 | tf_op jit(solution)/shard_map/ppermute | solution.py:1300
  807.0 72.3 %collective-permute-start.18 = (bf16[1024,384]{1,0:T(8,128)(2,1)S(1)}, bf16[1024,384]{1,0:T(8,128)(2,1)}, u32[]{:S(2)}, u32[]{:S(2)}) collective-permute-start(bf16[1024,384]{1,0:T(8,128)(2,1)S(1)} %copy-done.57), channel_id=1, source_target_pairs={{0,16},{16,0},{1,17},{17,1},{2,18},{18,2},{3,19},{19,3},{4,20},{20... | collective-permute-start | bytes 2359304 | tf_op jit(solution)/shard_map/ppermute | solution.py:1157
  891.4 93.4 %collective-permute-start.22 = (bf16[3,1024,256]{2,1,0:T(8,128)(2,1)}, bf16[3,1024,256]{2,1,0:T(8,128)(2,1)}, u32[]{:S(2)}, u32[]{:S(2)}) collective-permute-start(bf16[3,1024,256]{2,1,0:T(8,128)(2,1)} %add_convert_fusion.near_ref), channel_id=1, source_target_pairs={{0,4},{4,0},{8,12},{12,8},{1,5},{5,1},{9,13},{13,9},{2,6},{6,2},{1... | collective-permute-start | bytes 4718600 | tf_op jit(solution)/shard_map/ppermute | solution.py:1300
  (64 other events, 1150.9 us)
Sparse Core Ops, SparseCore 0:
  10.2 60.8 all-gather.12
  122.9 62.0 all-gather.8
  408.0 104.7 reduce-scatter.3
  527.7 58.6 reduce-scatter.5
  613.4 34.6 all-gather.14
  656.6 29.5 reduce-scatter.7
  697.1 29.8 all-gather.10
  883.8 100.2 all-gather.16
